TPU v7x, 512 devices: a whole 4x4x16 slice. The times are simulated.
512 devices in a mesh: rx: 32 (over z_lo, x), tx: 16 (over y, z_hi, core).
Axes of the slice: x: 4, y: 4, z: 16 (z_hi: 2, z_lo: 8; z = z_hi * 8 + z_lo), core: 2. Of those that a mesh axis runs over, the one named last changes fastest.
Arguments:
- sender_xy: int32 [2, 32768], P(None, ('tx', 'rx')), may hold values from 0 to 255, as said below
- listener_xy: int32 [2, 32768], P(None, ('rx', 'tx')), may hold values from 0 to 256, as said below
- powers: float32 [32768, 128], P(('tx', 'rx')), may hold values from 0.25 to 1
- weight: int32 [32768], P(('rx', 'tx')), may hold values from 1 to 16
- fairness: int32 [32768], P(('rx', 'tx')), may hold values from 0 to 2
- step_code: int32 [1], replicated, may hold values from 256 to 4096
Outputs:
- quality: float32 [32768, 128], P(('rx', 'tx'))
- gradient: float32 [32768, 128], P(('tx', 'rx'))
- new_power: float32 [32768, 128], P(('tx', 'rx'))
- duality_gap: float32 [1], replicated
Inputs may be any that keep to these rules, and one draw needn't show every extreme that they name: `sender_xy`: row 0 lies in 0 to 255 and row 1 in 0 to 255. `listener_xy`: each entry equals the sender_xy entry of the same user or exceeds it by one.
All inputs are finite; a program needn't handle non-finite values.
Results may differ from a plain program's by a relative error of at most 0.0003.
Values sent between devices are 32-bit elements; how exact they have to be, the bound alone decides.
No kernel may reach another device: no remote copies, remote signals or barrier semaphores. Data moves between devices by JAX's collectives and lax.ppermute only.
A program may use at most 64 MiB of HBM per device.

v0:
```python
import jax
import jax.numpy as jnp
from jax import lax
from jax.sharding import PartitionSpec as P

NOISE_POWER = 0.05
ARRAY_GAIN = 32.0
WEIGHT_UNIT = 1.0 / 16.0
PEAK_POWER = 1.0


def path_gain(listen, sender):
    delta_x = listen[0].astype(jnp.float32)[:, None] - sender[0].astype(jnp.float32)[None, :]
    delta_y = listen[1].astype(jnp.float32)[:, None] - sender[1].astype(jnp.float32)[None, :]
    return 1.0 / (1.0 + delta_x * delta_x + delta_y * delta_y)


def derivatives(interference, signal, user_weight, user_fair):
    denominator = NOISE_POWER + interference
    quality = signal / denominator
    user_scale = WEIGHT_UNIT * user_weight.astype(jnp.float32)
    marginal = (
        user_scale[:, None]
        * jnp.exp(-user_fair.astype(jnp.float32)[:, None] * jnp.log(quality))
        / denominator
    )
    return (quality, marginal, marginal * quality)


def per_device(sender_xy, listener_xy, powers, weight, fairness, step_code):
    rx_here = lax.axis_index("rx")
    tx_here = lax.axis_index("tx")
    user_rows = powers.shape[0]
    channels = powers.shape[1]
    senders, sender_power = (
        lax.all_gather(sender_xy, "rx", axis=1, tiled=True),
        lax.all_gather(powers, "rx", axis=0, tiled=True),
    )
    listeners = lax.all_gather(listener_xy, "tx", axis=1, tiled=True)
    rx_width = listeners.shape[1]
    tx_width = senders.shape[1]
    row_start = rx_here * rx_width
    col_start = tx_here * tx_width
    gain_tile = path_gain(listeners, senders)
    row_ids = row_start + jnp.arange(rx_width, dtype=jnp.int32)
    col_ids = col_start + jnp.arange(tx_width, dtype=jnp.int32)
    diagonal = row_ids[:, None] == col_ids[None, :]
    crossing = jnp.where(diagonal, 0.0, gain_tile)
    own_gain = jnp.sum(jnp.where(diagonal, gain_tile, 0.0), axis=1)
    offset = row_start % tx_width
    interference_part = jnp.dot(crossing, sender_power, precision=lax.Precision.HIGHEST)
    signal_part = (
        ARRAY_GAIN * own_gain[:, None] * lax.dynamic_slice_in_dim(sender_power, offset, rx_width, 0)
    )
    interference, signal = (
        lax.psum_scatter(interference_part, "tx", scatter_dimension=0, tiled=True),
        lax.psum_scatter(signal_part, "tx", scatter_dimension=0, tiled=True),
    )
    quality, marginal, pressure = derivatives(interference, signal, weight, fairness)
    marginal_all, pressure_all = (
        lax.all_gather(marginal, "tx", axis=0, tiled=True),
        lax.all_gather(pressure, "tx", axis=0, tiled=True),
    )
    own_term = ARRAY_GAIN * own_gain[:, None] * marginal_all
    own_full = lax.dynamic_update_slice_in_dim(
        jnp.zeros((tx_width, channels), jnp.float32), own_term, offset, 0
    )
    pushed = lax.dot_general(
        crossing, pressure_all, (((0,), (0,)), ((), ())), precision=lax.Precision.HIGHEST
    )
    totals = lax.psum(own_full - pushed, "rx")
    gradient = lax.dynamic_slice_in_dim(totals, rx_here * user_rows, user_rows, 0)
    target = PEAK_POWER * jax.nn.sigmoid(gradient)
    step_size = step_code[0].astype(jnp.float32) / 4096.0
    new_power = powers + step_size * (target - powers)
    gap_local = jnp.sum(PEAK_POWER * jnp.maximum(gradient, 0.0) - gradient * powers)
    gap_sum = lax.psum(gap_local, ("rx", "tx"))
    duality_gap = (
        gap_sum / (user_rows * channels * lax.axis_size("rx") * lax.axis_size("tx"))
    ).reshape(1)
    return (quality, gradient, new_power, duality_gap)


def solution(mesh):
    placed = (
        P(None, ("tx", "rx")),
        P(None, ("rx", "tx")),
        P(("tx", "rx"), None),
        P(("rx", "tx")),
        P(("rx", "tx")),
        P(),
    )
    return jax.shard_map(
        per_device,
        mesh=mesh,
        in_specs=placed,
        out_specs=(P(("rx", "tx"), None), P(("tx", "rx"), None), P(("tx", "rx"), None), P()),
        check_vma=False,
    )
```

profile of v0, /device:TPU:1, one launch (start us, length us, event | category | flops | bytes accessed | tf_op | source)
XLA Modules:
  0.0 1118.0 jit_solution(16016938262697707755)
XLA Ops:
  7.2 0.0 all-gather.4.cloned.1.call-start
  7.2 0.7 all-gather.4.cloned.1.call-update
  7.9 0.0 reduce-scatter.3.cloned.1.call-start
  8.0 51.2 %all-gather = s32[16,64,2]{1,2,0:T(2,128)S(1)} all-gather(s32[1,64,2]{1,2,0:T(2,128)} %bitcast.34), channel_id=1, replica_groups=mesh['rx'=32,'tx'=16] {'tx'}, dimensions={0}, use_global_device_ids=true | all-gather | bytes 8704 | tf_op jit(solution)/shard_map/all_gather | solution.py:39
  59.1 0.1 reshape.43
  59.3 104.0 %all-gather.1 = s32[32,64,2]{1,2,0:T(2,128)S(1)} all-gather(s32[1,64,2]{1,2,0:T(2,128)} %bitcast.35), channel_id=1, replica_groups=mesh['rx'=32,'tx'=16] {'rx'}, dimensions={0}, use_global_device_ids=true | all-gather | bytes 16896 | tf_op jit(solution)/shard_map/all_gather | solution.py:36
  163.3 0.1 reshape.45
  163.5 3.1 fusion
  166.5 49.7 %all-gather.4.cloned.1.call-done = f32[2048,128]{1,0:T(8,128)} async-done(((f32[64,128]{1,0:T(8,128)}), f32[2048,128]{1,0:T(8,128)}) %all-gather.4.cloned.1.call-update) | async-done | bytes 1048592 | tf_op jit(solution)/shard_map/all_gather | solution.py:37
  216.2 0.0 copy-start.1
  216.2 2.1 dynamic-slice_multiply_fusion
  218.4 0.0 reduce-scatter.3.cloned.1.call-update
  218.4 0.0 copy-start.3
  218.4 0.0 copy-start.4
  218.4 0.0 reduce-scatter.5.cloned.1.call-start
  218.5 0.0 copy-done.1
  218.5 9.3 fusion.2
  227.8 0.0 reduce-scatter.5.cloned.1.call-update
  227.8 0.0 all-reduce.2.cloned.1.call-start
  227.9 0.0 copy-done.3
  227.9 0.0 copy-done.4
  227.9 111.3 %reduce-scatter.3.cloned.1.call-done = f32[64,128]{1,0:T(8,128)} async-done(((f32[1024,128]{1,0:T(8,128)}), f32[64,128]{1,0:T(8,128)}) %reduce-scatter.3.cloned.1.call-update) | async-done | bytes 32784 | tf_op jit(solution)/shard_map/reduce_scatter | solution.py:57
  339.2 96.6 %reduce-scatter.5.cloned.1.call-done = f32[64,128]{1,0:T(8,128)} async-done(((f32[1024,128]{1,0:T(8,128)}), f32[64,128]{1,0:T(8,128)}) %reduce-scatter.5.cloned.1.call-update) | async-done | bytes 32784 | tf_op jit(solution)/shard_map/reduce_scatter | solution.py:56
  435.8 1.4 fusion.14
  437.2 43.2 %all_gather.18 = f32[1024,128]{1,0:T(8,128)S(1)} all-gather(f32[64,128]{1,0:T(8,128)S(1)} %get-tuple-element.7), channel_id=1, replica_groups=mesh['rx'=32,'tx'=16] {'tx'}, dimensions={0}, use_global_device_ids=true | all-gather | bytes 557056 | tf_op jit(solution)/shard_map/all_gather | solution.py:61
  480.4 49.4 %all_gather.19 = f32[1024,128]{1,0:T(8,128)S(1)} all-gather(f32[64,128]{1,0:T(8,128)S(1)} %get-tuple-element.6), channel_id=1, replica_groups=mesh['rx'=32,'tx'=16] {'tx'}, dimensions={0}, use_global_device_ids=true | all-gather | bytes 557056 | tf_op jit(solution)/shard_map/all_gather | solution.py:62
  529.7 0.1 broadcast_in_dim.7
  529.8 0.2 multiply_dynamic-update-slice_fusion
  530.0 16.3 %fusion.9 = f32[2048,128]{1,0:T(8,128)} fusion(f32[2048,128]{1,0:T(8,128)S(1)} %multiply_dynamic-update-slice_fusion, f32[1024,128]{1,0:T(8,128)S(1)} %all_gather.19, f32[2048]{0:T(1024)S(1)} %bitcast.27, f32[1024]{0:T(1024)S(1)} %bitcast.33, f32[2048]{0:T(1024)S(1)} %bitcast.24, f32[1024]{0:T(1024)S(1)} %bitcast.30, s32[2048]{0:T(1024)S(1)} %iota_add_fusion, ...), kind=kOutput, calls=%fused_computation.12 | convolution fusion | flops 3240361984 | bytes 2658304 | tf_op jit(solution)/shard_map/dot_general | solution.py:68
  546.3 0.0 copy-start
  546.3 0.0 all-reduce.2.cloned.1.call-update
  547.0 437.2 %all-reduce.2.cloned.1.call-done = f32[2048,128]{1,0:T(8,128)} async-done(((f32[2048,128]{1,0:T(8,128)}), f32[2048,128]{1,0:T(8,128)}) %all-reduce.2.cloned.1.call-update) | async-done | bytes 1048592 | tf_op jit(solution)/shard_map/psum | solution.py:71
  984.1 0.0 copy-done
  984.1 1.4 subtract_reduce_fusion
  985.5 0.0 copy-start.2
  985.5 123.6 %psum.15 = f32[]{:T(128)} all-reduce(f32[]{:T(128)} %get-tuple-element.4), channel_id=1, replica_groups=mesh['rx'=32,'tx'=16] {'rx','tx'}, use_global_device_ids=true, to_apply=%region_5.6 | all-reduce | flops 1 | bytes 8 | tf_op jit(solution)/shard_map/psum | solution.py:77
  1109.1 0.6 multiply_add_fusion
  1110.4 0.0 copy-done.2
  (8 shorter events, 0.0 us)
Async XLA Ops:
  7.2 209.1 %all-gather.4.cloned.1.call-start = ((), (), s32[]{:S(2)}) async-start(), calls=%async_computation.2 | async-start | bytes 1081344 | tf_op jit(solution)/shard_map/all_gather | solution.py:37
  7.9 331.3 %reduce-scatter.3.cloned.1.call-start = ((), (), s32[]{:S(2)}) async-start(), calls=%async_computation.3 | async-start | bytes 557056 | tf_op jit(solution)/shard_map/reduce_scatter | solution.py:57
  216.2 2.2 copy-start.1
  218.4 9.5 copy-start.3
  218.4 9.5 copy-start.4
  218.4 217.4 %reduce-scatter.5.cloned.1.call-start = ((), (), s32[]{:S(2)}) async-start(), calls=%async_computation.4 | async-start | bytes 557056 | tf_op jit(solution)/shard_map/reduce_scatter | solution.py:56
  227.8 756.3 %all-reduce.2.cloned.1.call-start = ((), (), s32[]{:S(2)}) async-start(), calls=%async_computation.5 | async-start | bytes 2097152 | tf_op jit(solution)/shard_map/psum | solution.py:71
  546.3 437.8 %copy-start = (f32[64,128]{1,0:T(8,128)S(1)}, f32[64,128]{1,0:T(8,128)}, u32[]{:S(2)}) copy-start(f32[64,128]{1,0:T(8,128)} %param.8) | copy-start | bytes 98308
  985.5 124.9 %copy-start.2 = (f32[64,128]{1,0:T(8,128)}, f32[64,128]{1,0:T(8,128)S(1)}, u32[]{:S(2)}) copy-start(f32[64,128]{1,0:T(8,128)S(1)} %get-tuple-element.5) | copy-start | bytes 98308
Sparse Core Ops, SparseCore 0:
  10.1 206.1 all-gather.3
  220.9 118.3 reduce-scatter.2
  344.6 91.1 reduce-scatter.4
  546.4 437.6 all-reduce.1
where the time goes:
time: 1120 us
  waiting for transfers between devices  695 us (62%)
  blocking collectives  371 us (33%)
  matrix products  25.6 us (2%)
  between operations  16.3 us (1%)
    psum x1, waiting for transfers between devices, per_device(): totals = lax.psum(own_full - pushed, 'rx')  437 us
    psum x1, blocking collectives, per_device(): gap_sum = lax.psum(gap_local, ('rx', 'tx'))  124 us
    reduce_scatter x1, waiting for transfers between devices, per_device(): lax.psum_scatter(signal_part, 'tx', scatter_dimension=0, tiled=True)  111 us
    all_gather x1, blocking collectives, per_device(): lax.all_gather(sender_xy, 'rx', axis=1, tiled=True)  104 us
    reduce_scatter x1, waiting for transfers between devices, per_device(): lax.psum_scatter(interference_part, 'tx', scatter_dimension=0, tiled=True)  96.6 us
    all_gather x1, blocking collectives, per_device(): listeners = lax.all_gather(listener_xy, 'tx', axis=1, tiled=True)  51.2 us
    all_gather x1, waiting for transfers between devices, per_device(): lax.all_gather(powers, 'rx', axis=0, tiled=True)  49.7 us
    all_gather x1, blocking collectives, per_device(): lax.all_gather(pressure, 'tx', axis=0, tiled=True)  49.4 us
  transfers between devices with their start and end apart: 4, of which 4 were waited for; matrix products, arithmetic and copies ran while one was open for 1% of the time, Pallas kernels for 0%

commit v1 on v0

v1 whole, which is shorter than its diff:
```python
import jax
import jax.numpy as jnp
from jax import lax
from jax.experimental import pallas as pl
from jax.experimental.pallas import tpu as pltpu
from jax.sharding import Mesh
from jax.sharding import PartitionSpec as P

NOISE_POWER = 0.05
ARRAY_GAIN = 32.0
WEIGHT_UNIT = 1.0 / 16.0
PEAK_POWER = 1.0

AXES = ("zlo", "x", "y", "zhi", "core")
Z = ("zhi", "zlo")
XY = ("x", "y")
NZ, NXY = 16, 16
BLOCK, BANDS = 64, 128
HALF = NZ * BLOCK
ROWS = NXY * BLOCK
USERS = 32768
VMEM_LIMIT = 48 * 1024 * 1024
F32, BF16 = jnp.float32, jnp.bfloat16


def whole():
    return pl.BlockSpec(memory_space=pltpu.VMEM)


def call(kernel, outs, n_in, flops=0, bytes_accessed=1 << 20, smem=(), scratch=()):
    specs = [pl.BlockSpec(memory_space=pltpu.SMEM) if i in smem else whole() for i in range(n_in)]
    many = isinstance(outs, (list, tuple))
    return pl.pallas_call(
        kernel,
        out_shape=outs,
        in_specs=specs,
        out_specs=[whole() for _ in outs] if many else whole(),
        scratch_shapes=scratch,
        compiler_params=pltpu.CompilerParams(vmem_limit_bytes=VMEM_LIMIT),
        cost_estimate=pl.CostEstimate(flops=flops, bytes_accessed=bytes_accessed, transcendentals=0),
    )


def shape(*dims, dtype=F32):
    return jax.ShapeDtypeStruct(dims, dtype)


def split_norm(norm):
    low = norm & 511
    odd = low & 1
    return norm - low, low - odd, odd


def pack_kernel(sender_ref, listener_ref, powers_ref, sent_ref, heard_ref):
    sx, sy = sender_ref[0:1, :], sender_ref[1:2, :]
    lx, ly = listener_ref[0:1, :], listener_ref[1:2, :]
    one = jnp.ones_like(sx)
    s1, s2, s3 = split_norm(sx * sx + sy * sy)
    l1, l2, l3 = split_norm(lx * lx + ly * ly + 1)
    sent = jnp.concatenate([-2 * sx, -2 * sy, one, one, one, s1, s2, s3], axis=0).astype(F32)
    heard = jnp.concatenate([lx, ly, l1, l2, l3, one, one, one], axis=0).astype(F32)
    pad = jnp.zeros_like(sent)
    sent_ref[0:BLOCK, :] = powers_ref[...]
    sent_ref[BLOCK : BLOCK + 8, :] = jnp.concatenate([sent, pad], axis=1)
    heard_ref[...] = jnp.concatenate([heard, pad], axis=1)


def spread(parts, row):
    pieces = []
    for k in range(0, 16, 2):
        left = parts[k, row : row + 8, 0:BLOCK]
        right = parts[k + 1, row : row + 8, 0:BLOCK]
        pieces.append(jnp.concatenate([left, right], axis=1))
    features = jnp.concatenate(pieces, axis=1)
    return jnp.concatenate([features, jnp.zeros_like(features)], axis=0).astype(BF16)


def split(value):
    high = value.astype(BF16)
    low = (value - high.astype(F32)).astype(BF16)
    return high, low


def interfere_kernel(first, place_ref, sent_ref, heard_ref, *rest):
    if first:
        total_ref, high_ref, low_ref = rest
    else:
        before_ref, total_ref, high_ref, low_ref = rest
    x, y, zlo, zhi, core, source_core = (place_ref[i] for i in range(6))
    senders = spread(sent_ref, BLOCK)
    listeners = spread(heard_ref, 0)
    powers = sent_ref[:, 0:BLOCK, :].reshape(HALF, BANDS)
    power_high, power_low = split(powers)
    power_both = jnp.concatenate([power_high, power_low], axis=1)
    tile_rows, tile_cols = 256, 128
    receiver_base = zlo * 4096 + zhi * 128 + core * 64
    sender_base = y * 8192 + source_core * 2048 + x * 64
    for r in range(0, ROWS, tile_rows):
        row = lax.broadcasted_iota(jnp.int32, (tile_rows, tile_cols), 0) + r
        block = row >> 6
        row_id = receiver_base + (block >> 2) * 1024 + (block & 3) * 256 + (row & 63)
        for c in range(0, HALF, tile_cols):
            col = lax.broadcasted_iota(jnp.int32, (1, tile_cols), 1) + c
            zed = col >> 6
            col_id = sender_base + (zed >> 3) * 4096 + (zed & 7) * 256 + (col & 63)
            square = lax.dot_general(
                listeners[:, r : r + tile_rows],
                senders[:, c : c + tile_cols],
                (((0,), (0,)), ((), ())),
                preferred_element_type=F32,
            )
            guess = pl.reciprocal(square, approx=True)
            gain = guess * (2.0 - square * guess)
            gain = jnp.where(row_id == col_id, 0.0, gain)
            high, low = split(gain)
            high_ref[r : r + tile_rows, c : c + tile_cols] = high
            low_ref[r : r + tile_rows, c : c + tile_cols] = low
        product = jnp.dot(high_ref[r : r + tile_rows, :], power_both, preferred_element_type=F32)
        product = product + jnp.dot(
            low_ref[r : r + tile_rows, :], power_both, preferred_element_type=F32
        )
        part = product[:, :BANDS] + product[:, BANDS:]
        if not first:
            part = part + before_ref[r : r + tile_rows, :]
        total_ref[r : r + tile_rows, :] = part


def react_kernel(pressure_ref, high_ref, low_ref, pushed_ref):
    pressure = pressure_ref[...].reshape(ROWS, BANDS).T
    pressure_high, pressure_low = split(pressure)
    both = jnp.concatenate([pressure_high, pressure_low], axis=0)
    step = 256
    for c in range(0, HALF, step):
        product = jnp.dot(both, high_ref[:, c : c + step], preferred_element_type=F32)
        product = product + jnp.dot(both, low_ref[:, c : c + step], preferred_element_type=F32)
        pushed_ref[c : c + step, :] = (product[:BANDS, :] + product[BANDS:, :]).T


def add_blocks(ref, count):
    total = ref[0]
    for k in range(1, count):
        total = total + ref[k]
    return total


def derive_kernel(parts_ref, mine_ref, listener_ref, user_ref, quality_ref, own_ref, pressure_ref):
    interference = add_blocks(parts_ref, NXY)
    powers = mine_ref[0:BLOCK, :]
    sx = -0.5 * mine_ref[BLOCK : BLOCK + 1, 0:BLOCK]
    sy = -0.5 * mine_ref[BLOCK + 1 : BLOCK + 2, 0:BLOCK]
    dx = listener_ref[0:1, :].astype(F32) - sx
    dy = listener_ref[1:2, :].astype(F32) - sy
    own_gain = 1.0 / (1.0 + dx * dx + dy * dy)
    weight = WEIGHT_UNIT * user_ref[0:1, :].astype(F32)
    fair = user_ref[1:2, :].astype(F32)
    rows = jnp.concatenate([own_gain, weight, fair, jnp.zeros((5, BLOCK), F32)], axis=0)
    rows = jnp.concatenate([rows, jnp.zeros_like(rows)], axis=1)
    columns = jnp.concatenate([rows, jnp.zeros((120, 128), F32)], axis=0).T
    own_gain = columns[0:BLOCK, 0:1]
    weight = columns[0:BLOCK, 1:2]
    fair = columns[0:BLOCK, 2:3]
    signal = ARRAY_GAIN * own_gain * powers
    denominator = NOISE_POWER + interference
    quality = signal / denominator
    marginal = weight * jnp.exp(-fair * jnp.log(quality)) / denominator
    quality_ref[...] = quality
    own_ref[...] = ARRAY_GAIN * own_gain * marginal
    pressure_ref[...] = marginal * quality


def finish_kernel(step_ref, parts_ref, own_ref, powers_ref, gradient_ref, power_ref, gap_ref):
    gradient = own_ref[...] - add_blocks(parts_ref, NZ)
    powers = powers_ref[...]
    target = PEAK_POWER * jax.nn.sigmoid(gradient)
    step_size = step_ref[0].astype(F32) / 4096.0
    gradient_ref[...] = gradient
    power_ref[...] = powers + step_size * (target - powers)
    gap = PEAK_POWER * jnp.maximum(gradient, 0.0) - gradient * powers
    gap_ref[...] = jnp.sum(gap, axis=0, keepdims=True)


def share(value, axes, count):
    return lax.all_to_all(jnp.broadcast_to(value[None], (count, *value.shape)), axes, 0, 0)


def per_device(sender_xy, listener_xy, powers, weight, fairness, step_code):
    at = {name: lax.axis_index(name).astype(jnp.int32) for name in AXES}
    place = [at["x"], at["y"], at["zlo"], at["zhi"], at["core"]]
    to_receiver = [((b % 32) * 16 + b // 32, b) for b in range(512)]
    to_sender = [(d, s) for s, d in to_receiver]
    swap = [(0, 1), (1, 0)]

    sent, heard = call(pack_kernel, (shape(BLOCK + 8, BANDS), shape(8, 128)), 3)(
        sender_xy, listener_xy, powers
    )
    mine = lax.ppermute(sent, AXES, to_receiver)
    listeners = share(heard, XY, NXY)
    near = share(sent, Z, NZ)
    far = lax.ppermute(near, "core", swap)

    gains = shape(ROWS, HALF, dtype=BF16)
    work = dict(flops=2 * ROWS * HALF * 512, bytes_accessed=1 << 23)
    outs = (shape(ROWS, BANDS), gains, gains)
    near_place = jnp.stack([*place, at["core"]])
    far_place = jnp.stack([*place, 1 - at["core"]])
    part, near_high, near_low = call(
        lambda *refs: interfere_kernel(True, *refs), outs, 3, smem=(0,), **work
    )(near_place, near, listeners)
    part, far_high, far_low = call(
        lambda *refs: interfere_kernel(False, *refs), outs, 4, smem=(0,), **work
    )(far_place, far, listeners, part)

    parts = lax.all_to_all(part.reshape(NXY, BLOCK, BANDS), XY, 0, 0)
    users = jnp.stack([weight, fairness])
    block = shape(BLOCK, BANDS)
    quality, own, pressure = call(derive_kernel, (block, block, block), 4)(
        parts, mine, listener_xy, users
    )
    own_here = lax.ppermute(own, AXES, to_sender)
    pressures = share(pressure, XY, NXY)

    react = call(react_kernel, shape(HALF, BANDS), 3, **work)
    pushed_far = react(pressures, far_high, far_low)
    pushed_far = lax.ppermute(pushed_far, "core", swap)
    pushed_near = react(pressures, near_high, near_low)
    pushed = pushed_near + pushed_far
    parts = lax.all_to_all(pushed.reshape(NZ, BLOCK, BANDS), Z, 0, 0)
    gradient, new_power, gap = call(finish_kernel, (block, block, shape(1, BANDS)), 4, smem=(0,))(
        step_code, parts, own_here, powers
    )
    gap = jnp.sum(share(gap, (*Z, "core"), 2 * NZ), axis=0)
    gap = jnp.sum(share(gap, XY, NXY))
    return quality, gradient, new_power, (gap / (USERS * BANDS)).reshape(1)


def solution(mesh):
    sizes = (8, 4, 4, 2, 2)
    fine = Mesh(mesh.devices.reshape(sizes), AXES)
    rx, tx = ("zlo", "x"), ("y", "zhi", "core")
    by_sender, by_receiver = (*tx, *rx), (*rx, *tx)
    return jax.shard_map(
        per_device,
        mesh=fine,
        in_specs=(
            P(None, by_sender),
            P(None, by_receiver),
            P(by_sender, None),
            P(by_receiver),
            P(by_receiver),
            P(),
        ),
        out_specs=(P(by_receiver, None), P(by_sender, None), P(by_sender, None), P()),
        check_vma=False,
    )
```

time: 1120 us -> 200 us (0.18)
  waiting for transfers between devices: 695 us -> 29.4 us
  blocking collectives: 371 us -> 110 us
  starting transfers between devices: 0.16 us -> 33.5 us
  matrix products: 25.6 us -> 0 us
  between operations: 16.3 us -> 3.24 us
  Pallas kernels: 0 us -> 12.4 us
    psum x1 -> x0, waiting for transfers between devices: 437 us -> none  [per_device(): totals = lax.psum(own_full - pushed, 'rx')]
    all_gather x4 -> x0, blocking collectives: 248 us -> none  [the longest x1 104 us: per_device(): lax.all_gather(sender_xy, 'rx', axis=1, tiled=True)]
    reduce_scatter x2 -> x0, waiting for transfers between devices: 208 us -> none  [the longest x1 111 us: per_device(): lax.psum_scatter(signal_part, 'tx', scatter_dimension=0, tiled=True)]
    psum x1 -> x0, blocking collectives: 124 us -> none  [per_device(): gap_sum = lax.psum(gap_local, ('rx', 'tx'))]
    all_to_all x0 -> x4, blocking collectives: none -> 110 us  [share(): lax.all_to_all(jnp.broadcast_to(value[None], (count, *value.shape)), axes...]
    all_gather x1 -> x0, waiting for transfers between devices: 49.7 us -> none  [per_device(): lax.all_gather(powers, 'rx', axis=0, tiled=True)]
    dot_general x2 -> x0, matrix products: 25.6 us -> none  [the longest x1 16.3 us: per_device(): lax.dot_general(crossing, pressure_all, (((0,), (0,)), ((), ())), precisi...]
    all_to_all x0 -> x3, waiting for transfers between devices: none -> 22.4 us  [the longest x1 16 us: per_device(): parts = lax.all_to_all(pushed.reshape(NZ, BLOCK, BANDS), Z, 0, 0)]
  transfers between devices with their start and end apart: 4 -> 7, of which waited for: 4 -> 5; matrix products, arithmetic and copies ran while one was open for 1% -> 0% of each run, Pallas kernels for 0% -> 3%
where the time goes in v1:
time: 200 us; the launch traced here: 199 us
  blocking collectives  110 us (55%)
  starting transfers between devices  33.5 us (17%)
  waiting for transfers between devices  29.4 us (15%)
  Pallas kernels  12.4 us (6%)
  local copies, waits for them, and re-layouts  8.59 us (4%)
  between operations  3.24 us (2%)
    all_to_all x4, blocking collectives, share(): lax.all_to_all(jnp.broadcast_to(value[None], (count, *value.shape)), axes...  110 us
    all_to_all x1, waiting for transfers between devices, per_device(): parts = lax.all_to_all(pushed.reshape(NZ, BLOCK, BANDS), Z, 0, 0)  16 us
    unnamed x26, local copies, waits for them, and re-layouts  7.69 us
    all_to_all x1, starting transfers between devices, share(): lax.all_to_all(jnp.broadcast_to(value[None], (count, *value.shape)), axes...  6.75 us
    all_to_all x1, waiting for transfers between devices, share(): lax.all_to_all(jnp.broadcast_to(value[None], (count, *value.shape)), axes...  6.34 us
    ppermute x1, starting transfers between devices, per_device(): mine = lax.ppermute(sent, AXES, to_receiver)  6.31 us
    ppermute x1, starting transfers between devices, per_device(): far = lax.ppermute(near, 'core', swap)  5.51 us
    ppermute x1, starting transfers between devices, per_device(): pushed_far = lax.ppermute(pushed_far, 'core', swap)  5.14 us
  transfers between devices with their start and end apart: 7, of which 5 were waited for; matrix products, arithmetic and copies ran while one was open for 0% of the time, Pallas kernels for 3%

profile of v1, /device:TPU:1, one launch (start us, length us, event | category | flops | bytes accessed | tf_op | source)
XLA Modules:
  0.0 198.7 jit_solution(7422125206140485022)
XLA Ops:
  0.6 0.0 copy-start.6
  0.6 0.7 copy-done.6
  1.4 0.0 copy-start.8
  1.4 0.7 copy-done.8
  2.1 0.0 copy-start.10
  2.1 0.7 copy-done.10
  2.8 47.8 %all_to_all.35.refs_1_ = f32[16,72,128]{2,1,0:T(8,128)S(1)} all-to-all(f32[16,72,128]{2,1,0:T(8,128)S(1)} %broadcast_in_dim.12), channel_id=1, replica_groups=mesh['zlo'=8,'x'=4,'y'=4,'zhi'=2,'core'=2] {'zhi','zlo'}, dimensions={0} | all-to-all | bytes 1179648 | tf_op jit(solution)/shard_map/all_to_all | solution.py:183
  50.6 5.5 %collective-permute-start = (f32[16,72,128]{2,1,0:T(8,128)S(1)}, f32[16,72,128]{2,1,0:T(8,128)S(1)}, u32[]{:S(2)}, u32[]{:S(2)}) collective-permute-start(f32[16,72,128]{2,1,0:T(8,128)S(1)} %all_to_all.35.refs_1_), channel_id=1, source_target_pairs={{0,1},{1,0},{2,3},{3,2},{4,5},{5,4},{6,7},{7,6},{8,9},{9,8},{10,11... | collective-permute-start | bytes 1769480 | tf_op jit(solution)/shard_map/ppermute | solution.py:199
  56.2 0.6 broadcast_in_dim.13
  56.8 6.8 %all-to-all-start.1 = ((f32[16,8,128]{2,1,0:T(8,128)}), f32[16,8,128]{2,1,0:T(8,128)S(1)}, u32[]{:S(2)}, u32[]{:S(2)}) async-start(f32[16,8,128]{2,1,0:T(8,128)} %broadcast_in_dim.13), calls=%async_computation.1 | async-start | bytes 131072 | tf_op jit(solution)/shard_map/all_to_all | solution.py:183
  63.6 0.1 stack.46.refs_0_
  63.6 0.1 stack.45.refs_0_
  63.7 6.3 %all-to-all-done.1.refs_2_ = f32[16,8,128]{2,1,0:T(8,128)S(1)} async-done(((f32[16,8,128]{2,1,0:T(8,128)}), f32[16,8,128]{2,1,0:T(8,128)S(1)}, u32[]{:S(2)}, u32[]{:S(2)}) %all-to-all-start.1) | async-done | bytes 65568 | tf_op jit(solution)/shard_map/all_to_all | solution.py:183
  70.1 3.6 %shard_map.94 = (f32[1024,128]{1,0:T(8,128)S(1)}, bf16[1024,1024]{1,0:T(8,128)(2,1)S(1)}, bf16[1024,1024]{1,0:T(8,128)(2,1)S(1)}) custom-call(s32[6]{0:T(128)S(1)} %stack.46.refs_0_, f32[16,72,128]{2,1,0:T(8,128)S(1)} %all_to_all.35.refs_1_, f32[16,8,128]{2,1,0:T(8,128)S(1)} %all-to-all-done.1.refs_2_), custom_call_target="tpu_custom_call" | custom-call | flops 1073741824 | bytes 8388608 | tf_op jit(solution)/shard_map/pallas_call | solution.py:206
  73.7 0.0 copy-start
  73.7 1.3 copy-done
  75.0 0.0 collective-permute-done.refs_1_
  75.0 0.0 copy-start.11
  75.0 4.5 %shard_map.95 = (f32[1024,128]{1,0:T(8,128)}, bf16[1024,1024]{1,0:T(8,128)(2,1)S(1)}, bf16[1024,1024]{1,0:T(8,128)(2,1)S(1)}) custom-call(s32[6]{0:T(128)S(1)} %stack.45.refs_0_, f32[16,72,128]{2,1,0:T(8,128)S(1)} %collective-permute-done.refs_1_, f32[16,8,128]{2,1,0:T(8,128)S(1)} %all-to-all-done.1.refs_2_, f32[1024,128]{1,0:T(8,128)S(1)} %get-tuple-element.20.refs_3_), custom_call_target="tpu_custom_call" | custom-call | flops 1073741824 | bytes 8388608 | tf_op jit(solution)/shard_map/pallas_call | solution.py:209
  79.5 1.3 copy-done.2
  80.8 1.3 copy-done.4
  82.2 3.6 %all-to-all-start.2 = ((f32[16,64,128]{2,1,0:T(8,128)}), f32[16,64,128]{2,1,0:T(8,128)S(1)}, u32[]{:S(2)}, u32[]{:S(2)}) async-start(f32[16,64,128]{2,1,0:T(8,128)} %bitcast.6), calls=%async_computation.2 | async-start | bytes 1048576 | tf_op jit(solution)/shard_map/all_to_all | solution.py:213
  85.7 6.3 %collective-permute-start.1 = (f32[72,128]{1,0:T(8,128)S(1)}, f32[72,128]{1,0:T(8,128)S(1)}, u32[]{:S(2)}, u32[]{:S(2)}) collective-permute-start(f32[72,128]{1,0:T(8,128)S(1)} %get-tuple-element.18), channel_id=1, source_target_pairs={{0,0},{16,1},{32,2},{48,3},{64,4},{80,5},{96,6},{112,7},{128,8},{1... | collective-permute-start | bytes 110600 | tf_op jit(solution)/shard_map/ppermute | solution.py:196
  92.1 0.0 copy-done.11
  92.1 0.0 copy-done.12
  92.1 2.8 %collective-permute-done.1.mine_ref = f32[72,128]{1,0:T(8,128)S(1)} collective-permute-done((f32[72,128]{1,0:T(8,128)S(1)}, f32[72,128]{1,0:T(8,128)S(1)}, u32[]{:S(2)}, u32[]{:S(2)}) %collective-permute-start.1) | collective-permute-done | bytes 36896 | tf_op jit(solution)/shard_map/ppermute | solution.py:196
  94.9 0.0 all-to-all-done.2.parts_ref
  94.9 0.0 copy-done.9
  94.9 0.8 shard_map.96
  95.7 23.2 %all_to_all.36.pressure_ref = f32[16,64,128]{2,1,0:T(8,128)S(1)} all-to-all(f32[16,64,128]{2,1,0:T(8,128)S(1)} %broadcast_in_dim.14), channel_id=1, replica_groups=mesh['zlo'=8,'x'=4,'y'=4,'zhi'=2,'core'=2] {'x','y'}, dimensions={0} | all-to-all | bytes 1048576 | tf_op jit(solution)/shard_map/all_to_all | solution.py:183
  119.0 0.0 copy-done.3
  119.0 1.6 copy-done.5
  120.6 1.4 shard_map.98
  122.0 5.1 %collective-permute-start.2 = (f32[1024,128]{1,0:T(8,128)S(1)}, f32[1024,128]{1,0:T(8,128)S(1)}, u32[]{:S(2)}, u32[]{:S(2)}) collective-permute-start(f32[1024,128]{1,0:T(8,128)S(1)} %shard_map.98), channel_id=1, source_target_pairs={{0,1},{1,0},{2,3},{3,2},{4,5},{5,4},{6,7},{7,6},{8,9},{9,8},{10,11... | collective-permute-start | bytes 1572872 | tf_op jit(solution)/shard_map/ppermute | solution.py:224
  127.1 0.0 copy-done.1
  127.1 1.4 shard_map.97
  128.5 0.0 copy-start.7
  128.5 0.1 collective-permute-done.2
  128.6 0.9 add.3
  129.5 4.3 %all-to-all-start.4 = ((f32[16,64,128]{2,1,0:T(8,128)}), f32[16,64,128]{2,1,0:T(8,128)S(1)}, u32[]{:S(2)}, u32[]{:S(2)}) async-start(f32[16,64,128]{2,1,0:T(8,128)} %bitcast.9), calls=%async_computation.4 | async-start | bytes 1048576 | tf_op jit(solution)/shard_map/all_to_all | solution.py:227
  133.8 1.9 collective-permute-start.3
  136.4 4.2 %collective-permute-done.3.own_ref = f32[64,128]{1,0:T(8,128)S(1)} collective-permute-done((f32[64,128]{1,0:T(8,128)S(1)}, f32[64,128]{1,0:T(8,128)S(1)}, u32[]{:S(2)}, u32[]{:S(2)}) %collective-permute-start.3) | collective-permute-done | bytes 32800 | tf_op jit(solution)/shard_map/ppermute | solution.py:219
  140.5 16.0 %all-to-all-done.4.parts_ref = f32[16,64,128]{2,1,0:T(8,128)S(1)} async-done(((f32[16,64,128]{2,1,0:T(8,128)}), f32[16,64,128]{2,1,0:T(8,128)S(1)}, u32[]{:S(2)}, u32[]{:S(2)}) %all-to-all-start.4) | async-done | bytes 524320 | tf_op jit(solution)/shard_map/all_to_all | solution.py:227
  156.5 0.0 copy-done.7
  156.5 0.7 shard_map.99
  157.2 27.4 %all_to_all.37 = f32[32,1,128]{2,1,0:T(1,128)S(1)} all-to-all(f32[32,1,128]{2,1,0:T(1,128)S(1)} %broadcast_in_dim.16), channel_id=1, replica_groups=mesh['zlo'=8,'x'=4,'y'=4,'zhi'=2,'core'=2] {'zhi','zlo','core'}, dimensions={0} | all-to-all | bytes 32768 | tf_op jit(solution)/shard_map/all_to_all | solution.py:183
  184.7 11.7 %all_to_all.38 = f32[16,1,128]{2,1,0:T(1,128)S(1)} all-to-all(f32[16,1,128]{2,1,0:T(1,128)S(1)} %broadcast_in_dim.17), channel_id=1, replica_groups=mesh['zlo'=8,'x'=4,'y'=4,'zhi'=2,'core'=2] {'x','y'}, dimensions={0} | all-to-all | bytes 16384 | tf_op jit(solution)/shard_map/all_to_all | solution.py:183
  196.4 0.6 reduce_sum.19
  (14 shorter events, 0.2 us)
Async XLA Ops:
  0.6 0.8 copy-start.6
  1.4 0.7 copy-start.8
  2.1 0.7 copy-start.10
  50.6 24.4 %collective-permute-start = (f32[16,72,128]{2,1,0:T(8,128)S(1)}, f32[16,72,128]{2,1,0:T(8,128)S(1)}, u32[]{:S(2)}, u32[]{:S(2)}) collective-permute-start(f32[16,72,128]{2,1,0:T(8,128)S(1)} %all_to_all.35.refs_1_), channel_id=1, source_target_pairs={{0,1},{1,0},{2,3},{3,2},{4,5},{5,4},{6,7},{7,6},{8,9},{9,8},{10,11... | collective-permute-start | bytes 1769480 | tf_op jit(solution)/shard_map/ppermute | solution.py:199
  56.8 13.3 %all-to-all-start.1 = ((f32[16,8,128]{2,1,0:T(8,128)}), f32[16,8,128]{2,1,0:T(8,128)S(1)}, u32[]{:S(2)}, u32[]{:S(2)}) async-start(f32[16,8,128]{2,1,0:T(8,128)} %broadcast_in_dim.13), calls=%async_computation.1 | async-start | bytes 131072 | tf_op jit(solution)/shard_map/all_to_all | solution.py:183
  73.7 1.3 copy-start
  75.0 17.0 %copy-start.11 = (s32[64]{0:T(128)S(1)}, s32[64]{0:T(128)}, u32[]{:S(2)}) copy-start(s32[64]{0:T(128)} %param.10) | copy-start | bytes 772
  75.0 17.0 %copy-start.12 = (s32[64]{0:T(128)S(1)}, s32[64]{0:T(128)}, u32[]{:S(2)}) copy-start(s32[64]{0:T(128)} %param.9) | copy-start | bytes 772
  75.0 19.8 %copy-start.9 = (s32[2,64]{1,0:T(2,128)S(1)}, s32[2,64]{1,0:T(2,128)}, u32[]{:S(2)}) copy-start(s32[2,64]{1,0:T(2,128)} %listener_ref.3) | copy-start | bytes 1540
  79.5 1.3 copy-start.2
  80.8 1.3 copy-start.4
  82.2 12.7 %all-to-all-start.2 = ((f32[16,64,128]{2,1,0:T(8,128)}), f32[16,64,128]{2,1,0:T(8,128)S(1)}, u32[]{:S(2)}, u32[]{:S(2)}) async-start(f32[16,64,128]{2,1,0:T(8,128)} %bitcast.6), calls=%async_computation.2 | async-start | bytes 1048576 | tf_op jit(solution)/shard_map/all_to_all | solution.py:213
  85.7 9.1 %collective-permute-start.1 = (f32[72,128]{1,0:T(8,128)S(1)}, f32[72,128]{1,0:T(8,128)S(1)}, u32[]{:S(2)}, u32[]{:S(2)}) collective-permute-start(f32[72,128]{1,0:T(8,128)S(1)} %get-tuple-element.18), channel_id=1, source_target_pairs={{0,0},{16,1},{32,2},{48,3},{64,4},{80,5},{96,6},{112,7},{128,8},{1... | collective-permute-start | bytes 110600 | tf_op jit(solution)/shard_map/ppermute | solution.py:196
  94.9 24.1 %copy-start.3 = (bf16[1024,1024]{1,0:T(8,128)(2,1)S(1)}, bf16[1024,1024]{1,0:T(8,128)(2,1)}, u32[]{:S(2)}) copy-start(bf16[1024,1024]{1,0:T(8,128)(2,1)} %copy-done.2) | copy-start | bytes 6291460
  119.0 1.6 copy-start.5
  120.6 6.6 %copy-start.1 = (bf16[1024,1024]{1,0:T(8,128)(2,1)S(1)}, bf16[1024,1024]{1,0:T(8,128)(2,1)}, u32[]{:S(2)}) copy-start(bf16[1024,1024]{1,0:T(8,128)(2,1)} %copy-done) | copy-start | bytes 6291460
  122.0 6.7 %collective-permute-start.2 = (f32[1024,128]{1,0:T(8,128)S(1)}, f32[1024,128]{1,0:T(8,128)S(1)}, u32[]{:S(2)}, u32[]{:S(2)}) collective-permute-start(f32[1024,128]{1,0:T(8,128)S(1)} %shard_map.98), channel_id=1, source_target_pairs={{0,1},{1,0},{2,3},{3,2},{4,5},{5,4},{6,7},{7,6},{8,9},{9,8},{10,11... | collective-permute-start | bytes 1572872 | tf_op jit(solution)/shard_map/ppermute | solution.py:224
  128.5 28.0 %copy-start.7 = (f32[64,128]{1,0:T(8,128)S(1)}, f32[64,128]{1,0:T(8,128)}, u32[]{:S(2)}) copy-start(f32[64,128]{1,0:T(8,128)} %powers_ref.3) | copy-start | bytes 98308
  129.5 27.0 %all-to-all-start.4 = ((f32[16,64,128]{2,1,0:T(8,128)}), f32[16,64,128]{2,1,0:T(8,128)S(1)}, u32[]{:S(2)}, u32[]{:S(2)}) async-start(f32[16,64,128]{2,1,0:T(8,128)} %bitcast.9), calls=%async_computation.4 | async-start | bytes 1048576 | tf_op jit(solution)/shard_map/all_to_all | solution.py:227
  133.8 6.7 %collective-permute-start.3 = (f32[64,128]{1,0:T(8,128)S(1)}, f32[64,128]{1,0:T(8,128)S(1)}, u32[]{:S(2)}, u32[]{:S(2)}) collective-permute-start(f32[64,128]{1,0:T(8,128)S(1)} %get-tuple-element.28), channel_id=1, source_target_pairs={{0,0},{1,16},{2,32},{3,48},{4,64},{5,80},{6,96},{7,112},{8,128},{9... | collective-permute-start | bytes 98312 | tf_op jit(solution)/shard_map/ppermute | solution.py:219

commit v2 on v1

v2 whole, which is shorter than its diff:
```python
import functools

import jax
import jax.numpy as jnp
from jax import lax
from jax.experimental import pallas as pl
from jax.experimental.pallas import tpu as pltpu
from jax.sharding import Mesh
from jax.sharding import PartitionSpec as P

NOISE_POWER = 0.05
ARRAY_GAIN = 32.0
WEIGHT_UNIT = 1.0 / 16.0
PEAK_POWER = 1.0

AXES = ("z2", "z1", "z0", "x", "y", "zhi", "core")
SIZES = (2, 2, 2, 4, 4, 2, 2)
EVEN = ("zhi", "z2", "z1")
Z = ("z0", *EVEN)
XY = ("x", "y")
NZ, NXY = 16, 16
BLOCK, BANDS = 64, 128
SENT = BLOCK + 8
HALF = NZ * BLOCK
ROWS = NXY * BLOCK
USERS = 32768
VMEM_LIMIT = 20 * 1024 * 1024
F32, BF16 = jnp.float32, jnp.bfloat16
PLACE = ("x", "y", "z0", "z2", "z1", "zhi", "core")


def whole():
    return pl.BlockSpec(memory_space=pltpu.VMEM)


def call(kernel, outs, n_in, flops=0, bytes_accessed=1 << 20, smem=()):
    def spec(i):
        return pl.BlockSpec(memory_space=pltpu.SMEM) if i in smem else whole()

    many = isinstance(outs, (list, tuple))
    return pl.pallas_call(
        kernel,
        out_shape=outs,
        in_specs=[spec(i) for i in range(n_in)],
        out_specs=[whole() for _ in outs] if many else whole(),
        compiler_params=pltpu.CompilerParams(vmem_limit_bytes=VMEM_LIMIT),
        cost_estimate=pl.CostEstimate(flops=flops, bytes_accessed=bytes_accessed, transcendentals=0),
    )


def shape(*dims, dtype=F32):
    return jax.ShapeDtypeStruct(dims, dtype)


def split_norm(norm):
    low = norm & 511
    odd = low & 1
    return norm - low, low - odd, odd


def pack_kernel(sender_ref, listener_ref, powers_ref, sent_ref, heard_ref):
    sx, sy = sender_ref[0:1, :], sender_ref[1:2, :]
    lx, ly = listener_ref[0:1, :], listener_ref[1:2, :]
    one = jnp.ones_like(sx)
    s1, s2, s3 = split_norm(sx * sx + sy * sy)
    l1, l2, l3 = split_norm(lx * lx + ly * ly + 1)
    sent = jnp.concatenate([-2 * sx, -2 * sy, one, one, one, s1, s2, s3], axis=0).astype(F32)
    heard = jnp.concatenate([lx, ly, l1, l2, l3, one, one, one], axis=0).astype(F32)
    pad = jnp.zeros_like(sent)
    sent = jnp.concatenate([sent, pad], axis=1)
    heard_ref[...] = jnp.concatenate([heard, pad], axis=1)
    powers = powers_ref[...]
    for k in range(NZ):
        sent_ref[k, 0:BLOCK, :] = powers
        sent_ref[k, BLOCK:SENT, :] = sent


def spread(parts, row, index):
    pieces = []
    for k in range(0, 16, 2):
        left = parts[index(k), row : row + 8, 0:BLOCK]
        right = parts[index(k + 1), row : row + 8, 0:BLOCK]
        pieces.append(jnp.concatenate([left, right], axis=1))
    features = jnp.concatenate(pieces, axis=1)
    return jnp.concatenate([features, jnp.zeros_like(features)], axis=0).astype(BF16)


def split(value):
    high = value.astype(BF16)
    low = (value - high.astype(F32)).astype(BF16)
    return high, low


def interfere_kernel(first, place_ref, sent_ref, heard_ref, *rest):
    if first:
        total_ref, high_ref, low_ref = rest
    else:
        near_ref, before_ref, total_ref, high_ref, low_ref = rest
    x, y, z0, z2, z1, zhi, core = (place_ref[i] for i in range(7))
    source_core = core if first else 1 - core
    senders = spread(sent_ref, BLOCK, lambda k: k)
    listeners = spread(heard_ref, 0, lambda k: (((k & 3) ^ y) << 2) | ((k >> 2) ^ x))
    powers = sent_ref[:, 0:BLOCK, :].reshape(HALF, BANDS)
    power_high, power_low = split(powers)
    power_both = jnp.concatenate([power_high, power_low], axis=1)
    tile_rows, tile_cols = 256, 128
    per_tile = tile_rows // BLOCK
    receiver_base = (z2 * 4 + z1 * 2 + z0) * 4096 + zhi * 128 + core * 64
    sender_base = y * 8192 + source_core * 2048 + x * 64
    for r in range(0, ROWS, tile_rows):
        row = lax.broadcasted_iota(jnp.int32, (tile_rows, tile_cols), 0) + r
        block = row >> 6
        row_id = receiver_base + (block >> 2) * 1024 + (block & 3) * 256 + (row & 63)
        for c in range(0, HALF, tile_cols):
            col = lax.broadcasted_iota(jnp.int32, (1, tile_cols), 1) + c
            zed = col >> 6
            zlo = ((zed >> 1) & 1) * 4 + (zed & 1) * 2 + (zed >> 3)
            col_id = sender_base + ((zed >> 2) & 1) * 4096 + zlo * 256 + (col & 63)
            square = lax.dot_general(
                listeners[:, r : r + tile_rows],
                senders[:, c : c + tile_cols],
                (((0,), (0,)), ((), ())),
                preferred_element_type=F32,
            )
            guess = pl.reciprocal(square, approx=True)
            gain = guess * (2.0 - square * guess)
            gain = jnp.where(row_id == col_id, 0.0, gain)
            high, low = split(gain)
            high_ref[r : r + tile_rows, c : c + tile_cols] = high
            low_ref[r : r + tile_rows, c : c + tile_cols] = low
        product = jnp.dot(high_ref[r : r + tile_rows, :], power_both, preferred_element_type=F32)
        product = product + jnp.dot(
            low_ref[r : r + tile_rows, :], power_both, preferred_element_type=F32
        )
        part = product[:, :BANDS] + product[:, BANDS:]
        if first:
            total_ref[r : r + tile_rows, :] = part
        else:
            k = r // BLOCK
            part = part + before_ref[r : r + tile_rows, :]
            total_ref[k : k + per_tile, 0:BLOCK, :] = part.reshape(per_tile, BLOCK, BANDS)
    if not first:
        for k in range(NXY):
            there_x, there_y = k >> 2, k & 3
            at = (there_y & 1) * 8 + z0 * 4 + (there_x & 1) * 2 + (there_y >> 1)
            total_ref[k, BLOCK:, :] = jnp.where(
                core == there_x >> 1, near_ref[at], sent_ref[at]
            )


def react_kernel(place_ref, pressure_ref, high_ref, low_ref, pushed_ref, *, other):
    pressure = pressure_ref[...].reshape(ROWS, BANDS).T
    pressure_high, pressure_low = split(pressure)
    both = jnp.concatenate([pressure_high, pressure_low], axis=0)
    parity = 1 - place_ref[2] if other else place_ref[2]
    step = 256
    for c in range(0, HALF // 2, step):
        columns = pl.ds(pl.multiple_of(parity * (HALF // 2) + c, step), step)
        product = jnp.dot(both, high_ref[:, columns], preferred_element_type=F32)
        product = product + jnp.dot(both, low_ref[:, columns], preferred_element_type=F32)
        pushed_ref[c : c + step, :] = (product[:BANDS, :] + product[BANDS:, :]).T


def add_kernel(*refs):
    total = refs[0][...]
    for ref in refs[1:-1]:
        total = total + ref[...]
    refs[-1][...] = total


def add(*parts):
    size = 4 * parts[0].size
    return call(add_kernel, shape(*parts[0].shape), len(parts), parts[0].size, 3 * size)(*parts)


def add_blocks(ref, count):
    total = ref[0, 0:BLOCK, :]
    for k in range(1, count):
        total = total + ref[k, 0:BLOCK, :]
    return total


def derive_kernel(
    place_ref, parts_ref, listener_ref, weight_ref, fair_ref, quality_ref, own_ref, pressure_ref
):
    interference = add_blocks(parts_ref, NXY)
    z2, z1, zhi, core = (place_ref[i] for i in range(3, 7))
    source = (zhi * 2 + core) * 4 + z2 * 2 + z1
    powers = parts_ref[source, BLOCK : 2 * BLOCK, :]
    place = -0.5 * parts_ref[source, 2 * BLOCK :, :]
    sx, sy = place[0:1, 0:BLOCK], place[1:2, 0:BLOCK]
    dx = listener_ref[0:1, :].astype(F32) - sx
    dy = listener_ref[1:2, :].astype(F32) - sy
    own_gain = 1.0 / (1.0 + dx * dx + dy * dy)
    weight = WEIGHT_UNIT * weight_ref[...].astype(F32)
    fair = fair_ref[...].astype(F32)
    rows = jnp.concatenate([own_gain, weight, fair, jnp.zeros((5, BLOCK), F32)], axis=0)
    rows = jnp.concatenate([rows, jnp.zeros_like(rows)], axis=1)
    columns = jnp.concatenate([rows, jnp.zeros((120, 128), F32)], axis=0).T
    own_gain = columns[0:BLOCK, 0:1]
    weight = columns[0:BLOCK, 1:2]
    fair = columns[0:BLOCK, 2:3]
    signal = ARRAY_GAIN * own_gain * powers
    denominator = NOISE_POWER + interference
    quality = signal / denominator
    marginal = weight * jnp.exp(-fair * jnp.log(quality)) / denominator
    quality_ref[...] = quality
    own_ref[...] = ARRAY_GAIN * own_gain * marginal
    pressure = marginal * quality
    for k in range(NXY):
        pressure_ref[k] = pressure


def finish_kernel(step_ref, parts_ref, own_ref, powers_ref, gradient_ref, power_ref, gap_ref):
    gradient = own_ref[...] - add_blocks(parts_ref, NZ // 2)
    powers = powers_ref[...]
    target = PEAK_POWER * jax.nn.sigmoid(gradient)
    step_size = step_ref[0].astype(F32) / 4096.0
    gradient_ref[...] = gradient
    power_ref[...] = powers + step_size * (target - powers)
    gap = PEAK_POWER * jnp.maximum(gradient, 0.0) - gradient * powers
    gap = jnp.sum(gap, axis=0, keepdims=True)
    for k in range(2 * NZ):
        gap_ref[k] = gap


def share(value, axes, count):
    return lax.all_to_all(jnp.broadcast_to(value[None], (count, *value.shape)), axes, 0, 0)


def per_device(sender_xy, listener_xy, powers, weight, fairness, step_code):
    place = jnp.stack([lax.axis_index(name).astype(jnp.int32) for name in PLACE])
    to_sender = [(b, (b % 32) * 16 + b // 32) for b in range(512)]
    swap = [(0, 1), (1, 0)]

    sent, heard = call(pack_kernel, (shape(NZ, SENT, BANDS), shape(8, 128)), 3)(
        sender_xy, listener_xy, powers
    )
    near = lax.all_to_all(sent, Z, 0, 0)
    for axis in XY:
        for bit in (1, 2):
            other = lax.ppermute(heard, axis, [(i, i ^ bit) for i in range(4)])
            heard = jnp.concatenate([heard, other], axis=0)
    near, heard = lax.optimization_barrier((near, heard))
    listeners = heard.reshape(NXY, 8, 128)
    far = lax.ppermute(near, "core", swap)

    gains = shape(ROWS, HALF, dtype=BF16)
    work = dict(flops=2 * ROWS * HALF * 512, bytes_accessed=1 << 23)
    part, near_high, near_low = call(
        lambda *refs: interfere_kernel(True, *refs), (shape(ROWS, BANDS), gains, gains), 3, smem=(0,), **work
    )(place, near, listeners)
    parts, far_high, far_low = call(
        lambda *refs: interfere_kernel(False, *refs),
        (shape(NXY, BLOCK + SENT, BANDS), gains, gains),
        5,
        smem=(0,),
        **work,
    )(place, far, listeners, near, part)

    parts = lax.all_to_all(parts, XY, 0, 0)
    block = shape(BLOCK, BANDS)
    quality, own, pressure = call(
        derive_kernel, (block, block, shape(NXY, BLOCK, BANDS)), 5, smem=(0,)
    )(place, parts, listener_xy, weight[None], fairness[None])
    pressures = lax.all_to_all(pressure, XY, 0, 0)

    def react(pressures, high, low, other):
        kernel = functools.partial(react_kernel, other=other)
        quarter = dict(flops=work["flops"] // 2, bytes_accessed=1 << 21)
        return call(kernel, shape(HALF // 2, BANDS), 4, smem=(0,), **quarter)(
            place, pressures, high, low
        )

    across = lax.ppermute(react(pressures, far_high, far_low, True), "core", swap)
    pushed = add(react(pressures, near_high, near_low, True), across)
    pressures, pushed = lax.optimization_barrier((pressures, pushed))
    from_neighbour = lax.ppermute(pushed, "z0", swap)
    across = lax.ppermute(react(pressures, far_high, far_low, False), "core", swap)
    pushed = add(react(pressures, near_high, near_low, False), across, from_neighbour)
    own_here = lax.ppermute(own, AXES, to_sender)
    parts = lax.all_to_all(pushed.reshape(NZ // 2, BLOCK, BANDS), EVEN, 0, 0)
    gradient, new_power, gap = call(
        finish_kernel, (block, block, shape(2 * NZ, 1, BANDS)), 4, smem=(0,)
    )(step_code, parts, own_here, powers)
    gap = jnp.sum(lax.all_to_all(gap, (*Z, "core"), 0, 0), axis=0)
    gap = lax.all_to_all(jnp.broadcast_to(gap[None], (NXY, 1, BANDS)), XY, 0, 0)
    return quality, gradient, new_power, (jnp.sum(gap) / (USERS * BANDS)).reshape(1)


def solution(mesh):
    fine = Mesh(mesh.devices.reshape(SIZES), AXES)
    rx, tx = ("z2", "z1", "z0", "x"), ("y", "zhi", "core")
    by_sender, by_receiver = (*tx, *rx), (*rx, *tx)
    return jax.shard_map(
        per_device,
        mesh=fine,
        in_specs=(
            P(None, by_sender),
            P(None, by_receiver),
            P(by_sender, None),
            P(by_receiver),
            P(by_receiver),
            P(),
        ),
        out_specs=(P(by_receiver, None), P(by_sender, None), P(by_sender, None), P()),
        check_vma=False,
    )
```

time: 200 us -> 182 us (0.910)
  blocking collectives: 110 us -> 71.8 us
  starting transfers between devices: 33.5 us -> 58.5 us
  local copies, waits for them, and re-layouts: 8.59 us -> 2.25 us
  Pallas kernels: 12.4 us -> 16.6 us
    all_to_all x4, blocking collectives: 110 us -> 71.8 us  [the longest x1 24.9 us: per_device(): gap = jnp.sum(lax.all_to_all(gap, (*Z, 'core'), 0, 0), axis=0)]
    ppermute x2 -> x7, starting transfers between devices: 11.5 us -> 25.8 us  [the longest x4 15.8 us: per_device(): other = lax.ppermute(heard, axis, [(i, i ^ bit) for i in range(4)])]
    all_to_all x3 -> x2, waiting for transfers between devices: 22.4 us -> 14 us  [the longest x1 9.02 us: per_device(): parts = lax.all_to_all(pushed.reshape(NZ // 2, BLOCK, BANDS), EVEN, 0, 0)]
    all_to_all x3 -> x2, starting transfers between devices: 14.6 us -> 22.9 us  [the longest x1 15.7 us: per_device(): near = lax.all_to_all(sent, Z, 0, 0)]
    ppermute x2 -> x7, waiting for transfers between devices: 2.86 us -> 10.9 us  [the longest x4 5.68 us: per_device(): other = lax.ppermute(heard, axis, [(i, i ^ bit) for i in range(4)])]
    unnamed x26 -> x18, local copies, waits for them, and re-layouts: 7.69 us -> 2.15 us
    pallas_call x7 -> x11, Pallas kernels: 12.4 us -> 16.6 us  [the longest x4 5.61 us: react(): call(kernel, shape(HALF // 2, BANDS), 4, smem=(0,), **quarter)]
  transfers between devices with their start and end apart: 7 -> 11, of which waited for: 5 -> 8; matrix products, arithmetic and copies ran while one was open for 0% -> 0% of each run, Pallas kernels for 3% -> 4%
where the time goes in v2:
time: 182 us; the launch traced here: 181 us
  blocking collectives  71.8 us (39%)
  starting transfers between devices  58.5 us (32%)
  waiting for transfers between devices  28.2 us (15%)
  Pallas kernels  16.6 us (9%)
  between operations  3.31 us (2%)
  local copies, waits for them, and re-layouts  2.25 us (1%)
    all_to_all x1, blocking collectives, per_device(): gap = jnp.sum(lax.all_to_all(gap, (*Z, 'core'), 0, 0), axis=0)  24.9 us
    all_to_all x1, blocking collectives, per_device(): parts = lax.all_to_all(parts, XY, 0, 0)  24.2 us
    ppermute x4, starting transfers between devices, per_device(): other = lax.ppermute(heard, axis, [(i, i ^ bit) for i in range(4)])  15.8 us
    all_to_all x1, starting transfers between devices, per_device(): near = lax.all_to_all(sent, Z, 0, 0)  15.7 us
    all_to_all x1, blocking collectives, per_device(): pressures = lax.all_to_all(pressure, XY, 0, 0)  12.1 us
    all_to_all x1, blocking collectives, per_device(): gap = lax.all_to_all(jnp.broadcast_to(gap[None], (NXY, 1, BANDS)), XY, 0, 0)  10.7 us
    all_to_all x1, waiting for transfers between devices, per_device(): parts = lax.all_to_all(pushed.reshape(NZ // 2, BLOCK, BANDS), EVEN, 0, 0)  9.02 us
    all_to_all x1, starting transfers between devices, per_device(): parts = lax.all_to_all(pushed.reshape(NZ // 2, BLOCK, BANDS), EVEN, 0, 0)  7.18 us
  transfers between devices with their start and end apart: 11, of which 8 were waited for; matrix products, arithmetic and copies ran while one was open for 0% of the time, Pallas kernels for 4%

profile of v2, /device:TPU:1, one launch (start us, length us, event | category | flops | bytes accessed | tf_op | source)
XLA Modules:
  0.0 181.3 jit_solution(5894255006312337103)
XLA Ops:
  0.6 0.0 copy-start
  0.6 0.7 copy-done
  1.4 0.7 copy-done.2
  2.1 0.7 copy-done.4
  2.8 0.9 shard_map.93
  3.6 15.7 %all-to-all-start = ((f32[16,72,128]{2,1,0:T(8,128)}), f32[16,72,128]{2,1,0:T(8,128)S(1)}, u32[]{:S(2)}, u32[]{:S(2)}) async-start(f32[16,72,128]{2,1,0:T(8,128)} %get-tuple-element.22), calls=%async_computation | async-start | bytes 1179648 | tf_op jit(solution)/shard_map/all_to_all | solution.py:239
  19.4 3.1 %collective-permute-start = (f32[8,128]{1,0:T(8,128)S(1)}, f32[8,128]{1,0:T(8,128)S(1)}, u32[]{:S(2)}, u32[]{:S(2)}) collective-permute-start(f32[8,128]{1,0:T(8,128)S(1)} %get-tuple-element.23), channel_id=1, source_target_pairs={{0,16},{16,0},{32,48},{48,32},{1,17},{17,1},{33,49},{49,33},{2,18}... | collective-permute-start | bytes 12296 | tf_op jit(solution)/shard_map/ppermute | solution.py:242
  22.5 1.2 collective-permute-done
  23.7 4.6 %collective-permute-start.1 = (f32[16,128]{1,0:T(8,128)S(1)}, f32[16,128]{1,0:T(8,128)S(1)}, u32[]{:S(2)}, u32[]{:S(2)}) collective-permute-start(f32[16,128]{1,0:T(8,128)S(1)} %pad_maximum_fusion.2), channel_id=1, source_target_pairs={{0,32},{16,48},{32,0},{48,16},{1,33},{17,49},{33,1},{49,17},{2,34}... | collective-permute-start | bytes 24584 | tf_op jit(solution)/shard_map/ppermute | solution.py:242
  28.4 1.2 collective-permute-done.1
  29.6 3.2 %collective-permute-start.2 = (f32[32,128]{1,0:T(8,128)S(1)}, f32[32,128]{1,0:T(8,128)S(1)}, u32[]{:S(2)}, u32[]{:S(2)}) collective-permute-start(f32[32,128]{1,0:T(8,128)S(1)} %pad_maximum_fusion.1), channel_id=1, source_target_pairs={{0,4},{4,0},{8,12},{12,8},{1,5},{5,1},{9,13},{13,9},{2,6},{6,2},{1... | collective-permute-start | bytes 49160 | tf_op jit(solution)/shard_map/ppermute | solution.py:242
  32.8 1.6 collective-permute-done.2
  34.4 4.8 %collective-permute-start.3 = (f32[64,128]{1,0:T(8,128)S(1)}, f32[64,128]{1,0:T(8,128)S(1)}, u32[]{:S(2)}, u32[]{:S(2)}) collective-permute-start(f32[64,128]{1,0:T(8,128)S(1)} %pad_maximum_fusion), channel_id=1, source_target_pairs={{0,8},{4,12},{8,0},{12,4},{1,9},{5,13},{9,1},{13,5},{2,10},{6,14},... | collective-permute-start | bytes 98312 | tf_op jit(solution)/shard_map/ppermute | solution.py:242
  39.2 1.7 collective-permute-done.3
  40.9 5.0 %all-to-all-done.refs_1_.refs_3_ = f32[16,72,128]{2,1,0:T(8,128)S(1)} async-done(((f32[16,72,128]{2,1,0:T(8,128)}), f32[16,72,128]{2,1,0:T(8,128)S(1)}, u32[]{:S(2)}, u32[]{:S(2)}) %all-to-all-start) | async-done | bytes 589856 | tf_op jit(solution)/shard_map/all_to_all | solution.py:239
  45.9 7.0 %collective-permute-start.4 = (f32[16,72,128]{2,1,0:T(8,128)S(1)}, f32[16,72,128]{2,1,0:T(8,128)S(1)}, u32[]{:S(2)}, u32[]{:S(2)}) collective-permute-start(f32[16,72,128]{2,1,0:T(8,128)S(1)} %all-to-all-done.refs_1_.refs_3_), channel_id=1, source_target_pairs={{0,1},{1,0},{2,3},{3,2},{4,5},{5,4},{6,7},{7,6},{8,9},{9,8},{10,11... | collective-permute-start | bytes 1769480 | tf_op jit(solution)/shard_map/ppermute | solution.py:246
  52.9 0.1 stack.31.refs_0_.place_ref
  53.0 3.7 %shard_map.94 = (f32[1024,128]{1,0:T(8,128)S(1)}, bf16[1024,1024]{1,0:T(8,128)(2,1)S(1)}, bf16[1024,1024]{1,0:T(8,128)(2,1)S(1)}) custom-call(s32[7]{0:T(128)S(1)} %stack.31.refs_0_.place_ref, f32[16,72,128]{2,1,0:T(8,128)S(1)} %all-to-all-done.refs_1_.refs_3_, f32[16,8,128]{2,1,0:T(8,128)S(1)} %bitcast.15), custom_call_target="tpu_custom_call" | custom-call | flops 1073741824 | bytes 8388608 | tf_op jit(solution)/shard_map/pallas_call | solution.py:250
  56.6 0.0 collective-permute-done.4.refs_1_
  56.7 3.7 %shard_map.95 = (f32[16,136,128]{2,1,0:T(8,128)S(1)}, bf16[1024,1024]{1,0:T(8,128)(2,1)S(1)}, bf16[1024,1024]{1,0:T(8,128)(2,1)S(1)}) custom-call(s32[7]{0:T(128)S(1)} %stack.31.refs_0_.place_ref, f32[16,72,128]{2,1,0:T(8,128)S(1)} %collective-permute-done.4.refs_1_, f32[16,8,128]{2,1,0:T(8,128)S(1)} %bitcast.16, ...), custom_call_target="tpu_custom_call" | custom-call | flops 1073741824 | bytes 8388608 | tf_op jit(solution)/shard_map/pallas_call | solution.py:253
  60.4 0.0 copy-start.3
  60.4 0.0 copy-start.5
  60.4 0.0 copy-start.6
  60.4 24.2 %all_to_all.30.parts_ref = f32[16,136,128]{2,1,0:T(8,128)S(1)} all-to-all(f32[16,136,128]{2,1,0:T(8,128)S(1)} %get-tuple-element.27), channel_id=1, replica_groups=mesh['z2'=2,'z1'=2,'z0'=2,'x'=4,'y'=4,'zhi'=2,'core'=2] {'x','y'}, dimensions={0} | all-to-all | bytes 2228224 | tf_op jit(solution)/shard_map/all_to_all | solution.py:261
  84.6 0.0 copy-done.3
  84.6 1.3 shard_map.96
  86.0 12.1 %all_to_all.31.pressure_ref = f32[16,64,128]{2,1,0:T(8,128)S(1)} all-to-all(f32[16,64,128]{2,1,0:T(8,128)S(1)} %get-tuple-element.29), channel_id=1, replica_groups=mesh['z2'=2,'z1'=2,'z0'=2,'x'=4,'y'=4,'zhi'=2,'core'=2] {'x','y'}, dimensions={0} | all-to-all | bytes 1048576 | tf_op jit(solution)/shard_map/all_to_all | solution.py:266
  98.1 1.4 shard_map.98
  99.5 5.4 %collective-permute-start.5 = (f32[512,128]{1,0:T(8,128)S(1)}, f32[512,128]{1,0:T(8,128)S(1)}, u32[]{:S(2)}, u32[]{:S(2)}) collective-permute-start(f32[512,128]{1,0:T(8,128)S(1)} %shard_map.98), channel_id=1, source_target_pairs={{0,1},{1,0},{2,3},{3,2},{4,5},{5,4},{6,7},{7,6},{8,9},{9,8},{10,11... | collective-permute-start | bytes 786440 | tf_op jit(solution)/shard_map/ppermute | solution.py:275
  104.9 1.4 shard_map.97.refs_0_
  106.3 0.0 collective-permute-done.5.refs_1_
  106.3 1.4 shard_map.101
  107.7 0.0 copy-start.1
  107.7 2.0 %collective-permute-start.6 = (f32[512,128]{1,0:T(8,128)S(1)}, f32[512,128]{1,0:T(8,128)S(1)}, u32[]{:S(2)}, u32[]{:S(2)}) collective-permute-start(f32[512,128]{1,0:T(8,128)S(1)} %shard_map.101), channel_id=1, source_target_pairs={{0,1},{1,0},{2,3},{3,2},{4,5},{5,4},{6,7},{7,6},{8,9},{9,8},{10,11... | collective-permute-start | bytes 786440 | tf_op jit(solution)/shard_map/ppermute | solution.py:279
  109.7 2.7 %collective-permute-start.7 = (f32[512,128]{1,0:T(8,128)S(1)}, f32[512,128]{1,0:T(8,128)S(1)}, u32[]{:S(2)}, u32[]{:S(2)}) collective-permute-start(f32[512,128]{1,0:T(8,128)S(1)} %shard_map.99), channel_id=1, source_target_pairs={{0,64},{64,0},{1,65},{65,1},{2,66},{66,2},{3,67},{67,3},{4,68},{68... | collective-permute-start | bytes 786440 | tf_op jit(solution)/shard_map/ppermute | solution.py:278
  112.5 1.4 shard_map.100.refs_0_
  113.9 0.0 collective-permute-done.6.refs_1_
  113.9 5.2 %collective-permute-done.7.refs_2_ = f32[512,128]{1,0:T(8,128)S(1)} collective-permute-done((f32[512,128]{1,0:T(8,128)S(1)}, f32[512,128]{1,0:T(8,128)S(1)}, u32[]{:S(2)}, u32[]{:S(2)}) %collective-permute-start.7) | collective-permute-done | bytes 262176 | tf_op jit(solution)/shard_map/ppermute | solution.py:278
  119.1 0.7 shard_map.102
  119.8 7.2 %all-to-all-start.3 = ((f32[8,64,128]{2,1,0:T(8,128)}), f32[8,64,128]{2,1,0:T(8,128)S(1)}, u32[]{:S(2)}, u32[]{:S(2)}) async-start(f32[8,64,128]{2,1,0:T(8,128)} %bitcast.10), calls=%async_computation.3 | async-start | bytes 524288 | tf_op jit(solution)/shard_map/all_to_all | solution.py:282
  127.0 2.8 %collective-permute-start.8 = (f32[64,128]{1,0:T(8,128)S(1)}, f32[64,128]{1,0:T(8,128)S(1)}, u32[]{:S(2)}, u32[]{:S(2)}) collective-permute-start(f32[64,128]{1,0:T(8,128)S(1)} %get-tuple-element.36), channel_id=1, source_target_pairs={{0,0},{1,16},{2,32},{3,48},{4,64},{5,80},{6,96},{7,112},{8,128},{9... | collective-permute-start | bytes 98312 | tf_op jit(solution)/shard_map/ppermute | solution.py:281
  130.4 3.3 %collective-permute-done.8.own_ref = f32[64,128]{1,0:T(8,128)S(1)} collective-permute-done((f32[64,128]{1,0:T(8,128)S(1)}, f32[64,128]{1,0:T(8,128)S(1)}, u32[]{:S(2)}, u32[]{:S(2)}) %collective-permute-start.8) | collective-permute-done | bytes 32800 | tf_op jit(solution)/shard_map/ppermute | solution.py:281
  133.7 9.0 %all-to-all-done.3.parts_ref = f32[8,64,128]{2,1,0:T(8,128)S(1)} async-done(((f32[8,64,128]{2,1,0:T(8,128)}), f32[8,64,128]{2,1,0:T(8,128)S(1)}, u32[]{:S(2)}, u32[]{:S(2)}) %all-to-all-start.3) | async-done | bytes 262176 | tf_op jit(solution)/shard_map/all_to_all | solution.py:282
  142.7 0.7 shard_map.103
  143.4 24.9 %all_to_all.32 = f32[32,1,128]{2,1,0:T(1,128)S(1)} all-to-all(f32[32,1,128]{2,1,0:T(1,128)S(1)} %get-tuple-element.39), channel_id=1, replica_groups=mesh['z2'=2,'z1'=2,'z0'=2,'x'=4,'y'=4,'zhi'=2,'core'=2] {'z0','zhi','z2'..., dimensions={0} | all-to-all | bytes 32768 | tf_op jit(solution)/shard_map/all_to_all | solution.py:286
  168.3 0.1 reduce_sum.18
  168.3 10.7 %all_to_all.33 = f32[16,1,128]{2,1,0:T(1,128)S(1)} all-to-all(f32[16,1,128]{2,1,0:T(1,128)S(1)} %broadcast_in_dim.14), channel_id=1, replica_groups=mesh['z2'=2,'z1'=2,'z0'=2,'x'=4,'y'=4,'zhi'=2,'core'=2] {'x','y'}, dimensions={0} | all-to-all | bytes 16384 | tf_op jit(solution)/shard_map/all_to_all | solution.py:287
  179.0 0.6 reduce_sum.19
  (15 shorter events, 0.1 us)
Async XLA Ops:
  0.6 0.8 copy-start
  1.4 0.7 copy-start.2
  2.1 0.7 copy-start.4
  3.6 42.3 %all-to-all-start = ((f32[16,72,128]{2,1,0:T(8,128)}), f32[16,72,128]{2,1,0:T(8,128)S(1)}, u32[]{:S(2)}, u32[]{:S(2)}) async-start(f32[16,72,128]{2,1,0:T(8,128)} %get-tuple-element.22), calls=%async_computation | async-start | bytes 1179648 | tf_op jit(solution)/shard_map/all_to_all | solution.py:239
  19.4 4.4 %collective-permute-start = (f32[8,128]{1,0:T(8,128)S(1)}, f32[8,128]{1,0:T(8,128)S(1)}, u32[]{:S(2)}, u32[]{:S(2)}) collective-permute-start(f32[8,128]{1,0:T(8,128)S(1)} %get-tuple-element.23), channel_id=1, source_target_pairs={{0,16},{16,0},{32,48},{48,32},{1,17},{17,1},{33,49},{49,33},{2,18}... | collective-permute-start | bytes 12296 | tf_op jit(solution)/shard_map/ppermute | solution.py:242
  23.7 5.9 %collective-permute-start.1 = (f32[16,128]{1,0:T(8,128)S(1)}, f32[16,128]{1,0:T(8,128)S(1)}, u32[]{:S(2)}, u32[]{:S(2)}) collective-permute-start(f32[16,128]{1,0:T(8,128)S(1)} %pad_maximum_fusion.2), channel_id=1, source_target_pairs={{0,32},{16,48},{32,0},{48,16},{1,33},{17,49},{33,1},{49,17},{2,34}... | collective-permute-start | bytes 24584 | tf_op jit(solution)/shard_map/ppermute | solution.py:242
  29.6 4.8 %collective-permute-start.2 = (f32[32,128]{1,0:T(8,128)S(1)}, f32[32,128]{1,0:T(8,128)S(1)}, u32[]{:S(2)}, u32[]{:S(2)}) collective-permute-start(f32[32,128]{1,0:T(8,128)S(1)} %pad_maximum_fusion.1), channel_id=1, source_target_pairs={{0,4},{4,0},{8,12},{12,8},{1,5},{5,1},{9,13},{13,9},{2,6},{6,2},{1... | collective-permute-start | bytes 49160 | tf_op jit(solution)/shard_map/ppermute | solution.py:242
  34.4 6.5 %collective-permute-start.3 = (f32[64,128]{1,0:T(8,128)S(1)}, f32[64,128]{1,0:T(8,128)S(1)}, u32[]{:S(2)}, u32[]{:S(2)}) collective-permute-start(f32[64,128]{1,0:T(8,128)S(1)} %pad_maximum_fusion), channel_id=1, source_target_pairs={{0,8},{4,12},{8,0},{12,4},{1,9},{5,13},{9,1},{13,5},{2,10},{6,14},... | collective-permute-start | bytes 98312 | tf_op jit(solution)/shard_map/ppermute | solution.py:242
  45.9 10.8 %collective-permute-start.4 = (f32[16,72,128]{2,1,0:T(8,128)S(1)}, f32[16,72,128]{2,1,0:T(8,128)S(1)}, u32[]{:S(2)}, u32[]{:S(2)}) collective-permute-start(f32[16,72,128]{2,1,0:T(8,128)S(1)} %all-to-all-done.refs_1_.refs_3_), channel_id=1, source_target_pairs={{0,1},{1,0},{2,3},{3,2},{4,5},{5,4},{6,7},{7,6},{8,9},{9,8},{10,11... | collective-permute-start | bytes 1769480 | tf_op jit(solution)/shard_map/ppermute | solution.py:246
  60.4 24.2 %copy-start.3 = (s32[2,64]{1,0:T(2,128)S(1)}, s32[2,64]{1,0:T(2,128)}, u32[]{:S(2)}) copy-start(s32[2,64]{1,0:T(2,128)} %listener_ref.3) | copy-start | bytes 1540
  60.4 24.2 %copy-start.5 = (s32[64]{0:T(128)S(1)}, s32[64]{0:T(128)}, u32[]{:S(2)}) copy-start(s32[64]{0:T(128)} %param.9) | copy-start | bytes 772
  60.4 24.2 %copy-start.6 = (s32[64]{0:T(128)S(1)}, s32[64]{0:T(128)}, u32[]{:S(2)}) copy-start(s32[64]{0:T(128)} %param.10) | copy-start | bytes 772
  99.5 6.8 %collective-permute-start.5 = (f32[512,128]{1,0:T(8,128)S(1)}, f32[512,128]{1,0:T(8,128)S(1)}, u32[]{:S(2)}, u32[]{:S(2)}) collective-permute-start(f32[512,128]{1,0:T(8,128)S(1)} %shard_map.98), channel_id=1, source_target_pairs={{0,1},{1,0},{2,3},{3,2},{4,5},{5,4},{6,7},{7,6},{8,9},{9,8},{10,11... | collective-permute-start | bytes 786440 | tf_op jit(solution)/shard_map/ppermute | solution.py:275
  107.7 35.0 %copy-start.1 = (f32[64,128]{1,0:T(8,128)S(1)}, f32[64,128]{1,0:T(8,128)}, u32[]{:S(2)}) copy-start(f32[64,128]{1,0:T(8,128)} %powers_ref.3) | copy-start | bytes 98308
  107.7 6.1 %collective-permute-start.6 = (f32[512,128]{1,0:T(8,128)S(1)}, f32[512,128]{1,0:T(8,128)S(1)}, u32[]{:S(2)}, u32[]{:S(2)}) collective-permute-start(f32[512,128]{1,0:T(8,128)S(1)} %shard_map.101), channel_id=1, source_target_pairs={{0,1},{1,0},{2,3},{3,2},{4,5},{5,4},{6,7},{7,6},{8,9},{9,8},{10,11... | collective-permute-start | bytes 786440 | tf_op jit(solution)/shard_map/ppermute | solution.py:279
  109.7 9.3 %collective-permute-start.7 = (f32[512,128]{1,0:T(8,128)S(1)}, f32[512,128]{1,0:T(8,128)S(1)}, u32[]{:S(2)}, u32[]{:S(2)}) collective-permute-start(f32[512,128]{1,0:T(8,128)S(1)} %shard_map.99), channel_id=1, source_target_pairs={{0,64},{64,0},{1,65},{65,1},{2,66},{66,2},{3,67},{67,3},{4,68},{68... | collective-permute-start | bytes 786440 | tf_op jit(solution)/shard_map/ppermute | solution.py:278
  119.8 22.9 %all-to-all-start.3 = ((f32[8,64,128]{2,1,0:T(8,128)}), f32[8,64,128]{2,1,0:T(8,128)S(1)}, u32[]{:S(2)}, u32[]{:S(2)}) async-start(f32[8,64,128]{2,1,0:T(8,128)} %bitcast.10), calls=%async_computation.3 | async-start | bytes 524288 | tf_op jit(solution)/shard_map/all_to_all | solution.py:282
  127.0 6.7 %collective-permute-start.8 = (f32[64,128]{1,0:T(8,128)S(1)}, f32[64,128]{1,0:T(8,128)S(1)}, u32[]{:S(2)}, u32[]{:S(2)}) collective-permute-start(f32[64,128]{1,0:T(8,128)S(1)} %get-tuple-element.36), channel_id=1, source_target_pairs={{0,0},{1,16},{2,32},{3,48},{4,64},{5,80},{6,96},{7,112},{8,128},{9... | collective-permute-start | bytes 98312 | tf_op jit(solution)/shard_map/ppermute | solution.py:281

commit v3 on v2

--- a/solution.py
+++ b/solution.py
@@ -58,9 +58,8 @@
     return norm - low, low - odd, odd
 
 
-def pack_kernel(sender_ref, listener_ref, powers_ref, sent_ref, heard_ref):
-    sx, sy = sender_ref[0:1, :], sender_ref[1:2, :]
-    lx, ly = listener_ref[0:1, :], listener_ref[1:2, :]
+def pack_kernel(info_ref, powers_ref, sent_ref, heard_ref):
+    sx, sy, lx, ly = (info_ref[i : i + 1, :] for i in range(4))
     one = jnp.ones_like(sx)
     s1, s2, s3 = split_norm(sx * sx + sy * sy)
     l1, l2, l3 = split_norm(lx * lx + ly * ly + 1)
@@ -68,7 +67,8 @@
     heard = jnp.concatenate([lx, ly, l1, l2, l3, one, one, one], axis=0).astype(F32)
     pad = jnp.zeros_like(sent)
     sent = jnp.concatenate([sent, pad], axis=1)
-    heard_ref[...] = jnp.concatenate([heard, pad], axis=1)
+    user = jnp.concatenate([info_ref[4:6, :].astype(F32), jnp.zeros((6, BLOCK), F32)], axis=0)
+    heard_ref[...] = jnp.concatenate([heard, user], axis=1)
     powers = powers_ref[...]
     for k in range(NZ):
         sent_ref[k, 0:BLOCK, :] = powers
@@ -95,7 +95,7 @@
     if first:
         total_ref, high_ref, low_ref = rest
     else:
-        near_ref, before_ref, total_ref, high_ref, low_ref = rest
+        before_ref, total_ref, high_ref, low_ref = rest
     x, y, z0, z2, z1, zhi, core = (place_ref[i] for i in range(7))
     source_core = core if first else 1 - core
     senders = spread(sent_ref, BLOCK, lambda k: k)
@@ -104,13 +104,12 @@
     power_high, power_low = split(powers)
     power_both = jnp.concatenate([power_high, power_low], axis=1)
     tile_rows, tile_cols = 256, 128
-    per_tile = tile_rows // BLOCK
-    receiver_base = (z2 * 4 + z1 * 2 + z0) * 4096 + zhi * 128 + core * 64
+    receiver_base = zhi * 4096 + core * 2048 + (z2 * 4 + z1 * 2 + z0) * 256
     sender_base = y * 8192 + source_core * 2048 + x * 64
     for r in range(0, ROWS, tile_rows):
         row = lax.broadcasted_iota(jnp.int32, (tile_rows, tile_cols), 0) + r
         block = row >> 6
-        row_id = receiver_base + (block >> 2) * 1024 + (block & 3) * 256 + (row & 63)
+        row_id = receiver_base + (block & 3) * 8192 + (block >> 2) * 64 + (row & 63)
         for c in range(0, HALF, tile_cols):
             col = lax.broadcasted_iota(jnp.int32, (1, tile_cols), 1) + c
             zed = col >> 6
@@ -133,25 +132,20 @@
             low_ref[r : r + tile_rows, :], power_both, preferred_element_type=F32
         )
         part = product[:, :BANDS] + product[:, BANDS:]
-        if first:
-            total_ref[r : r + tile_rows, :] = part
-        else:
-            k = r // BLOCK
+        if not first:
             part = part + before_ref[r : r + tile_rows, :]
-            total_ref[k : k + per_tile, 0:BLOCK, :] = part.reshape(per_tile, BLOCK, BANDS)
-    if not first:
-        for k in range(NXY):
-            there_x, there_y = k >> 2, k & 3
-            at = (there_y & 1) * 8 + z0 * 4 + (there_x & 1) * 2 + (there_y >> 1)
-            total_ref[k, BLOCK:, :] = jnp.where(
-                core == there_x >> 1, near_ref[at], sent_ref[at]
-            )
-
-
-def react_kernel(place_ref, pressure_ref, high_ref, low_ref, pushed_ref, *, other):
+        total_ref[r : r + tile_rows, :] = part
+
+
+def turn_kernel(pressure_ref, both_ref):
     pressure = pressure_ref[...].reshape(ROWS, BANDS).T
     pressure_high, pressure_low = split(pressure)
-    both = jnp.concatenate([pressure_high, pressure_low], axis=0)
+    both_ref[0:BANDS, :] = pressure_high
+    both_ref[BANDS:, :] = pressure_low
+
+
+def react_kernel(place_ref, both_ref, high_ref, low_ref, pushed_ref, *, other):
+    both = both_ref[...]
     parity = 1 - place_ref[2] if other else place_ref[2]
     step = 256
     for c in range(0, HALF // 2, step):
@@ -161,6 +155,17 @@
         pushed_ref[c : c + step, :] = (product[:BANDS, :] + product[BANDS:, :]).T
 
 
+def join_kernel(a_ref, b_ref, out_ref):
+    rows = a_ref.shape[0]
+    out_ref[0:rows, :] = a_ref[...]
+    out_ref[rows:, :] = b_ref[...]
+
+
+def join(a, b):
+    rows, lanes = a.shape
+    return call(join_kernel, shape(2 * rows, lanes), 2, 0, 16 * a.size)(a, b)
+
+
 def add_kernel(*refs):
     total = refs[0][...]
     for ref in refs[1:-1]:
@@ -181,19 +186,15 @@
 
 
 def derive_kernel(
-    place_ref, parts_ref, listener_ref, weight_ref, fair_ref, quality_ref, own_ref, pressure_ref
+    parts_ref, powers_ref, sender_ref, heard_ref, quality_ref, own_ref, pressure_ref
 ):
     interference = add_blocks(parts_ref, NXY)
-    z2, z1, zhi, core = (place_ref[i] for i in range(3, 7))
-    source = (zhi * 2 + core) * 4 + z2 * 2 + z1
-    powers = parts_ref[source, BLOCK : 2 * BLOCK, :]
-    place = -0.5 * parts_ref[source, 2 * BLOCK :, :]
-    sx, sy = place[0:1, 0:BLOCK], place[1:2, 0:BLOCK]
-    dx = listener_ref[0:1, :].astype(F32) - sx
-    dy = listener_ref[1:2, :].astype(F32) - sy
+    powers = powers_ref[...]
+    dx = heard_ref[0:1, 0:BLOCK] - sender_ref[0:1, :].astype(F32)
+    dy = heard_ref[1:2, 0:BLOCK] - sender_ref[1:2, :].astype(F32)
     own_gain = 1.0 / (1.0 + dx * dx + dy * dy)
-    weight = WEIGHT_UNIT * weight_ref[...].astype(F32)
-    fair = fair_ref[...].astype(F32)
+    weight = WEIGHT_UNIT * heard_ref[0:1, BLOCK:]
+    fair = heard_ref[1:2, BLOCK:]
     rows = jnp.concatenate([own_gain, weight, fair, jnp.zeros((5, BLOCK), F32)], axis=0)
     rows = jnp.concatenate([rows, jnp.zeros_like(rows)], axis=1)
     columns = jnp.concatenate([rows, jnp.zeros((120, 128), F32)], axis=0).T
@@ -231,16 +232,18 @@
 def per_device(sender_xy, listener_xy, powers, weight, fairness, step_code):
     place = jnp.stack([lax.axis_index(name).astype(jnp.int32) for name in PLACE])
     to_sender = [(b, (b % 32) * 16 + b // 32) for b in range(512)]
+    to_receiver = [(s, b) for b, s in to_sender]
     swap = [(0, 1), (1, 0)]
 
-    sent, heard = call(pack_kernel, (shape(NZ, SENT, BANDS), shape(8, 128)), 3)(
-        sender_xy, listener_xy, powers
-    )
+    rows = [sender_xy, listener_xy, weight[None], fairness[None], jnp.zeros((2, BLOCK), jnp.int32)]
+    info = jnp.concatenate(rows, axis=0)
+    sent, heard = call(pack_kernel, (shape(NZ, SENT, BANDS), shape(8, 128)), 2)(info, powers)
+    mine = heard = lax.ppermute(heard, AXES, to_sender)
     near = lax.all_to_all(sent, Z, 0, 0)
     for axis in XY:
         for bit in (1, 2):
             other = lax.ppermute(heard, axis, [(i, i ^ bit) for i in range(4)])
-            heard = jnp.concatenate([heard, other], axis=0)
+            heard = join(heard, other)
     near, heard = lax.optimization_barrier((near, heard))
     listeners = heard.reshape(NXY, 8, 128)
     far = lax.ppermute(near, "core", swap)
@@ -252,18 +255,19 @@
     )(place, near, listeners)
     parts, far_high, far_low = call(
         lambda *refs: interfere_kernel(False, *refs),
-        (shape(NXY, BLOCK + SENT, BANDS), gains, gains),
-        5,
+        (shape(ROWS, BANDS), gains, gains),
+        4,
         smem=(0,),
         **work,
-    )(place, far, listeners, near, part)
-
-    parts = lax.all_to_all(parts, XY, 0, 0)
+    )(place, far, listeners, part)
+
+    parts = lax.all_to_all(parts.reshape(NXY, BLOCK, BANDS), XY, 0, 0)
     block = shape(BLOCK, BANDS)
     quality, own, pressure = call(
-        derive_kernel, (block, block, shape(NXY, BLOCK, BANDS)), 5, smem=(0,)
-    )(place, parts, listener_xy, weight[None], fairness[None])
+        derive_kernel, (block, block, shape(NXY, BLOCK, BANDS)), 4
+    )(parts, powers, sender_xy, mine)
     pressures = lax.all_to_all(pressure, XY, 0, 0)
+    pressures = call(turn_kernel, shape(2 * BANDS, ROWS, dtype=BF16), 1)(pressures)
 
     def react(pressures, high, low, other):
         kernel = functools.partial(react_kernel, other=other)
@@ -278,11 +282,11 @@
     from_neighbour = lax.ppermute(pushed, "z0", swap)
     across = lax.ppermute(react(pressures, far_high, far_low, False), "core", swap)
     pushed = add(react(pressures, near_high, near_low, False), across, from_neighbour)
-    own_here = lax.ppermute(own, AXES, to_sender)
+    quality = lax.ppermute(quality, AXES, to_receiver)
     parts = lax.all_to_all(pushed.reshape(NZ // 2, BLOCK, BANDS), EVEN, 0, 0)
     gradient, new_power, gap = call(
         finish_kernel, (block, block, shape(2 * NZ, 1, BANDS)), 4, smem=(0,)
-    )(step_code, parts, own_here, powers)
+    )(step_code, parts, own, powers)
     gap = jnp.sum(lax.all_to_all(gap, (*Z, "core"), 0, 0), axis=0)
     gap = lax.all_to_all(jnp.broadcast_to(gap[None], (NXY, 1, BANDS)), XY, 0, 0)
     return quality, gradient, new_power, (jnp.sum(gap) / (USERS * BANDS)).reshape(1)

time: 182 us -> 198 us (1.088)
  blocking collectives: 71.8 us -> 27.9 us
  starting transfers between devices: 58.5 us -> 99 us
  waiting for transfers between devices: 28.2 us -> 47.6 us
    all_to_all x3 -> x1, blocking collectives: 59.7 us -> 14.7 us  [per_device(): parts = lax.all_to_all(parts.reshape(NXY, BLOCK, BANDS), XY, 0, 0)]
    ppermute x4, starting transfers between devices: 15.8 us -> 41.6 us  [per_device(): other = lax.ppermute(heard, axis, [(i, i ^ bit) for i in range(4)])]
    all_to_all x0 -> x2, waiting for transfers between devices: none -> 15 us  [the longest x1 8.77 us: per_device(): gap = jnp.sum(lax.all_to_all(gap, (*Z, 'core'), 0, 0), axis=0)]
    all_to_all x0 -> x2, starting transfers between devices: none -> 13.1 us  [the longest x1 9.65 us: per_device(): gap = jnp.sum(lax.all_to_all(gap, (*Z, 'core'), 0, 0), axis=0)]
    all_to_all x1, waiting for transfers between devices: 9.02 us -> 15.8 us  [per_device(): parts = lax.all_to_all(pushed.reshape(NZ // 2, BLOCK, BANDS), EVEN, 0, 0)]
    all_to_all x1, waiting for transfers between devices: 4.97 us -> 0.01 us  [per_device(): near = lax.all_to_all(sent, Z, 0, 0)]
    ppermute x1 -> x2, starting transfers between devices: 2.77 us -> 6.89 us  [the longest x1 3.96 us: per_device(): mine = heard = lax.ppermute(heard, AXES, to_sender)]
    ppermute x4, waiting for transfers between devices: 5.68 us -> 9.07 us  [per_device(): other = lax.ppermute(heard, axis, [(i, i ^ bit) for i in range(4)])]
  transfers between devices with their start and end apart: 11 -> 14, of which waited for: 8 -> 9; matrix products, arithmetic and copies ran while one was open for 0% -> 0% of each run, Pallas kernels for 4% -> 3%
where the time goes in v3:
time: 198 us; the launch traced here: 197 us
  starting transfers between devices  99 us (50%)
  waiting for transfers between devices  47.6 us (24%)
  blocking collectives  27.9 us (14%)
  Pallas kernels  15.7 us (8%)
  between operations  3.31 us (2%)
  local copies, waits for them, and re-layouts  2.81 us (1%)
    ppermute x4, starting transfers between devices, per_device(): other = lax.ppermute(heard, axis, [(i, i ^ bit) for i in range(4)])  41.6 us
    all_to_all x1, waiting for transfers between devices, per_device(): parts = lax.all_to_all(pushed.reshape(NZ // 2, BLOCK, BANDS), EVEN, 0, 0)  15.8 us
    all_to_all x1, starting transfers between devices, per_device(): near = lax.all_to_all(sent, Z, 0, 0)  15.7 us
    all_to_all x1, blocking collectives, per_device(): parts = lax.all_to_all(parts.reshape(NXY, BLOCK, BANDS), XY, 0, 0)  14.7 us
    all_to_all x1, blocking collectives, per_device(): pressures = lax.all_to_all(pressure, XY, 0, 0)  13.2 us
    all_to_all x1, starting transfers between devices, per_device(): gap = jnp.sum(lax.all_to_all(gap, (*Z, 'core'), 0, 0), axis=0)  9.65 us
    ppermute x4, waiting for transfers between devices, per_device(): other = lax.ppermute(heard, axis, [(i, i ^ bit) for i in range(4)])  9.07 us
    all_to_all x1, waiting for transfers between devices, per_device(): gap = jnp.sum(lax.all_to_all(gap, (*Z, 'core'), 0, 0), axis=0)  8.77 us
  transfers between devices with their start and end apart: 14, of which 9 were waited for; matrix products, arithmetic and copies ran while one was open for 0% of the time, Pallas kernels for 3%

profile of v3, /device:TPU:1, one launch (start us, length us, event | category | flops | bytes accessed | tf_op | source)
XLA Modules:
  0.0 196.9 jit_solution(7716897009492968350)
XLA Ops:
  0.6 0.7 concatenate.3.info_ref
  1.4 0.8 copy-done
  2.1 0.9 shard_map.93
  3.0 15.7 %all-to-all-start = ((f32[16,72,128]{2,1,0:T(8,128)}), f32[16,72,128]{2,1,0:T(8,128)S(1)}, u32[]{:S(2)}, u32[]{:S(2)}) async-start(f32[16,72,128]{2,1,0:T(8,128)} %get-tuple-element.22), calls=%async_computation | async-start | bytes 1179648 | tf_op jit(solution)/shard_map/all_to_all | solution.py:242
  18.7 4.0 %collective-permute-start = (f32[8,128]{1,0:T(8,128)S(1)}, f32[8,128]{1,0:T(8,128)S(1)}, u32[]{:S(2)}, u32[]{:S(2)}) collective-permute-start(f32[8,128]{1,0:T(8,128)S(1)} %get-tuple-element.23), channel_id=1, source_target_pairs={{0,0},{1,16},{2,32},{3,48},{4,64},{5,80},{6,96},{7,112},{8,128},{9... | collective-permute-start | bytes 12296 | tf_op jit(solution)/shard_map/ppermute | solution.py:241
  22.7 2.8 %collective-permute-done.a_ref.heard_ref = f32[8,128]{1,0:T(8,128)S(1)} collective-permute-done((f32[8,128]{1,0:T(8,128)S(1)}, f32[8,128]{1,0:T(8,128)S(1)}, u32[]{:S(2)}, u32[]{:S(2)}) %collective-permute-start) | collective-permute-done | bytes 4128 | tf_op jit(solution)/shard_map/ppermute | solution.py:241
  25.5 11.5 %collective-permute-start.1 = (f32[8,128]{1,0:T(8,128)S(1)}, f32[8,128]{1,0:T(8,128)S(1)}, u32[]{:S(2)}, u32[]{:S(2)}) collective-permute-start(f32[8,128]{1,0:T(8,128)S(1)} %collective-permute-done.a_ref.heard_ref), channel_id=1, source_target_pairs={{0,16},{16,0},{32,48},{48,32},{1,17},{17,1},{33,49},{49,33},{2,18}... | collective-permute-start | bytes 12296 | tf_op jit(solution)/shard_map/ppermute | solution.py:245
  37.1 1.3 collective-permute-done.1.b_ref
  38.4 26.2 %collective-permute-start.2 = (f32[16,128]{1,0:T(8,128)S(1)}, f32[16,128]{1,0:T(8,128)S(1)}, u32[]{:S(2)}, u32[]{:S(2)}) collective-permute-start(f32[16,128]{1,0:T(8,128)S(1)} %shard_map.94.a_ref), channel_id=1, source_target_pairs={{0,32},{16,48},{32,0},{48,16},{1,33},{17,49},{33,1},{49,17},{2,34}... | collective-permute-start | bytes 24584 | tf_op jit(solution)/shard_map/ppermute | solution.py:245
  64.6 1.0 collective-permute-done.2.b_ref
  65.6 1.9 collective-permute-start.3
  67.5 2.6 %collective-permute-done.3.b_ref = f32[32,128]{1,0:T(8,128)S(1)} collective-permute-done((f32[32,128]{1,0:T(8,128)S(1)}, f32[32,128]{1,0:T(8,128)S(1)}, u32[]{:S(2)}, u32[]{:S(2)}) %collective-permute-start.3) | collective-permute-done | bytes 16416 | tf_op jit(solution)/shard_map/ppermute | solution.py:245
  70.1 1.9 collective-permute-start.4
  72.0 4.2 %collective-permute-done.4.b_ref = f32[64,128]{1,0:T(8,128)S(1)} collective-permute-done((f32[64,128]{1,0:T(8,128)S(1)}, f32[64,128]{1,0:T(8,128)S(1)}, u32[]{:S(2)}, u32[]{:S(2)}) %collective-permute-start.4) | collective-permute-done | bytes 32800 | tf_op jit(solution)/shard_map/ppermute | solution.py:245
  76.2 0.0 all-to-all-done.refs_1_
  76.2 6.6 %collective-permute-start.5 = (f32[16,72,128]{2,1,0:T(8,128)S(1)}, f32[16,72,128]{2,1,0:T(8,128)S(1)}, u32[]{:S(2)}, u32[]{:S(2)}) collective-permute-start(f32[16,72,128]{2,1,0:T(8,128)S(1)} %all-to-all-done.refs_1_), channel_id=1, source_target_pairs={{0,1},{1,0},{2,3},{3,2},{4,5},{5,4},{6,7},{7,6},{8,9},{9,8},{10,11... | collective-permute-start | bytes 1769480 | tf_op jit(solution)/shard_map/ppermute | solution.py:249
  82.9 0.1 stack.31.refs_0_.place_ref
  83.0 3.7 %shard_map.98 = (f32[1024,128]{1,0:T(8,128)S(1)}, bf16[1024,1024]{1,0:T(8,128)(2,1)S(1)}, bf16[1024,1024]{1,0:T(8,128)(2,1)S(1)}) custom-call(s32[7]{0:T(128)S(1)} %stack.31.refs_0_.place_ref, f32[16,72,128]{2,1,0:T(8,128)S(1)} %all-to-all-done.refs_1_, f32[16,8,128]{2,1,0:T(8,128)S(1)} %bitcast.15), custom_call_target="tpu_custom_call" | custom-call | flops 1073741824 | bytes 8388608 | tf_op jit(solution)/shard_map/pallas_call | solution.py:253
  86.6 0.0 collective-permute-done.5.refs_1_
  86.7 0.0 copy-start.1
  86.7 0.0 copy-start.2
  86.7 3.7 %shard_map.99 = (f32[1024,128]{1,0:T(8,128)S(1)}, bf16[1024,1024]{1,0:T(8,128)(2,1)S(1)}, bf16[1024,1024]{1,0:T(8,128)(2,1)S(1)}) custom-call(s32[7]{0:T(128)S(1)} %stack.31.refs_0_.place_ref, f32[16,72,128]{2,1,0:T(8,128)S(1)} %collective-permute-done.5.refs_1_, f32[16,8,128]{2,1,0:T(8,128)S(1)} %bitcast.16, f32[1024,128]{1,0:T(8,128)S(1)} %get-tuple-element.26.refs_3_), custom_call_target="tpu_custom_call" | custom-call | flops 1073741824 | bytes 8388608 | tf_op jit(solution)/shard_map/pallas_call | solution.py:256
  90.4 14.7 %all_to_all.30.parts_ref = f32[16,64,128]{2,1,0:T(8,128)S(1)} all-to-all(f32[16,64,128]{2,1,0:T(8,128)S(1)} %bitcast.14), channel_id=1, replica_groups=mesh['z2'=2,'z1'=2,'z0'=2,'x'=4,'y'=4,'zhi'=2,'core'=2] {'x','y'}, dimensions={0} | all-to-all | bytes 1048576 | tf_op jit(solution)/shard_map/all_to_all | solution.py:264
  105.1 0.3 shard_map.100
  105.4 13.2 %all_to_all.31.pressure_ref = f32[16,64,128]{2,1,0:T(8,128)S(1)} all-to-all(f32[16,64,128]{2,1,0:T(8,128)S(1)} %get-tuple-element.29), channel_id=1, replica_groups=mesh['z2'=2,'z1'=2,'z0'=2,'x'=4,'y'=4,'zhi'=2,'core'=2] {'x','y'}, dimensions={0} | all-to-all | bytes 1048576 | tf_op jit(solution)/shard_map/all_to_all | solution.py:269
  118.6 0.2 shard_map.101.both_ref
  118.8 1.4 shard_map.103
  120.2 5.4 %collective-permute-start.7 = (f32[512,128]{1,0:T(8,128)S(1)}, f32[512,128]{1,0:T(8,128)S(1)}, u32[]{:S(2)}, u32[]{:S(2)}) collective-permute-start(f32[512,128]{1,0:T(8,128)S(1)} %shard_map.103), channel_id=1, source_target_pairs={{0,1},{1,0},{2,3},{3,2},{4,5},{5,4},{6,7},{7,6},{8,9},{9,8},{10,11... | collective-permute-start | bytes 786440 | tf_op jit(solution)/shard_map/ppermute | solution.py:279
  125.6 1.4 shard_map.102.refs_0_
  127.0 1.4 shard_map.106
  128.4 2.0 %collective-permute-start.8 = (f32[512,128]{1,0:T(8,128)S(1)}, f32[512,128]{1,0:T(8,128)S(1)}, u32[]{:S(2)}, u32[]{:S(2)}) collective-permute-start(f32[512,128]{1,0:T(8,128)S(1)} %shard_map.106), channel_id=1, source_target_pairs={{0,1},{1,0},{2,3},{3,2},{4,5},{5,4},{6,7},{7,6},{8,9},{9,8},{10,11... | collective-permute-start | bytes 786440 | tf_op jit(solution)/shard_map/ppermute | solution.py:283
  130.4 3.2 %collective-permute-start.9 = (f32[512,128]{1,0:T(8,128)S(1)}, f32[512,128]{1,0:T(8,128)S(1)}, u32[]{:S(2)}, u32[]{:S(2)}) collective-permute-start(f32[512,128]{1,0:T(8,128)S(1)} %shard_map.104), channel_id=1, source_target_pairs={{0,64},{64,0},{1,65},{65,1},{2,66},{66,2},{3,67},{67,3},{4,68},{68... | collective-permute-start | bytes 786440 | tf_op jit(solution)/shard_map/ppermute | solution.py:282
  133.6 1.4 shard_map.105.refs_0_
  135.0 0.0 collective-permute-done.8.refs_1_
  135.0 4.8 %collective-permute-done.9.refs_2_ = f32[512,128]{1,0:T(8,128)S(1)} collective-permute-done((f32[512,128]{1,0:T(8,128)S(1)}, f32[512,128]{1,0:T(8,128)S(1)}, u32[]{:S(2)}, u32[]{:S(2)}) %collective-permute-start.9) | collective-permute-done | bytes 262176 | tf_op jit(solution)/shard_map/ppermute | solution.py:282
  139.8 0.7 shard_map.107
  140.5 4.4 %all-to-all-start.3 = ((f32[8,64,128]{2,1,0:T(8,128)}), f32[8,64,128]{2,1,0:T(8,128)S(1)}, u32[]{:S(2)}, u32[]{:S(2)}) async-start(f32[8,64,128]{2,1,0:T(8,128)} %bitcast.11), calls=%async_computation.3 | async-start | bytes 524288 | tf_op jit(solution)/shard_map/all_to_all | solution.py:286
  145.6 15.8 %all-to-all-done.3.parts_ref = f32[8,64,128]{2,1,0:T(8,128)S(1)} async-done(((f32[8,64,128]{2,1,0:T(8,128)}), f32[8,64,128]{2,1,0:T(8,128)S(1)}, u32[]{:S(2)}, u32[]{:S(2)}) %all-to-all-start.3) | async-done | bytes 262176 | tf_op jit(solution)/shard_map/all_to_all | solution.py:286
  161.4 0.7 shard_map.108
  162.1 9.7 %all-to-all-start.4 = ((f32[32,1,128]{2,1,0:T(1,128)}), f32[32,1,128]{2,1,0:T(1,128)S(1)}, u32[]{:S(2)}, u32[]{:S(2)}) async-start(f32[32,1,128]{2,1,0:T(1,128)} %get-tuple-element.39), calls=%async_computation.4 | async-start | bytes 32768 | tf_op jit(solution)/shard_map/all_to_all | solution.py:290
  171.7 2.9 %collective-permute-start.6 = (f32[64,128]{1,0:T(8,128)S(1)}, f32[64,128]{1,0:T(8,128)S(1)}, u32[]{:S(2)}, u32[]{:S(2)}) collective-permute-start(f32[64,128]{1,0:T(8,128)S(1)} %get-tuple-element.28), channel_id=1, source_target_pairs={{0,0},{16,1},{32,2},{48,3},{64,4},{80,5},{96,6},{112,7},{128,8},{1... | collective-permute-start | bytes 98312 | tf_op jit(solution)/shard_map/ppermute | solution.py:285
  174.7 8.8 %all-to-all-done.4 = f32[32,1,128]{2,1,0:T(1,128)S(1)} async-done(((f32[32,1,128]{2,1,0:T(1,128)}), f32[32,1,128]{2,1,0:T(1,128)S(1)}, u32[]{:S(2)}, u32[]{:S(2)}) %all-to-all-start.4) | async-done | bytes 16416 | tf_op jit(solution)/shard_map/all_to_all | solution.py:290
  183.5 0.1 reduce_sum.18
  183.5 0.6 broadcast_in_dim.18
  184.1 3.5 %all-to-all-start.5 = ((f32[16,1,128]{2,1,0:T(1,128)}), f32[16,1,128]{2,1,0:T(1,128)S(1)}, u32[]{:S(2)}, u32[]{:S(2)}) async-start(f32[16,1,128]{2,1,0:T(1,128)} %broadcast_in_dim.18), calls=%async_computation.5 | async-start | bytes 16384 | tf_op jit(solution)/shard_map/all_to_all | solution.py:291
  187.6 6.3 %all-to-all-done.5 = f32[16,1,128]{2,1,0:T(1,128)S(1)} async-done(((f32[16,1,128]{2,1,0:T(1,128)}), f32[16,1,128]{2,1,0:T(1,128)S(1)}, u32[]{:S(2)}, u32[]{:S(2)}) %all-to-all-start.5) | async-done | bytes 8224 | tf_op jit(solution)/shard_map/all_to_all | solution.py:291
  193.9 0.6 reduce_sum.19
  195.1 0.6 copy.13
  (11 shorter events, 0.1 us)
Async XLA Ops:
  1.4 0.8 copy-start
  3.0 73.2 %all-to-all-start = ((f32[16,72,128]{2,1,0:T(8,128)}), f32[16,72,128]{2,1,0:T(8,128)S(1)}, u32[]{:S(2)}, u32[]{:S(2)}) async-start(f32[16,72,128]{2,1,0:T(8,128)} %get-tuple-element.22), calls=%async_computation | async-start | bytes 1179648 | tf_op jit(solution)/shard_map/all_to_all | solution.py:242
  18.7 6.8 %collective-permute-start = (f32[8,128]{1,0:T(8,128)S(1)}, f32[8,128]{1,0:T(8,128)S(1)}, u32[]{:S(2)}, u32[]{:S(2)}) collective-permute-start(f32[8,128]{1,0:T(8,128)S(1)} %get-tuple-element.23), channel_id=1, source_target_pairs={{0,0},{1,16},{2,32},{3,48},{4,64},{5,80},{6,96},{7,112},{8,128},{9... | collective-permute-start | bytes 12296 | tf_op jit(solution)/shard_map/ppermute | solution.py:241
  25.5 12.8 %collective-permute-start.1 = (f32[8,128]{1,0:T(8,128)S(1)}, f32[8,128]{1,0:T(8,128)S(1)}, u32[]{:S(2)}, u32[]{:S(2)}) collective-permute-start(f32[8,128]{1,0:T(8,128)S(1)} %collective-permute-done.a_ref.heard_ref), channel_id=1, source_target_pairs={{0,16},{16,0},{32,48},{48,32},{1,17},{17,1},{33,49},{49,33},{2,18}... | collective-permute-start | bytes 12296 | tf_op jit(solution)/shard_map/ppermute | solution.py:245
  38.4 27.2 %collective-permute-start.2 = (f32[16,128]{1,0:T(8,128)S(1)}, f32[16,128]{1,0:T(8,128)S(1)}, u32[]{:S(2)}, u32[]{:S(2)}) collective-permute-start(f32[16,128]{1,0:T(8,128)S(1)} %shard_map.94.a_ref), channel_id=1, source_target_pairs={{0,32},{16,48},{32,0},{48,16},{1,33},{17,49},{33,1},{49,17},{2,34}... | collective-permute-start | bytes 24584 | tf_op jit(solution)/shard_map/ppermute | solution.py:245
  65.6 4.5 %collective-permute-start.3 = (f32[32,128]{1,0:T(8,128)S(1)}, f32[32,128]{1,0:T(8,128)S(1)}, u32[]{:S(2)}, u32[]{:S(2)}) collective-permute-start(f32[32,128]{1,0:T(8,128)S(1)} %shard_map.95.a_ref), channel_id=1, source_target_pairs={{0,4},{4,0},{8,12},{12,8},{1,5},{5,1},{9,13},{13,9},{2,6},{6,2},{1... | collective-permute-start | bytes 49160 | tf_op jit(solution)/shard_map/ppermute | solution.py:245
  70.1 6.2 %collective-permute-start.4 = (f32[64,128]{1,0:T(8,128)S(1)}, f32[64,128]{1,0:T(8,128)S(1)}, u32[]{:S(2)}, u32[]{:S(2)}) collective-permute-start(f32[64,128]{1,0:T(8,128)S(1)} %shard_map.96.a_ref), channel_id=1, source_target_pairs={{0,8},{4,12},{8,0},{12,4},{1,9},{5,13},{9,1},{13,5},{2,10},{6,14},... | collective-permute-start | bytes 98312 | tf_op jit(solution)/shard_map/ppermute | solution.py:245
  76.2 10.4 %collective-permute-start.5 = (f32[16,72,128]{2,1,0:T(8,128)S(1)}, f32[16,72,128]{2,1,0:T(8,128)S(1)}, u32[]{:S(2)}, u32[]{:S(2)}) collective-permute-start(f32[16,72,128]{2,1,0:T(8,128)S(1)} %all-to-all-done.refs_1_), channel_id=1, source_target_pairs={{0,1},{1,0},{2,3},{3,2},{4,5},{5,4},{6,7},{7,6},{8,9},{9,8},{10,11... | collective-permute-start | bytes 1769480 | tf_op jit(solution)/shard_map/ppermute | solution.py:249
  86.7 18.5 %copy-start.1 = (f32[64,128]{1,0:T(8,128)S(1)}, f32[64,128]{1,0:T(8,128)}, u32[]{:S(2)}) copy-start(f32[64,128]{1,0:T(8,128)} %powers_ref.5) | copy-start | bytes 98308
  86.7 18.5 %copy-start.2 = (s32[2,64]{1,0:T(2,128)S(1)}, s32[2,64]{1,0:T(2,128)}, u32[]{:S(2)}) copy-start(s32[2,64]{1,0:T(2,128)} %sender_ref.1) | copy-start | bytes 1540
  120.2 6.7 %collective-permute-start.7 = (f32[512,128]{1,0:T(8,128)S(1)}, f32[512,128]{1,0:T(8,128)S(1)}, u32[]{:S(2)}, u32[]{:S(2)}) collective-permute-start(f32[512,128]{1,0:T(8,128)S(1)} %shard_map.103), channel_id=1, source_target_pairs={{0,1},{1,0},{2,3},{3,2},{4,5},{5,4},{6,7},{7,6},{8,9},{9,8},{10,11... | collective-permute-start | bytes 786440 | tf_op jit(solution)/shard_map/ppermute | solution.py:279
  128.4 6.6 %collective-permute-start.8 = (f32[512,128]{1,0:T(8,128)S(1)}, f32[512,128]{1,0:T(8,128)S(1)}, u32[]{:S(2)}, u32[]{:S(2)}) collective-permute-start(f32[512,128]{1,0:T(8,128)S(1)} %shard_map.106), channel_id=1, source_target_pairs={{0,1},{1,0},{2,3},{3,2},{4,5},{5,4},{6,7},{7,6},{8,9},{9,8},{10,11... | collective-permute-start | bytes 786440 | tf_op jit(solution)/shard_map/ppermute | solution.py:283
  130.4 9.4 %collective-permute-start.9 = (f32[512,128]{1,0:T(8,128)S(1)}, f32[512,128]{1,0:T(8,128)S(1)}, u32[]{:S(2)}, u32[]{:S(2)}) collective-permute-start(f32[512,128]{1,0:T(8,128)S(1)} %shard_map.104), channel_id=1, source_target_pairs={{0,64},{64,0},{1,65},{65,1},{2,66},{66,2},{3,67},{67,3},{4,68},{68... | collective-permute-start | bytes 786440 | tf_op jit(solution)/shard_map/ppermute | solution.py:282
  140.5 20.9 %all-to-all-start.3 = ((f32[8,64,128]{2,1,0:T(8,128)}), f32[8,64,128]{2,1,0:T(8,128)S(1)}, u32[]{:S(2)}, u32[]{:S(2)}) async-start(f32[8,64,128]{2,1,0:T(8,128)} %bitcast.11), calls=%async_computation.3 | async-start | bytes 524288 | tf_op jit(solution)/shard_map/all_to_all | solution.py:286
  162.1 21.4 %all-to-all-start.4 = ((f32[32,1,128]{2,1,0:T(1,128)}), f32[32,1,128]{2,1,0:T(1,128)S(1)}, u32[]{:S(2)}, u32[]{:S(2)}) async-start(f32[32,1,128]{2,1,0:T(1,128)} %get-tuple-element.39), calls=%async_computation.4 | async-start | bytes 32768 | tf_op jit(solution)/shard_map/all_to_all | solution.py:290
  171.7 15.8 %collective-permute-start.6 = (f32[64,128]{1,0:T(8,128)S(1)}, f32[64,128]{1,0:T(8,128)S(1)}, u32[]{:S(2)}, u32[]{:S(2)}) collective-permute-start(f32[64,128]{1,0:T(8,128)S(1)} %get-tuple-element.28), channel_id=1, source_target_pairs={{0,0},{16,1},{32,2},{48,3},{64,4},{80,5},{96,6},{112,7},{128,8},{1... | collective-permute-start | bytes 98312 | tf_op jit(solution)/shard_map/ppermute | solution.py:285
  184.1 9.8 %all-to-all-start.5 = ((f32[16,1,128]{2,1,0:T(1,128)}), f32[16,1,128]{2,1,0:T(1,128)S(1)}, u32[]{:S(2)}, u32[]{:S(2)}) async-start(f32[16,1,128]{2,1,0:T(1,128)} %broadcast_in_dim.18), calls=%async_computation.5 | async-start | bytes 16384 | tf_op jit(solution)/shard_map/all_to_all | solution.py:291

commit v4 on v3

--- a/solution.py
+++ b/solution.py
@@ -1,5 +1,3 @@
-import functools
-
 import jax
 import jax.numpy as jnp
 from jax import lax
@@ -22,6 +20,7 @@
 BLOCK, BANDS = 64, 128
 SENT = BLOCK + 8
 HALF = NZ * BLOCK
+WIDE = HALF // 2
 ROWS = NXY * BLOCK
 USERS = 32768
 VMEM_LIMIT = 20 * 1024 * 1024
@@ -58,7 +57,7 @@
     return norm - low, low - odd, odd
 
 
-def pack_kernel(info_ref, powers_ref, sent_ref, heard_ref):
+def pack_kernel(info_ref, powers_ref, sent_ref, heard_ref, mine_ref):
     sx, sy, lx, ly = (info_ref[i : i + 1, :] for i in range(4))
     one = jnp.ones_like(sx)
     s1, s2, s3 = split_norm(sx * sx + sy * sy)
@@ -67,9 +66,10 @@
     heard = jnp.concatenate([lx, ly, l1, l2, l3, one, one, one], axis=0).astype(F32)
     pad = jnp.zeros_like(sent)
     sent = jnp.concatenate([sent, pad], axis=1)
-    user = jnp.concatenate([info_ref[4:6, :].astype(F32), jnp.zeros((6, BLOCK), F32)], axis=0)
-    heard_ref[...] = jnp.concatenate([heard, user], axis=1)
+    heard_ref[...] = jnp.concatenate([heard, pad], axis=1)
     powers = powers_ref[...]
+    mine_ref[0:BLOCK, :] = powers
+    mine_ref[BLOCK:, :] = sent
     for k in range(NZ):
         sent_ref[k, 0:BLOCK, :] = powers
         sent_ref[k, BLOCK:SENT, :] = sent
@@ -95,7 +95,7 @@
     if first:
         total_ref, high_ref, low_ref = rest
     else:
-        before_ref, total_ref, high_ref, low_ref = rest
+        _, before_ref, total_ref, high_ref, low_ref = rest
     x, y, z0, z2, z1, zhi, core = (place_ref[i] for i in range(7))
     source_core = core if first else 1 - core
     senders = spread(sent_ref, BLOCK, lambda k: k)
@@ -104,12 +104,12 @@
     power_high, power_low = split(powers)
     power_both = jnp.concatenate([power_high, power_low], axis=1)
     tile_rows, tile_cols = 256, 128
-    receiver_base = zhi * 4096 + core * 2048 + (z2 * 4 + z1 * 2 + z0) * 256
+    receiver_base = (z2 * 4 + z1 * 2 + z0) * 4096 + zhi * 128 + core * 64
     sender_base = y * 8192 + source_core * 2048 + x * 64
     for r in range(0, ROWS, tile_rows):
         row = lax.broadcasted_iota(jnp.int32, (tile_rows, tile_cols), 0) + r
         block = row >> 6
-        row_id = receiver_base + (block & 3) * 8192 + (block >> 2) * 64 + (row & 63)
+        row_id = receiver_base + (block >> 2) * 1024 + (block & 3) * 256 + (row & 63)
         for c in range(0, HALF, tile_cols):
             col = lax.broadcasted_iota(jnp.int32, (1, tile_cols), 1) + c
             zed = col >> 6
@@ -125,12 +125,15 @@
             gain = guess * (2.0 - square * guess)
             gain = jnp.where(row_id == col_id, 0.0, gain)
             high, low = split(gain)
-            high_ref[r : r + tile_rows, c : c + tile_cols] = high
-            low_ref[r : r + tile_rows, c : c + tile_cols] = low
-        product = jnp.dot(high_ref[r : r + tile_rows, :], power_both, preferred_element_type=F32)
-        product = product + jnp.dot(
-            low_ref[r : r + tile_rows, :], power_both, preferred_element_type=F32
-        )
+            side, at = c // WIDE, c % WIDE
+            high_ref[side, r : r + tile_rows, at : at + tile_cols] = high
+            low_ref[side, r : r + tile_rows, at : at + tile_cols] = low
+        product = jnp.zeros((tile_rows, 2 * BANDS), F32)
+        for side in (0, 1):
+            right = power_both[side * WIDE : (side + 1) * WIDE, :]
+            for gain_ref in (high_ref, low_ref):
+                left = gain_ref[side, r : r + tile_rows, :]
+                product = product + jnp.dot(left, right, preferred_element_type=F32)
         part = product[:, :BANDS] + product[:, BANDS:]
         if not first:
             part = part + before_ref[r : r + tile_rows, :]
@@ -144,15 +147,17 @@
     both_ref[BANDS:, :] = pressure_low
 
 
-def react_kernel(place_ref, both_ref, high_ref, low_ref, pushed_ref, *, other):
+def react_kernel(place_ref, both_ref, high_ref, low_ref, pushed_ref):
     both = both_ref[...]
-    parity = 1 - place_ref[2] if other else place_ref[2]
     step = 256
-    for c in range(0, HALF // 2, step):
-        columns = pl.ds(pl.multiple_of(parity * (HALF // 2) + c, step), step)
-        product = jnp.dot(both, high_ref[:, columns], preferred_element_type=F32)
-        product = product + jnp.dot(both, low_ref[:, columns], preferred_element_type=F32)
-        pushed_ref[c : c + step, :] = (product[:BANDS, :] + product[BANDS:, :]).T
+    for k in (0, 1):
+        side = place_ref[2] ^ k
+        for c in range(0, WIDE, step):
+            product = jnp.dot(both, high_ref[side, :, c : c + step], preferred_element_type=F32)
+            product = product + jnp.dot(
+                both, low_ref[side, :, c : c + step], preferred_element_type=F32
+            )
+            pushed_ref[k, c : c + step, :] = (product[:BANDS, :] + product[BANDS:, :]).T
 
 
 def join_kernel(a_ref, b_ref, out_ref):
@@ -166,16 +171,13 @@
     return call(join_kernel, shape(2 * rows, lanes), 2, 0, 16 * a.size)(a, b)
 
 
-def add_kernel(*refs):
-    total = refs[0][...]
-    for ref in refs[1:-1]:
-        total = total + ref[...]
-    refs[-1][...] = total
-
-
-def add(*parts):
-    size = 4 * parts[0].size
-    return call(add_kernel, shape(*parts[0].shape), len(parts), parts[0].size, 3 * size)(*parts)
+def combine_kernel(a_ref, b_ref, kept_ref, passed_ref):
+    kept_ref[...] = a_ref[0] + b_ref[0]
+    passed_ref[...] = a_ref[1] + b_ref[1]
+
+
+def add_kernel(a_ref, b_ref, sum_ref):
+    sum_ref[...] = a_ref[...] + b_ref[...]
 
 
 def add_blocks(ref, count):
@@ -186,15 +188,15 @@
 
 
 def derive_kernel(
-    parts_ref, powers_ref, sender_ref, heard_ref, quality_ref, own_ref, pressure_ref
+    parts_ref, mine_ref, listener_ref, weight_ref, fair_ref, quality_ref, own_ref, pressure_ref
 ):
     interference = add_blocks(parts_ref, NXY)
-    powers = powers_ref[...]
-    dx = heard_ref[0:1, 0:BLOCK] - sender_ref[0:1, :].astype(F32)
-    dy = heard_ref[1:2, 0:BLOCK] - sender_ref[1:2, :].astype(F32)
+    powers = mine_ref[0:BLOCK, :]
+    dx = listener_ref[0:1, :].astype(F32) + 0.5 * mine_ref[BLOCK : BLOCK + 1, 0:BLOCK]
+    dy = listener_ref[1:2, :].astype(F32) + 0.5 * mine_ref[BLOCK + 1 : BLOCK + 2, 0:BLOCK]
     own_gain = 1.0 / (1.0 + dx * dx + dy * dy)
-    weight = WEIGHT_UNIT * heard_ref[0:1, BLOCK:]
-    fair = heard_ref[1:2, BLOCK:]
+    weight = WEIGHT_UNIT * weight_ref[...].astype(F32)
+    fair = fair_ref[...].astype(F32)
     rows = jnp.concatenate([own_gain, weight, fair, jnp.zeros((5, BLOCK), F32)], axis=0)
     rows = jnp.concatenate([rows, jnp.zeros_like(rows)], axis=1)
     columns = jnp.concatenate([rows, jnp.zeros((120, 128), F32)], axis=0).T
@@ -234,55 +236,48 @@
     to_sender = [(b, (b % 32) * 16 + b // 32) for b in range(512)]
     to_receiver = [(s, b) for b, s in to_sender]
     swap = [(0, 1), (1, 0)]
-
-    rows = [sender_xy, listener_xy, weight[None], fairness[None], jnp.zeros((2, BLOCK), jnp.int32)]
-    info = jnp.concatenate(rows, axis=0)
-    sent, heard = call(pack_kernel, (shape(NZ, SENT, BANDS), shape(8, 128)), 2)(info, powers)
-    mine = heard = lax.ppermute(heard, AXES, to_sender)
+    block, blocks = shape(BLOCK, BANDS), shape(NXY, BLOCK, BANDS)
+
+    rows = [sender_xy, listener_xy, jnp.zeros((4, BLOCK), jnp.int32)]
+    sent, heard, mine = call(
+        pack_kernel, (shape(NZ, SENT, BANDS), shape(8, 128), shape(SENT, BANDS)), 2
+    )(jnp.concatenate(rows, axis=0), powers)
     near = lax.all_to_all(sent, Z, 0, 0)
     for axis in XY:
         for bit in (1, 2):
             other = lax.ppermute(heard, axis, [(i, i ^ bit) for i in range(4)])
             heard = join(heard, other)
-    near, heard = lax.optimization_barrier((near, heard))
+    near, heard, mine = lax.optimization_barrier((near, heard, mine))
     listeners = heard.reshape(NXY, 8, 128)
     far = lax.ppermute(near, "core", swap)
-
-    gains = shape(ROWS, HALF, dtype=BF16)
+    mine = lax.ppermute(mine, AXES, to_receiver)
+
+    gains = shape(2, ROWS, WIDE, dtype=BF16)
     work = dict(flops=2 * ROWS * HALF * 512, bytes_accessed=1 << 23)
+    outs = (shape(ROWS, BANDS), gains, gains)
     part, near_high, near_low = call(
-        lambda *refs: interfere_kernel(True, *refs), (shape(ROWS, BANDS), gains, gains), 3, smem=(0,), **work
+        lambda *refs: interfere_kernel(True, *refs), outs, 3, smem=(0,), **work
     )(place, near, listeners)
-    parts, far_high, far_low = call(
-        lambda *refs: interfere_kernel(False, *refs),
-        (shape(ROWS, BANDS), gains, gains),
-        4,
-        smem=(0,),
-        **work,
-    )(place, far, listeners, part)
-
-    parts = lax.all_to_all(parts.reshape(NXY, BLOCK, BANDS), XY, 0, 0)
-    block = shape(BLOCK, BANDS)
-    quality, own, pressure = call(
-        derive_kernel, (block, block, shape(NXY, BLOCK, BANDS)), 4
-    )(parts, powers, sender_xy, mine)
+    part, far_high, far_low = call(
+        lambda *refs: interfere_kernel(False, *refs), outs, 5, smem=(0,), **work
+    )(place, far, listeners, mine, part)
+
+    parts = lax.all_to_all(part.reshape(NXY, BLOCK, BANDS), XY, 0, 0)
+    quality, own, pressure = call(derive_kernel, (block, block, blocks), 5)(
+        parts, mine, listener_xy, weight[None], fairness[None]
+    )
     pressures = lax.all_to_all(pressure, XY, 0, 0)
-    pressures = call(turn_kernel, shape(2 * BANDS, ROWS, dtype=BF16), 1)(pressures)
-
-    def react(pressures, high, low, other):
-        kernel = functools.partial(react_kernel, other=other)
-        quarter = dict(flops=work["flops"] // 2, bytes_accessed=1 << 21)
-        return call(kernel, shape(HALF // 2, BANDS), 4, smem=(0,), **quarter)(
-            place, pressures, high, low
-        )
-
-    across = lax.ppermute(react(pressures, far_high, far_low, True), "core", swap)
-    pushed = add(react(pressures, near_high, near_low, True), across)
-    pressures, pushed = lax.optimization_barrier((pressures, pushed))
-    from_neighbour = lax.ppermute(pushed, "z0", swap)
-    across = lax.ppermute(react(pressures, far_high, far_low, False), "core", swap)
-    pushed = add(react(pressures, near_high, near_low, False), across, from_neighbour)
-    quality = lax.ppermute(quality, AXES, to_receiver)
+    both = call(turn_kernel, shape(2 * BANDS, ROWS, dtype=BF16), 1)(pressures)
+
+    half = shape(2, WIDE, BANDS)
+    react = call(react_kernel, half, 4, smem=(0,), **work)
+    across = lax.ppermute(react(place, both, far_high, far_low), "core", swap)
+    pushed = react(place, both, near_high, near_low)
+    side = shape(WIDE, BANDS)
+    kept, passed = call(combine_kernel, (side, side), 2)(pushed, across)
+    passed = lax.ppermute(passed, "z0", swap)
+    pushed = call(add_kernel, side, 2)(kept, passed)
+    own = lax.ppermute(own, AXES, to_sender)
     parts = lax.all_to_all(pushed.reshape(NZ // 2, BLOCK, BANDS), EVEN, 0, 0)
     gradient, new_power, gap = call(
         finish_kernel, (block, block, shape(2 * NZ, 1, BANDS)), 4, smem=(0,)

time: 198 us -> 184 us (0.929)
  blocking collectives: 27.9 us -> 72 us
  starting transfers between devices: 99 us -> 59.2 us
  waiting for transfers between devices: 47.6 us -> 32.7 us
    all_to_all x1 -> x3, blocking collectives: 14.7 us -> 59.3 us  [the longest x1 25.6 us: per_device(): parts = lax.all_to_all(part.reshape(NXY, BLOCK, BANDS), XY, 0, 0)]
    ppermute x4, starting transfers between devices: 41.6 us -> 15.8 us  [per_device(): other = lax.ppermute(heard, axis, [(i, i ^ bit) for i in range(4)])]
    all_to_all x2 -> x0, waiting for transfers between devices: 15 us -> none  [the longest x1 8.77 us: per_device(): gap = jnp.sum(lax.all_to_all(gap, (*Z, 'core'), 0, 0), axis=0)]
    all_to_all x2 -> x0, starting transfers between devices: 13.1 us -> none  [the longest x1 9.65 us: per_device(): gap = jnp.sum(lax.all_to_all(gap, (*Z, 'core'), 0, 0), axis=0)]
    all_to_all x1, waiting for transfers between devices: 15.8 us -> 10.4 us  [per_device(): parts = lax.all_to_all(pushed.reshape(NZ // 2, BLOCK, BANDS), EVEN, 0, 0)]
    all_to_all x1, waiting for transfers between devices: 0.01 us -> 4.97 us  [per_device(): near = lax.all_to_all(sent, Z, 0, 0)]
    ppermute x5 -> x4, waiting for transfers between devices: 7.63 us -> 11.7 us  [the longest x1 7.9 us: per_device(): passed = lax.ppermute(passed, 'z0', swap)]
    ppermute x5 -> x4, starting transfers between devices: 17.5 us -> 14 us  [the longest x1 5.21 us: per_device(): across = lax.ppermute(react(place, both, far_high, far_low), 'core', swap)]
  transfers between devices with their start and end apart: 14 -> 11, of which waited for: 9 -> 8; matrix products, arithmetic and copies ran while one was open for 0% -> 0% of each run, Pallas kernels for 3% -> 3%
where the time goes in v4:
time: 184 us
  blocking collectives  72 us (39%)
  starting transfers between devices  59.2 us (32%)
  waiting for transfers between devices  32.7 us (18%)
  Pallas kernels  14.1 us (8%)
  between operations  3.27 us (2%)
    all_to_all x1, blocking collectives, per_device(): parts = lax.all_to_all(part.reshape(NXY, BLOCK, BANDS), XY, 0, 0)  25.6 us
    all_to_all x1, blocking collectives, per_device(): gap = jnp.sum(lax.all_to_all(gap, (*Z, 'core'), 0, 0), axis=0)  22.8 us
    ppermute x4, starting transfers between devices, per_device(): other = lax.ppermute(heard, axis, [(i, i ^ bit) for i in range(4)])  15.8 us
    all_to_all x1, starting transfers between devices, per_device(): near = lax.all_to_all(sent, Z, 0, 0)  15.7 us
    all_to_all x1, blocking collectives, per_device(): pressures = lax.all_to_all(pressure, XY, 0, 0)  12.7 us
    all_to_all x1, blocking collectives, per_device(): gap = lax.all_to_all(jnp.broadcast_to(gap[None], (NXY, 1, BANDS)), XY, 0, 0)  10.9 us
    all_to_all x1, waiting for transfers between devices, per_device(): parts = lax.all_to_all(pushed.reshape(NZ // 2, BLOCK, BANDS), EVEN, 0, 0)  10.4 us
    ppermute x1, waiting for transfers between devices, per_device(): passed = lax.ppermute(passed, 'z0', swap)  7.9 us
  transfers between devices with their start and end apart: 11, of which 8 were waited for; matrix products, arithmetic and copies ran while one was open for 0% of the time, Pallas kernels for 3%

profile of v4, /device:TPU:1, one launch (start us, length us, event | category | flops | bytes accessed | tf_op | source)
XLA Modules:
  0.0 183.6 jit_solution(17300520636108123657)
XLA Ops:
  0.6 0.1 pad.2.clone
  0.7 0.8 add_add_fusion.info_ref
  1.5 0.8 copy-done
  2.2 0.9 shard_map.93
  3.1 15.7 %all-to-all-start = ((f32[16,72,128]{2,1,0:T(8,128)}), f32[16,72,128]{2,1,0:T(8,128)S(1)}, u32[]{:S(2)}, u32[]{:S(2)}) async-start(f32[16,72,128]{2,1,0:T(8,128)} %get-tuple-element.24), calls=%async_computation | async-start | bytes 1179648 | tf_op jit(solution)/shard_map/all_to_all | solution.py:245
  18.9 3.1 %collective-permute-start = (f32[8,128]{1,0:T(8,128)S(1)}, f32[8,128]{1,0:T(8,128)S(1)}, u32[]{:S(2)}, u32[]{:S(2)}) collective-permute-start(f32[8,128]{1,0:T(8,128)S(1)} %get-tuple-element.25.a_ref), channel_id=1, source_target_pairs={{0,16},{16,0},{32,48},{48,32},{1,17},{17,1},{33,49},{49,33},{2,18}... | collective-permute-start | bytes 12296 | tf_op jit(solution)/shard_map/ppermute | solution.py:248
  22.0 1.2 collective-permute-done.b_ref
  23.2 4.6 %collective-permute-start.1 = (f32[16,128]{1,0:T(8,128)S(1)}, f32[16,128]{1,0:T(8,128)S(1)}, u32[]{:S(2)}, u32[]{:S(2)}) collective-permute-start(f32[16,128]{1,0:T(8,128)S(1)} %shard_map.94.a_ref), channel_id=1, source_target_pairs={{0,32},{16,48},{32,0},{48,16},{1,33},{17,49},{33,1},{49,17},{2,34}... | collective-permute-start | bytes 24584 | tf_op jit(solution)/shard_map/ppermute | solution.py:248
  27.9 1.2 collective-permute-done.1.b_ref
  29.1 3.2 %collective-permute-start.2 = (f32[32,128]{1,0:T(8,128)S(1)}, f32[32,128]{1,0:T(8,128)S(1)}, u32[]{:S(2)}, u32[]{:S(2)}) collective-permute-start(f32[32,128]{1,0:T(8,128)S(1)} %shard_map.95.a_ref), channel_id=1, source_target_pairs={{0,4},{4,0},{8,12},{12,8},{1,5},{5,1},{9,13},{13,9},{2,6},{6,2},{1... | collective-permute-start | bytes 49160 | tf_op jit(solution)/shard_map/ppermute | solution.py:248
  32.3 1.6 collective-permute-done.2.b_ref
  33.9 4.8 %collective-permute-start.3 = (f32[64,128]{1,0:T(8,128)S(1)}, f32[64,128]{1,0:T(8,128)S(1)}, u32[]{:S(2)}, u32[]{:S(2)}) collective-permute-start(f32[64,128]{1,0:T(8,128)S(1)} %shard_map.96.a_ref), channel_id=1, source_target_pairs={{0,8},{4,12},{8,0},{12,4},{1,9},{5,13},{9,1},{13,5},{2,10},{6,14},... | collective-permute-start | bytes 98312 | tf_op jit(solution)/shard_map/ppermute | solution.py:248
  38.7 1.7 collective-permute-done.3.b_ref
  40.4 5.0 %all-to-all-done.refs_1_ = f32[16,72,128]{2,1,0:T(8,128)S(1)} async-done(((f32[16,72,128]{2,1,0:T(8,128)}), f32[16,72,128]{2,1,0:T(8,128)S(1)}, u32[]{:S(2)}, u32[]{:S(2)}) %all-to-all-start) | async-done | bytes 589856 | tf_op jit(solution)/shard_map/all_to_all | solution.py:245
  45.4 7.0 %collective-permute-start.4 = (f32[16,72,128]{2,1,0:T(8,128)S(1)}, f32[16,72,128]{2,1,0:T(8,128)S(1)}, u32[]{:S(2)}, u32[]{:S(2)}) collective-permute-start(f32[16,72,128]{2,1,0:T(8,128)S(1)} %all-to-all-done.refs_1_), channel_id=1, source_target_pairs={{0,1},{1,0},{2,3},{3,2},{4,5},{5,4},{6,7},{7,6},{8,9},{9,8},{10,11... | collective-permute-start | bytes 1769480 | tf_op jit(solution)/shard_map/ppermute | solution.py:252
  52.4 0.1 stack.31.refs_0_.place_ref
  52.5 4.5 %collective-permute-start.5 = (f32[72,128]{1,0:T(8,128)S(1)}, f32[72,128]{1,0:T(8,128)S(1)}, u32[]{:S(2)}, u32[]{:S(2)}) collective-permute-start(f32[72,128]{1,0:T(8,128)S(1)} %get-tuple-element.29), channel_id=1, source_target_pairs={{0,0},{16,1},{32,2},{48,3},{64,4},{80,5},{96,6},{112,7},{128,8},{1... | collective-permute-start | bytes 110600 | tf_op jit(solution)/shard_map/ppermute | solution.py:253
  57.0 3.4 %shard_map.98 = (f32[1024,128]{1,0:T(8,128)S(1)}, bf16[2,1024,512]{2,1,0:T(8,128)(2,1)S(1)}, bf16[2,1024,512]{2,1,0:T(8,128)(2,1)S(1)}) custom-call(s32[7]{0:T(128)S(1)} %stack.31.refs_0_.place_ref, f32[16,72,128]{2,1,0:T(8,128)S(1)} %all-to-all-done.refs_1_, f32[16,8,128]{2,1,0:T(8,128)S(1)} %bitcast.15), custom_call_target="tpu_custom_call" | custom-call | flops 1073741824 | bytes 8388608 | tf_op jit(solution)/shard_map/pallas_call | solution.py:258
  60.5 0.0 collective-permute-done.5.refs_3_.mine_ref
  60.5 0.0 collective-permute-done.4.refs_1_
  60.5 0.0 copy-start.2
  60.5 0.0 copy-start.3
  60.5 0.0 copy-start.4
  60.5 3.5 %shard_map.99 = (f32[1024,128]{1,0:T(8,128)S(1)}, bf16[2,1024,512]{2,1,0:T(8,128)(2,1)S(1)}, bf16[2,1024,512]{2,1,0:T(8,128)(2,1)S(1)}) custom-call(s32[7]{0:T(128)S(1)} %stack.31.refs_0_.place_ref, f32[16,72,128]{2,1,0:T(8,128)S(1)} %collective-permute-done.4.refs_1_, f32[16,8,128]{2,1,0:T(8,128)S(1)} %bitcast.16, ...), custom_call_target="tpu_custom_call" | custom-call | flops 1073741824 | bytes 8388608 | tf_op jit(solution)/shard_map/pallas_call | solution.py:261
  64.0 25.6 %all_to_all.30.parts_ref = f32[16,64,128]{2,1,0:T(8,128)S(1)} all-to-all(f32[16,64,128]{2,1,0:T(8,128)S(1)} %bitcast.14), channel_id=1, replica_groups=mesh['z2'=2,'z1'=2,'z0'=2,'x'=4,'y'=4,'zhi'=2,'core'=2] {'x','y'}, dimensions={0} | all-to-all | bytes 1048576 | tf_op jit(solution)/shard_map/all_to_all | solution.py:265
  89.6 0.0 copy-done.3
  89.6 0.8 shard_map.100
  90.4 12.7 %all_to_all.31.pressure_ref = f32[16,64,128]{2,1,0:T(8,128)S(1)} all-to-all(f32[16,64,128]{2,1,0:T(8,128)S(1)} %get-tuple-element.33), channel_id=1, replica_groups=mesh['z2'=2,'z1'=2,'z0'=2,'x'=4,'y'=4,'zhi'=2,'core'=2] {'x','y'}, dimensions={0} | all-to-all | bytes 1048576 | tf_op jit(solution)/shard_map/all_to_all | solution.py:269
  103.1 0.2 shard_map.101.both_ref
  103.3 1.9 %shard_map.103 = f32[2,512,128]{2,1,0:T(8,128)S(1)} custom-call(s32[7]{0:T(128)S(1)} %stack.31.refs_0_.place_ref, bf16[256,1024]{1,0:T(8,128)(2,1)S(1)} %shard_map.101.both_ref, bf16[2,1024,512]{2,1,0:T(8,128)(2,1)S(1)} %get-tuple-element.36.high_ref, bf16[2,1024,512]{2,1,0:T(8,128)(2,1)S(1)} %get-tuple-element.37.low_ref), custom_call_target="tpu_custom_call" | custom-call | flops 1073741824 | bytes 8388608 | tf_op jit(solution)/shard_map/pallas_call | solution.py:274
  105.2 5.2 %collective-permute-start.6 = (f32[2,512,128]{2,1,0:T(8,128)S(1)}, f32[2,512,128]{2,1,0:T(8,128)S(1)}, u32[]{:S(2)}, u32[]{:S(2)}) collective-permute-start(f32[2,512,128]{2,1,0:T(8,128)S(1)} %shard_map.103), channel_id=1, source_target_pairs={{0,1},{1,0},{2,3},{3,2},{4,5},{5,4},{6,7},{7,6},{8,9},{9,8},{10,11... | collective-permute-start | bytes 1572872 | tf_op jit(solution)/shard_map/ppermute | solution.py:274
  110.4 1.9 %shard_map.102.a_ref = f32[2,512,128]{2,1,0:T(8,128)S(1)} custom-call(s32[7]{0:T(128)S(1)} %stack.31.refs_0_.place_ref, bf16[256,1024]{1,0:T(8,128)(2,1)S(1)} %shard_map.101.both_ref, bf16[2,1024,512]{2,1,0:T(8,128)(2,1)S(1)} %get-tuple-element.34.high_ref, bf16[2,1024,512]{2,1,0:T(8,128)(2,1)S(1)} %get-tuple-element.35.low_ref), custom_call_target="tpu_custom_call" | custom-call | flops 1073741824 | bytes 8388608 | tf_op jit(solution)/shard_map/pallas_call | solution.py:275
  112.4 0.0 copy-start.1
  112.4 0.0 collective-permute-done.6.b_ref
  112.4 0.1 shard_map.104
  112.4 1.9 %collective-permute-start.7 = (f32[512,128]{1,0:T(8,128)S(1)}, f32[512,128]{1,0:T(8,128)S(1)}, u32[]{:S(2)}, u32[]{:S(2)}) collective-permute-start(f32[512,128]{1,0:T(8,128)S(1)} %get-tuple-element.39), channel_id=1, source_target_pairs={{0,64},{64,0},{1,65},{65,1},{2,66},{66,2},{3,67},{67,3},{4,68},{68... | collective-permute-start | bytes 786440 | tf_op jit(solution)/shard_map/ppermute | solution.py:278
  114.4 7.9 %collective-permute-done.7.b_ref = f32[512,128]{1,0:T(8,128)S(1)} collective-permute-done((f32[512,128]{1,0:T(8,128)S(1)}, f32[512,128]{1,0:T(8,128)S(1)}, u32[]{:S(2)}, u32[]{:S(2)}) %collective-permute-start.7) | collective-permute-done | bytes 262176 | tf_op jit(solution)/shard_map/ppermute | solution.py:278
  122.3 0.7 shard_map.105
  123.0 6.7 %all-to-all-start.3 = ((f32[8,64,128]{2,1,0:T(8,128)}), f32[8,64,128]{2,1,0:T(8,128)S(1)}, u32[]{:S(2)}, u32[]{:S(2)}) async-start(f32[8,64,128]{2,1,0:T(8,128)} %bitcast.11), calls=%async_computation.3 | async-start | bytes 524288 | tf_op jit(solution)/shard_map/all_to_all | solution.py:281
  129.7 2.3 %collective-permute-start.8 = (f32[64,128]{1,0:T(8,128)S(1)}, f32[64,128]{1,0:T(8,128)S(1)}, u32[]{:S(2)}, u32[]{:S(2)}) collective-permute-start(f32[64,128]{1,0:T(8,128)S(1)} %get-tuple-element.40), channel_id=1, source_target_pairs={{0,0},{1,16},{2,32},{3,48},{4,64},{5,80},{6,96},{7,112},{8,128},{9... | collective-permute-start | bytes 98312 | tf_op jit(solution)/shard_map/ppermute | solution.py:280
  132.7 3.8 %collective-permute-done.8.own_ref = f32[64,128]{1,0:T(8,128)S(1)} collective-permute-done((f32[64,128]{1,0:T(8,128)S(1)}, f32[64,128]{1,0:T(8,128)S(1)}, u32[]{:S(2)}, u32[]{:S(2)}) %collective-permute-start.8) | collective-permute-done | bytes 32800 | tf_op jit(solution)/shard_map/ppermute | solution.py:280
  136.5 10.4 %all-to-all-done.3.parts_ref = f32[8,64,128]{2,1,0:T(8,128)S(1)} async-done(((f32[8,64,128]{2,1,0:T(8,128)}), f32[8,64,128]{2,1,0:T(8,128)S(1)}, u32[]{:S(2)}, u32[]{:S(2)}) %all-to-all-start.3) | async-done | bytes 262176 | tf_op jit(solution)/shard_map/all_to_all | solution.py:281
  146.8 0.0 copy-done.1
  146.8 0.7 shard_map.106
  147.5 22.8 %all_to_all.32 = f32[32,1,128]{2,1,0:T(1,128)S(1)} all-to-all(f32[32,1,128]{2,1,0:T(1,128)S(1)} %get-tuple-element.43), channel_id=1, replica_groups=mesh['z2'=2,'z1'=2,'z0'=2,'x'=4,'y'=4,'zhi'=2,'core'=2] {'z0','zhi','z2'..., dimensions={0} | all-to-all | bytes 32768 | tf_op jit(solution)/shard_map/all_to_all | solution.py:285
  170.3 0.1 reduce_sum.18
  170.3 10.9 %all_to_all.33 = f32[16,1,128]{2,1,0:T(1,128)S(1)} all-to-all(f32[16,1,128]{2,1,0:T(1,128)S(1)} %broadcast_in_dim.18), channel_id=1, replica_groups=mesh['z2'=2,'z1'=2,'z0'=2,'x'=4,'y'=4,'zhi'=2,'core'=2] {'x','y'}, dimensions={0} | all-to-all | bytes 16384 | tf_op jit(solution)/shard_map/all_to_all | solution.py:286
  181.3 0.6 reduce_sum.19
  (9 shorter events, 0.0 us)
Async XLA Ops:
  1.5 0.8 copy-start
  3.1 42.3 %all-to-all-start = ((f32[16,72,128]{2,1,0:T(8,128)}), f32[16,72,128]{2,1,0:T(8,128)S(1)}, u32[]{:S(2)}, u32[]{:S(2)}) async-start(f32[16,72,128]{2,1,0:T(8,128)} %get-tuple-element.24), calls=%async_computation | async-start | bytes 1179648 | tf_op jit(solution)/shard_map/all_to_all | solution.py:245
  18.9 4.4 %collective-permute-start = (f32[8,128]{1,0:T(8,128)S(1)}, f32[8,128]{1,0:T(8,128)S(1)}, u32[]{:S(2)}, u32[]{:S(2)}) collective-permute-start(f32[8,128]{1,0:T(8,128)S(1)} %get-tuple-element.25.a_ref), channel_id=1, source_target_pairs={{0,16},{16,0},{32,48},{48,32},{1,17},{17,1},{33,49},{49,33},{2,18}... | collective-permute-start | bytes 12296 | tf_op jit(solution)/shard_map/ppermute | solution.py:248
  23.2 5.9 %collective-permute-start.1 = (f32[16,128]{1,0:T(8,128)S(1)}, f32[16,128]{1,0:T(8,128)S(1)}, u32[]{:S(2)}, u32[]{:S(2)}) collective-permute-start(f32[16,128]{1,0:T(8,128)S(1)} %shard_map.94.a_ref), channel_id=1, source_target_pairs={{0,32},{16,48},{32,0},{48,16},{1,33},{17,49},{33,1},{49,17},{2,34}... | collective-permute-start | bytes 24584 | tf_op jit(solution)/shard_map/ppermute | solution.py:248
  29.1 4.8 %collective-permute-start.2 = (f32[32,128]{1,0:T(8,128)S(1)}, f32[32,128]{1,0:T(8,128)S(1)}, u32[]{:S(2)}, u32[]{:S(2)}) collective-permute-start(f32[32,128]{1,0:T(8,128)S(1)} %shard_map.95.a_ref), channel_id=1, source_target_pairs={{0,4},{4,0},{8,12},{12,8},{1,5},{5,1},{9,13},{13,9},{2,6},{6,2},{1... | collective-permute-start | bytes 49160 | tf_op jit(solution)/shard_map/ppermute | solution.py:248
  33.9 6.5 %collective-permute-start.3 = (f32[64,128]{1,0:T(8,128)S(1)}, f32[64,128]{1,0:T(8,128)S(1)}, u32[]{:S(2)}, u32[]{:S(2)}) collective-permute-start(f32[64,128]{1,0:T(8,128)S(1)} %shard_map.96.a_ref), channel_id=1, source_target_pairs={{0,8},{4,12},{8,0},{12,4},{1,9},{5,13},{9,1},{13,5},{2,10},{6,14},... | collective-permute-start | bytes 98312 | tf_op jit(solution)/shard_map/ppermute | solution.py:248
  45.4 15.1 %collective-permute-start.4 = (f32[16,72,128]{2,1,0:T(8,128)S(1)}, f32[16,72,128]{2,1,0:T(8,128)S(1)}, u32[]{:S(2)}, u32[]{:S(2)}) collective-permute-start(f32[16,72,128]{2,1,0:T(8,128)S(1)} %all-to-all-done.refs_1_), channel_id=1, source_target_pairs={{0,1},{1,0},{2,3},{3,2},{4,5},{5,4},{6,7},{7,6},{8,9},{9,8},{10,11... | collective-permute-start | bytes 1769480 | tf_op jit(solution)/shard_map/ppermute | solution.py:252
  52.5 8.0 %collective-permute-start.5 = (f32[72,128]{1,0:T(8,128)S(1)}, f32[72,128]{1,0:T(8,128)S(1)}, u32[]{:S(2)}, u32[]{:S(2)}) collective-permute-start(f32[72,128]{1,0:T(8,128)S(1)} %get-tuple-element.29), channel_id=1, source_target_pairs={{0,0},{16,1},{32,2},{48,3},{64,4},{80,5},{96,6},{112,7},{128,8},{1... | collective-permute-start | bytes 110600 | tf_op jit(solution)/shard_map/ppermute | solution.py:253
  60.5 29.1 %copy-start.2 = (s32[2,64]{1,0:T(2,128)S(1)}, s32[2,64]{1,0:T(2,128)}, u32[]{:S(2)}) copy-start(s32[2,64]{1,0:T(2,128)} %listener_ref.1) | copy-start | bytes 1540
  60.5 29.1 %copy-start.3 = (s32[64]{0:T(128)S(1)}, s32[64]{0:T(128)}, u32[]{:S(2)}) copy-start(s32[64]{0:T(128)} %param.9) | copy-start | bytes 772
  60.5 29.1 %copy-start.4 = (s32[64]{0:T(128)S(1)}, s32[64]{0:T(128)}, u32[]{:S(2)}) copy-start(s32[64]{0:T(128)} %param.10) | copy-start | bytes 772
  105.2 7.1 %collective-permute-start.6 = (f32[2,512,128]{2,1,0:T(8,128)S(1)}, f32[2,512,128]{2,1,0:T(8,128)S(1)}, u32[]{:S(2)}, u32[]{:S(2)}) collective-permute-start(f32[2,512,128]{2,1,0:T(8,128)S(1)} %shard_map.103), channel_id=1, source_target_pairs={{0,1},{1,0},{2,3},{3,2},{4,5},{5,4},{6,7},{7,6},{8,9},{9,8},{10,11... | collective-permute-start | bytes 1572872 | tf_op jit(solution)/shard_map/ppermute | solution.py:274
  112.4 34.5 %copy-start.1 = (f32[64,128]{1,0:T(8,128)S(1)}, f32[64,128]{1,0:T(8,128)}, u32[]{:S(2)}) copy-start(f32[64,128]{1,0:T(8,128)} %powers_ref.3) | copy-start | bytes 98308
  112.4 9.8 %collective-permute-start.7 = (f32[512,128]{1,0:T(8,128)S(1)}, f32[512,128]{1,0:T(8,128)S(1)}, u32[]{:S(2)}, u32[]{:S(2)}) collective-permute-start(f32[512,128]{1,0:T(8,128)S(1)} %get-tuple-element.39), channel_id=1, source_target_pairs={{0,64},{64,0},{1,65},{65,1},{2,66},{66,2},{3,67},{67,3},{4,68},{68... | collective-permute-start | bytes 786440 | tf_op jit(solution)/shard_map/ppermute | solution.py:278
  123.0 23.8 %all-to-all-start.3 = ((f32[8,64,128]{2,1,0:T(8,128)}), f32[8,64,128]{2,1,0:T(8,128)S(1)}, u32[]{:S(2)}, u32[]{:S(2)}) async-start(f32[8,64,128]{2,1,0:T(8,128)} %bitcast.11), calls=%async_computation.3 | async-start | bytes 524288 | tf_op jit(solution)/shard_map/all_to_all | solution.py:281
  129.7 6.7 %collective-permute-start.8 = (f32[64,128]{1,0:T(8,128)S(1)}, f32[64,128]{1,0:T(8,128)S(1)}, u32[]{:S(2)}, u32[]{:S(2)}) collective-permute-start(f32[64,128]{1,0:T(8,128)S(1)} %get-tuple-element.40), channel_id=1, source_target_pairs={{0,0},{1,16},{2,32},{3,48},{4,64},{5,80},{6,96},{7,112},{8,128},{9... | collective-permute-start | bytes 98312 | tf_op jit(solution)/shard_map/ppermute | solution.py:280

commit v5 on v4

--- a/solution.py
+++ b/solution.py
@@ -57,19 +57,22 @@
     return norm - low, low - odd, odd
 
 
-def pack_kernel(info_ref, powers_ref, sent_ref, heard_ref, mine_ref):
-    sx, sy, lx, ly = (info_ref[i : i + 1, :] for i in range(4))
+def hear_kernel(info_ref, heard_ref):
+    lx, ly = info_ref[0:1, :], info_ref[1:2, :]
+    one = jnp.ones_like(lx)
+    l1, l2, l3 = split_norm(lx * lx + ly * ly + 1)
+    heard = jnp.concatenate([lx, ly, l1, l2, l3, one, one, one], axis=0).astype(F32)
+    user = jnp.concatenate([info_ref[2:4, :].astype(F32), jnp.zeros((6, BLOCK), F32)], axis=0)
+    heard_ref[...] = jnp.concatenate([heard, user], axis=1)
+
+
+def pack_kernel(sender_ref, powers_ref, sent_ref):
+    sx, sy = sender_ref[0:1, :], sender_ref[1:2, :]
     one = jnp.ones_like(sx)
     s1, s2, s3 = split_norm(sx * sx + sy * sy)
-    l1, l2, l3 = split_norm(lx * lx + ly * ly + 1)
     sent = jnp.concatenate([-2 * sx, -2 * sy, one, one, one, s1, s2, s3], axis=0).astype(F32)
-    heard = jnp.concatenate([lx, ly, l1, l2, l3, one, one, one], axis=0).astype(F32)
-    pad = jnp.zeros_like(sent)
-    sent = jnp.concatenate([sent, pad], axis=1)
-    heard_ref[...] = jnp.concatenate([heard, pad], axis=1)
+    sent = jnp.concatenate([sent, jnp.zeros_like(sent)], axis=1)
     powers = powers_ref[...]
-    mine_ref[0:BLOCK, :] = powers
-    mine_ref[BLOCK:, :] = sent
     for k in range(NZ):
         sent_ref[k, 0:BLOCK, :] = powers
         sent_ref[k, BLOCK:SENT, :] = sent
@@ -95,7 +98,7 @@
     if first:
         total_ref, high_ref, low_ref = rest
     else:
-        _, before_ref, total_ref, high_ref, low_ref = rest
+        before_ref, total_ref, high_ref, low_ref = rest
     x, y, z0, z2, z1, zhi, core = (place_ref[i] for i in range(7))
     source_core = core if first else 1 - core
     senders = spread(sent_ref, BLOCK, lambda k: k)
@@ -104,12 +107,12 @@
     power_high, power_low = split(powers)
     power_both = jnp.concatenate([power_high, power_low], axis=1)
     tile_rows, tile_cols = 256, 128
-    receiver_base = (z2 * 4 + z1 * 2 + z0) * 4096 + zhi * 128 + core * 64
+    receiver_base = zhi * 4096 + core * 2048 + (z2 * 4 + z1 * 2 + z0) * 256
     sender_base = y * 8192 + source_core * 2048 + x * 64
     for r in range(0, ROWS, tile_rows):
         row = lax.broadcasted_iota(jnp.int32, (tile_rows, tile_cols), 0) + r
         block = row >> 6
-        row_id = receiver_base + (block >> 2) * 1024 + (block & 3) * 256 + (row & 63)
+        row_id = receiver_base + (block & 3) * 8192 + (block >> 2) * 64 + (row & 63)
         for c in range(0, HALF, tile_cols):
             col = lax.broadcasted_iota(jnp.int32, (1, tile_cols), 1) + c
             zed = col >> 6
@@ -147,11 +150,11 @@
     both_ref[BANDS:, :] = pressure_low
 
 
-def react_kernel(place_ref, both_ref, high_ref, low_ref, pushed_ref):
+def react_kernel(sides, place_ref, both_ref, high_ref, low_ref, pushed_ref):
     both = both_ref[...]
     step = 256
-    for k in (0, 1):
-        side = place_ref[2] ^ k
+    for k, flip in enumerate(sides):
+        side = place_ref[2] ^ flip
         for c in range(0, WIDE, step):
             product = jnp.dot(both, high_ref[side, :, c : c + step], preferred_element_type=F32)
             product = product + jnp.dot(
@@ -171,13 +174,25 @@
     return call(join_kernel, shape(2 * rows, lanes), 2, 0, 16 * a.size)(a, b)
 
 
-def combine_kernel(a_ref, b_ref, kept_ref, passed_ref):
-    kept_ref[...] = a_ref[0] + b_ref[0]
-    passed_ref[...] = a_ref[1] + b_ref[1]
-
-
-def add_kernel(a_ref, b_ref, sum_ref):
-    sum_ref[...] = a_ref[...] + b_ref[...]
+def add_kernel(side, near_ref, across_ref, *rest):
+    total = near_ref[0] + across_ref[side]
+    for ref in rest[:-1]:
+        total = total + ref[...]
+    rest[-1][...] = total
+
+
+def add(side, *parts):
+    def kernel(*refs):
+        add_kernel(side, *refs)
+
+    size = WIDE * BANDS
+    return call(kernel, shape(WIDE, BANDS), len(parts), size, 12 * size)(*parts)
+
+
+def fold_kernel(parts_ref, out_ref):
+    total = jnp.sum(parts_ref[...], axis=0)
+    for k in range(NXY):
+        out_ref[k] = total
 
 
 def add_blocks(ref, count):
@@ -188,15 +203,15 @@
 
 
 def derive_kernel(
-    parts_ref, mine_ref, listener_ref, weight_ref, fair_ref, quality_ref, own_ref, pressure_ref
+    parts_ref, powers_ref, sender_ref, heard_ref, quality_ref, own_ref, pressure_ref
 ):
     interference = add_blocks(parts_ref, NXY)
-    powers = mine_ref[0:BLOCK, :]
-    dx = listener_ref[0:1, :].astype(F32) + 0.5 * mine_ref[BLOCK : BLOCK + 1, 0:BLOCK]
-    dy = listener_ref[1:2, :].astype(F32) + 0.5 * mine_ref[BLOCK + 1 : BLOCK + 2, 0:BLOCK]
+    powers = powers_ref[...]
+    dx = heard_ref[0:1, 0:BLOCK] - sender_ref[0:1, :].astype(F32)
+    dy = heard_ref[1:2, 0:BLOCK] - sender_ref[1:2, :].astype(F32)
     own_gain = 1.0 / (1.0 + dx * dx + dy * dy)
-    weight = WEIGHT_UNIT * weight_ref[...].astype(F32)
-    fair = fair_ref[...].astype(F32)
+    weight = WEIGHT_UNIT * heard_ref[0:1, BLOCK:]
+    fair = heard_ref[1:2, BLOCK:]
     rows = jnp.concatenate([own_gain, weight, fair, jnp.zeros((5, BLOCK), F32)], axis=0)
     rows = jnp.concatenate([rows, jnp.zeros_like(rows)], axis=1)
     columns = jnp.concatenate([rows, jnp.zeros((120, 128), F32)], axis=0).T
@@ -238,19 +253,20 @@
     swap = [(0, 1), (1, 0)]
     block, blocks = shape(BLOCK, BANDS), shape(NXY, BLOCK, BANDS)
 
-    rows = [sender_xy, listener_xy, jnp.zeros((4, BLOCK), jnp.int32)]
-    sent, heard, mine = call(
-        pack_kernel, (shape(NZ, SENT, BANDS), shape(8, 128), shape(SENT, BANDS)), 2
-    )(jnp.concatenate(rows, axis=0), powers)
+    rows = [listener_xy, weight[None], fairness[None]]
+    heard = call(hear_kernel, shape(8, 128), 1)(jnp.concatenate(rows, axis=0))
+    heard = lax.ppermute(heard, AXES, to_sender)
+    sent = call(pack_kernel, shape(NZ, SENT, BANDS), 2)(sender_xy, powers)
+    heard, sent = lax.optimization_barrier((heard, sent))
+    mine = heard
     near = lax.all_to_all(sent, Z, 0, 0)
     for axis in XY:
         for bit in (1, 2):
             other = lax.ppermute(heard, axis, [(i, i ^ bit) for i in range(4)])
             heard = join(heard, other)
-    near, heard, mine = lax.optimization_barrier((near, heard, mine))
+    near, heard = lax.optimization_barrier((near, heard))
     listeners = heard.reshape(NXY, 8, 128)
     far = lax.ppermute(near, "core", swap)
-    mine = lax.ppermute(mine, AXES, to_receiver)
 
     gains = shape(2, ROWS, WIDE, dtype=BF16)
     work = dict(flops=2 * ROWS * HALF * 512, bytes_accessed=1 << 23)
@@ -259,31 +275,36 @@
         lambda *refs: interfere_kernel(True, *refs), outs, 3, smem=(0,), **work
     )(place, near, listeners)
     part, far_high, far_low = call(
-        lambda *refs: interfere_kernel(False, *refs), outs, 5, smem=(0,), **work
-    )(place, far, listeners, mine, part)
+        lambda *refs: interfere_kernel(False, *refs), outs, 4, smem=(0,), **work
+    )(place, far, listeners, part)
 
     parts = lax.all_to_all(part.reshape(NXY, BLOCK, BANDS), XY, 0, 0)
-    quality, own, pressure = call(derive_kernel, (block, block, blocks), 5)(
-        parts, mine, listener_xy, weight[None], fairness[None]
+    quality, own, pressure = call(derive_kernel, (block, block, blocks), 4)(
+        parts, powers, sender_xy, mine
     )
     pressures = lax.all_to_all(pressure, XY, 0, 0)
     both = call(turn_kernel, shape(2 * BANDS, ROWS, dtype=BF16), 1)(pressures)
 
-    half = shape(2, WIDE, BANDS)
-    react = call(react_kernel, half, 4, smem=(0,), **work)
-    across = lax.ppermute(react(place, both, far_high, far_low), "core", swap)
-    pushed = react(place, both, near_high, near_low)
-    side = shape(WIDE, BANDS)
-    kept, passed = call(combine_kernel, (side, side), 2)(pushed, across)
+    def react(high, low, *sides):
+        def kernel(*refs):
+            react_kernel(sides, *refs)
+
+        cost = dict(flops=len(sides) * work["flops"] // 2, bytes_accessed=len(sides) << 21)
+        out = shape(len(sides), WIDE, BANDS)
+        return call(kernel, out, 4, smem=(0,), **cost)(place, both, high, low)
+
+    across = lax.ppermute(react(far_high, far_low, 0, 1), "core", swap)
+    passed = add(1, react(near_high, near_low, 1), across)
     passed = lax.ppermute(passed, "z0", swap)
-    pushed = call(add_kernel, side, 2)(kept, passed)
-    own = lax.ppermute(own, AXES, to_sender)
+    pushed = add(0, react(near_high, near_low, 0), across, passed)
+    quality = lax.ppermute(quality, AXES, to_receiver)
     parts = lax.all_to_all(pushed.reshape(NZ // 2, BLOCK, BANDS), EVEN, 0, 0)
     gradient, new_power, gap = call(
         finish_kernel, (block, block, shape(2 * NZ, 1, BANDS)), 4, smem=(0,)
     )(step_code, parts, own, powers)
-    gap = jnp.sum(lax.all_to_all(gap, (*Z, "core"), 0, 0), axis=0)
-    gap = lax.all_to_all(jnp.broadcast_to(gap[None], (NXY, 1, BANDS)), XY, 0, 0)
+    gap = lax.all_to_all(gap, (*Z, "core"), 0, 0)
+    gap = call(fold_kernel, shape(NXY, 1, BANDS), 1)(gap)
+    gap = lax.all_to_all(gap, XY, 0, 0)
     return quality, gradient, new_power, (jnp.sum(gap) / (USERS * BANDS)).reshape(1)
 
 

time: 184 us -> 183 us (level)
  blocking collectives: 72 us -> 28.5 us
  waiting for transfers between devices: 32.7 us -> 58.2 us
  starting transfers between devices: 59.2 us -> 72.7 us
    all_to_all x2 -> x0, blocking collectives: 33.7 us -> none  [the longest x1 22.8 us: per_device(): gap = jnp.sum(lax.all_to_all(gap, (*Z, 'core'), 0, 0), axis=0)]
    all_to_all x0 -> x2, waiting for transfers between devices: none -> 15 us  [the longest x1 8.76 us: per_device(): gap = lax.all_to_all(gap, (*Z, 'core'), 0, 0)]
    all_to_all x0 -> x2, starting transfers between devices: none -> 11.8 us  [the longest x1 8.37 us: per_device(): gap = lax.all_to_all(gap, (*Z, 'core'), 0, 0)]
    all_to_all x1, blocking collectives: 25.6 us -> 15.3 us  [per_device(): parts = lax.all_to_all(part.reshape(NXY, BLOCK, BANDS), XY, 0, 0)]
    all_to_all x1, starting transfers between devices: 15.7 us -> 25.1 us  [per_device(): near = lax.all_to_all(sent, Z, 0, 0)]
    ppermute x4, waiting for transfers between devices: 5.72 us -> 12.1 us  [per_device(): other = lax.ppermute(heard, axis, [(i, i ^ bit) for i in range(4)])]
    ppermute x4, starting transfers between devices: 15.8 us -> 9.6 us  [per_device(): other = lax.ppermute(heard, axis, [(i, i ^ bit) for i in range(4)])]
    all_to_all x1, waiting for transfers between devices: 10.4 us -> 16.4 us  [per_device(): parts = lax.all_to_all(pushed.reshape(NZ // 2, BLOCK, BANDS), EVEN, 0, 0)]
  transfers between devices with their start and end apart: 11 -> 13, of which waited for: 8 -> 11; matrix products, arithmetic and copies ran while one was open for 0% -> 0% of each run, Pallas kernels for 3% -> 4%
where the time goes in v5:
time: 183 us; the launch traced here: 181 us
  starting transfers between devices  72.7 us (40%)
  waiting for transfers between devices  58.2 us (32%)
  blocking collectives  28.5 us (16%)
  Pallas kernels  15.1 us (8%)
  between operations  3.28 us (2%)
  local copies, waits for them, and re-layouts  2.15 us (1%)
    all_to_all x1, starting transfers between devices, per_device(): near = lax.all_to_all(sent, Z, 0, 0)  25.1 us
    all_to_all x1, waiting for transfers between devices, per_device(): parts = lax.all_to_all(pushed.reshape(NZ // 2, BLOCK, BANDS), EVEN, 0, 0)  16.4 us
    all_to_all x1, blocking collectives, per_device(): parts = lax.all_to_all(part.reshape(NXY, BLOCK, BANDS), XY, 0, 0)  15.3 us
    all_to_all x1, blocking collectives, per_device(): pressures = lax.all_to_all(pressure, XY, 0, 0)  13.2 us
    ppermute x4, waiting for transfers between devices, per_device(): other = lax.ppermute(heard, axis, [(i, i ^ bit) for i in range(4)])  12.1 us
    ppermute x4, starting transfers between devices, per_device(): other = lax.ppermute(heard, axis, [(i, i ^ bit) for i in range(4)])  9.6 us
    all_to_all x1, starting transfers between devices, per_device(): parts = lax.all_to_all(pushed.reshape(NZ // 2, BLOCK, BANDS), EVEN, 0, 0)  8.92 us
    all_to_all x1, waiting for transfers between devices, per_device(): gap = lax.all_to_all(gap, (*Z, 'core'), 0, 0)  8.76 us
  transfers between devices with their start and end apart: 13, of which 11 were waited for; matrix products, arithmetic and copies ran while one was open for 0% of the time, Pallas kernels for 4%

profile of v5, /device:TPU:1, one launch (start us, length us, event | category | flops | bytes accessed | tf_op | source)
XLA Modules:
  0.0 181.3 jit_solution(18226414097478991643)
XLA Ops:
  0.6 0.7 pad_add_fusion.info_ref
  1.4 0.1 shard_map.93
  1.4 4.5 %collective-permute-start = (f32[8,128]{1,0:T(8,128)S(1)}, f32[8,128]{1,0:T(8,128)S(1)}, u32[]{:S(2)}, u32[]{:S(2)}) collective-permute-start(f32[8,128]{1,0:T(8,128)S(1)} %shard_map.93), channel_id=1, source_target_pairs={{0,0},{1,16},{2,32},{3,48},{4,64},{5,80},{6,96},{7,112},{8,128},{9... | collective-permute-start | bytes 12296 | tf_op jit(solution)/shard_map/ppermute | solution.py:258
  5.9 0.0 copy-start
  5.9 0.7 copy-done
  6.7 0.7 copy-done.2
  7.4 0.9 shard_map.94
  8.2 0.5 collective-permute-done.a_ref.heard_ref
  8.7 25.1 %all-to-all-start = ((f32[16,72,128]{2,1,0:T(8,128)}), f32[16,72,128]{2,1,0:T(8,128)S(1)}, u32[]{:S(2)}, u32[]{:S(2)}) async-start(f32[16,72,128]{2,1,0:T(8,128)} %shard_map.94), calls=%async_computation | async-start | bytes 1179648 | tf_op jit(solution)/shard_map/all_to_all | solution.py:262
  33.8 1.9 %collective-permute-start.1 = (f32[8,128]{1,0:T(8,128)S(1)}, f32[8,128]{1,0:T(8,128)S(1)}, u32[]{:S(2)}, u32[]{:S(2)}) collective-permute-start(f32[8,128]{1,0:T(8,128)S(1)} %collective-permute-done.a_ref.heard_ref), channel_id=1, source_target_pairs={{0,16},{16,0},{32,48},{48,32},{1,17},{17,1},{33,49},{49,33},{2,18}... | collective-permute-start | bytes 12296 | tf_op jit(solution)/shard_map/ppermute | solution.py:265
  35.8 2.4 %collective-permute-done.1.b_ref = f32[8,128]{1,0:T(8,128)S(1)} collective-permute-done((f32[8,128]{1,0:T(8,128)S(1)}, f32[8,128]{1,0:T(8,128)S(1)}, u32[]{:S(2)}, u32[]{:S(2)}) %collective-permute-start.1) | collective-permute-done | bytes 4128 | tf_op jit(solution)/shard_map/ppermute | solution.py:265
  38.2 1.9 %collective-permute-start.2 = (f32[16,128]{1,0:T(8,128)S(1)}, f32[16,128]{1,0:T(8,128)S(1)}, u32[]{:S(2)}, u32[]{:S(2)}) collective-permute-start(f32[16,128]{1,0:T(8,128)S(1)} %shard_map.95.a_ref), channel_id=1, source_target_pairs={{0,32},{16,48},{32,0},{48,16},{1,33},{17,49},{33,1},{49,17},{2,34}... | collective-permute-start | bytes 24584 | tf_op jit(solution)/shard_map/ppermute | solution.py:265
  40.1 4.3 %collective-permute-done.2.b_ref = f32[16,128]{1,0:T(8,128)S(1)} collective-permute-done((f32[16,128]{1,0:T(8,128)S(1)}, f32[16,128]{1,0:T(8,128)S(1)}, u32[]{:S(2)}, u32[]{:S(2)}) %collective-permute-start.2) | collective-permute-done | bytes 8224 | tf_op jit(solution)/shard_map/ppermute | solution.py:265
  44.4 3.6 %collective-permute-start.3 = (f32[32,128]{1,0:T(8,128)S(1)}, f32[32,128]{1,0:T(8,128)S(1)}, u32[]{:S(2)}, u32[]{:S(2)}) collective-permute-start(f32[32,128]{1,0:T(8,128)S(1)} %shard_map.96.a_ref), channel_id=1, source_target_pairs={{0,4},{4,0},{8,12},{12,8},{1,5},{5,1},{9,13},{13,9},{2,6},{6,2},{1... | collective-permute-start | bytes 49160 | tf_op jit(solution)/shard_map/ppermute | solution.py:265
  48.0 1.4 collective-permute-done.3.b_ref
  49.4 2.1 %collective-permute-start.4 = (f32[64,128]{1,0:T(8,128)S(1)}, f32[64,128]{1,0:T(8,128)S(1)}, u32[]{:S(2)}, u32[]{:S(2)}) collective-permute-start(f32[64,128]{1,0:T(8,128)S(1)} %shard_map.97.a_ref), channel_id=1, source_target_pairs={{0,8},{4,12},{8,0},{12,4},{1,9},{5,13},{9,1},{13,5},{2,10},{6,14},... | collective-permute-start | bytes 98312 | tf_op jit(solution)/shard_map/ppermute | solution.py:265
  51.6 4.0 %collective-permute-done.4.b_ref = f32[64,128]{1,0:T(8,128)S(1)} collective-permute-done((f32[64,128]{1,0:T(8,128)S(1)}, f32[64,128]{1,0:T(8,128)S(1)}, u32[]{:S(2)}, u32[]{:S(2)}) %collective-permute-start.4) | collective-permute-done | bytes 32800 | tf_op jit(solution)/shard_map/ppermute | solution.py:265
  55.6 8.6 %all-to-all-done.refs_1_ = f32[16,72,128]{2,1,0:T(8,128)S(1)} async-done(((f32[16,72,128]{2,1,0:T(8,128)}), f32[16,72,128]{2,1,0:T(8,128)S(1)}, u32[]{:S(2)}, u32[]{:S(2)}) %all-to-all-start) | async-done | bytes 589856 | tf_op jit(solution)/shard_map/all_to_all | solution.py:262
  64.2 1.9 %collective-permute-start.5 = (f32[16,72,128]{2,1,0:T(8,128)S(1)}, f32[16,72,128]{2,1,0:T(8,128)S(1)}, u32[]{:S(2)}, u32[]{:S(2)}) collective-permute-start(f32[16,72,128]{2,1,0:T(8,128)S(1)} %all-to-all-done.refs_1_), channel_id=1, source_target_pairs={{0,1},{1,0},{2,3},{3,2},{4,5},{5,4},{6,7},{7,6},{8,9},{9,8},{10,11... | collective-permute-start | bytes 1769480 | tf_op jit(solution)/shard_map/ppermute | solution.py:269
  66.1 0.1 stack.31.refs_0_
  66.2 3.5 %shard_map.99 = (f32[1024,128]{1,0:T(8,128)S(1)}, bf16[2,1024,512]{2,1,0:T(8,128)(2,1)S(1)}, bf16[2,1024,512]{2,1,0:T(8,128)(2,1)S(1)}) custom-call(s32[7]{0:T(128)S(1)} %stack.31.refs_0_, f32[16,72,128]{2,1,0:T(8,128)S(1)} %all-to-all-done.refs_1_, f32[16,8,128]{2,1,0:T(8,128)S(1)} %bitcast.14), custom_call_target="tpu_custom_call" | custom-call | flops 1073741824 | bytes 8388608 | tf_op jit(solution)/shard_map/pallas_call | solution.py:274
  69.7 0.0 copy-start.1
  69.7 0.0 copy-start.3
  69.7 3.5 %shard_map.100 = (f32[1024,128]{1,0:T(8,128)S(1)}, bf16[2,1024,512]{2,1,0:T(8,128)(2,1)S(1)}, bf16[2,1024,512]{2,1,0:T(8,128)(2,1)S(1)}) custom-call(s32[7]{0:T(128)S(1)} %stack.31.refs_0_, f32[16,72,128]{2,1,0:T(8,128)S(1)} %collective-permute-done.5.refs_1_, f32[16,8,128]{2,1,0:T(8,128)S(1)} %bitcast.15, f32[1024,128]{1,0:T(8,128)S(1)} %get-tuple-element.24.refs_3_), custom_call_target="tpu_custom_call" | custom-call | flops 1073741824 | bytes 8388608 | tf_op jit(solution)/shard_map/pallas_call | solution.py:277
  73.2 15.3 %all_to_all.30.parts_ref = f32[16,64,128]{2,1,0:T(8,128)S(1)} all-to-all(f32[16,64,128]{2,1,0:T(8,128)S(1)} %bitcast.13), channel_id=1, replica_groups=mesh['z2'=2,'z1'=2,'z0'=2,'x'=4,'y'=4,'zhi'=2,'core'=2] {'x','y'}, dimensions={0} | all-to-all | bytes 1048576 | tf_op jit(solution)/shard_map/all_to_all | solution.py:281
  88.5 0.3 shard_map.101
  88.8 13.2 %all_to_all.31.pressure_ref = f32[16,64,128]{2,1,0:T(8,128)S(1)} all-to-all(f32[16,64,128]{2,1,0:T(8,128)S(1)} %get-tuple-element.27), channel_id=1, replica_groups=mesh['z2'=2,'z1'=2,'z0'=2,'x'=4,'y'=4,'zhi'=2,'core'=2] {'x','y'}, dimensions={0} | all-to-all | bytes 1048576 | tf_op jit(solution)/shard_map/all_to_all | solution.py:285
  102.0 0.2 shard_map.102.refs_1_
  102.2 1.9 %shard_map.104 = f32[2,512,128]{2,1,0:T(8,128)S(1)} custom-call(s32[7]{0:T(128)S(1)} %stack.31.refs_0_, bf16[256,1024]{1,0:T(8,128)(2,1)S(1)} %shard_map.102.refs_1_, bf16[2,1024,512]{2,1,0:T(8,128)(2,1)S(1)} %get-tuple-element.30.refs_2_, bf16[2,1024,512]{2,1,0:T(8,128)(2,1)S(1)} %get-tuple-element.31.refs_3_), custom_call_target="tpu_custom_call" | custom-call | flops 1073741824 | bytes 4194304 | tf_op jit(solution)/shard_map/pallas_call | solution.py:294
  104.1 5.4 %collective-permute-start.7 = (f32[2,512,128]{2,1,0:T(8,128)S(1)}, f32[2,512,128]{2,1,0:T(8,128)S(1)}, u32[]{:S(2)}, u32[]{:S(2)}) collective-permute-start(f32[2,512,128]{2,1,0:T(8,128)S(1)} %shard_map.104), channel_id=1, source_target_pairs={{0,1},{1,0},{2,3},{3,2},{4,5},{5,4},{6,7},{7,6},{8,9},{9,8},{10,11... | collective-permute-start | bytes 1572872 | tf_op jit(solution)/shard_map/ppermute | solution.py:296
  109.5 1.3 shard_map.105.refs_0_
  110.8 0.2 collective-permute-done.7.refs_1_
  111.0 2.5 %collective-permute-start.8 = (f32[512,128]{1,0:T(8,128)S(1)}, f32[512,128]{1,0:T(8,128)S(1)}, u32[]{:S(2)}, u32[]{:S(2)}) collective-permute-start(f32[512,128]{1,0:T(8,128)S(1)} %shard_map.106), channel_id=1, source_target_pairs={{0,64},{64,0},{1,65},{65,1},{2,66},{66,2},{3,67},{67,3},{4,68},{68... | collective-permute-start | bytes 786440 | tf_op jit(solution)/shard_map/ppermute | solution.py:298
  113.6 1.3 shard_map.103.refs_0_
  114.9 5.5 %collective-permute-done.8.refs_2_ = f32[512,128]{1,0:T(8,128)S(1)} collective-permute-done((f32[512,128]{1,0:T(8,128)S(1)}, f32[512,128]{1,0:T(8,128)S(1)}, u32[]{:S(2)}, u32[]{:S(2)}) %collective-permute-start.8) | collective-permute-done | bytes 262176 | tf_op jit(solution)/shard_map/ppermute | solution.py:298
  120.4 0.7 shard_map.107
  121.2 8.9 %all-to-all-start.3 = ((f32[8,64,128]{2,1,0:T(8,128)}), f32[8,64,128]{2,1,0:T(8,128)S(1)}, u32[]{:S(2)}, u32[]{:S(2)}) async-start(f32[8,64,128]{2,1,0:T(8,128)} %bitcast.11), calls=%async_computation.3 | async-start | bytes 524288 | tf_op jit(solution)/shard_map/all_to_all | solution.py:301
  130.7 16.4 %all-to-all-done.3.parts_ref = f32[8,64,128]{2,1,0:T(8,128)S(1)} async-done(((f32[8,64,128]{2,1,0:T(8,128)}), f32[8,64,128]{2,1,0:T(8,128)S(1)}, u32[]{:S(2)}, u32[]{:S(2)}) %all-to-all-start.3) | async-done | bytes 262176 | tf_op jit(solution)/shard_map/all_to_all | solution.py:301
  147.1 0.7 shard_map.108
  147.8 8.4 %all-to-all-start.4 = ((f32[32,1,128]{2,1,0:T(1,128)}), f32[32,1,128]{2,1,0:T(1,128)S(1)}, u32[]{:S(2)}, u32[]{:S(2)}) async-start(f32[32,1,128]{2,1,0:T(1,128)} %get-tuple-element.35), calls=%async_computation.4 | async-start | bytes 32768 | tf_op jit(solution)/shard_map/all_to_all | solution.py:305
  156.1 2.9 %collective-permute-start.6 = (f32[64,128]{1,0:T(8,128)S(1)}, f32[64,128]{1,0:T(8,128)S(1)}, u32[]{:S(2)}, u32[]{:S(2)}) collective-permute-start(f32[64,128]{1,0:T(8,128)S(1)} %get-tuple-element.26), channel_id=1, source_target_pairs={{0,0},{16,1},{32,2},{48,3},{64,4},{80,5},{96,6},{112,7},{128,8},{1... | collective-permute-start | bytes 98312 | tf_op jit(solution)/shard_map/ppermute | solution.py:300
  159.1 8.8 %all-to-all-done.4.parts_ref = f32[32,1,128]{2,1,0:T(1,128)S(1)} async-done(((f32[32,1,128]{2,1,0:T(1,128)}), f32[32,1,128]{2,1,0:T(1,128)S(1)}, u32[]{:S(2)}, u32[]{:S(2)}) %all-to-all-start.4) | async-done | bytes 16416 | tf_op jit(solution)/shard_map/all_to_all | solution.py:305
  167.8 0.6 shard_map.109
  168.5 3.5 %all-to-all-start.5 = ((f32[16,1,128]{2,1,0:T(1,128)}), f32[16,1,128]{2,1,0:T(1,128)S(1)}, u32[]{:S(2)}, u32[]{:S(2)}) async-start(f32[16,1,128]{2,1,0:T(1,128)} %shard_map.109), calls=%async_computation.5 | async-start | bytes 16384 | tf_op jit(solution)/shard_map/all_to_all | solution.py:307
  172.0 0.0 collective-permute-done.6
  172.0 6.3 %all-to-all-done.5 = f32[16,1,128]{2,1,0:T(1,128)S(1)} async-done(((f32[16,1,128]{2,1,0:T(1,128)}), f32[16,1,128]{2,1,0:T(1,128)S(1)}, u32[]{:S(2)}, u32[]{:S(2)}) %all-to-all-start.5) | async-done | bytes 8224 | tf_op jit(solution)/shard_map/all_to_all | solution.py:307
  178.2 0.6 reduce_sum.9
  179.5 0.6 copy.12
  (9 shorter events, 0.0 us)
Async XLA Ops:
  1.4 7.3 %collective-permute-start = (f32[8,128]{1,0:T(8,128)S(1)}, f32[8,128]{1,0:T(8,128)S(1)}, u32[]{:S(2)}, u32[]{:S(2)}) collective-permute-start(f32[8,128]{1,0:T(8,128)S(1)} %shard_map.93), channel_id=1, source_target_pairs={{0,0},{1,16},{2,32},{3,48},{4,64},{5,80},{6,96},{7,112},{8,128},{9... | collective-permute-start | bytes 12296 | tf_op jit(solution)/shard_map/ppermute | solution.py:258
  5.9 0.8 copy-start
  6.7 0.7 copy-start.2
  8.7 55.4 %all-to-all-start = ((f32[16,72,128]{2,1,0:T(8,128)}), f32[16,72,128]{2,1,0:T(8,128)S(1)}, u32[]{:S(2)}, u32[]{:S(2)}) async-start(f32[16,72,128]{2,1,0:T(8,128)} %shard_map.94), calls=%async_computation | async-start | bytes 1179648 | tf_op jit(solution)/shard_map/all_to_all | solution.py:262
  33.8 4.4 %collective-permute-start.1 = (f32[8,128]{1,0:T(8,128)S(1)}, f32[8,128]{1,0:T(8,128)S(1)}, u32[]{:S(2)}, u32[]{:S(2)}) collective-permute-start(f32[8,128]{1,0:T(8,128)S(1)} %collective-permute-done.a_ref.heard_ref), channel_id=1, source_target_pairs={{0,16},{16,0},{32,48},{48,32},{1,17},{17,1},{33,49},{49,33},{2,18}... | collective-permute-start | bytes 12296 | tf_op jit(solution)/shard_map/ppermute | solution.py:265
  38.2 6.2 %collective-permute-start.2 = (f32[16,128]{1,0:T(8,128)S(1)}, f32[16,128]{1,0:T(8,128)S(1)}, u32[]{:S(2)}, u32[]{:S(2)}) collective-permute-start(f32[16,128]{1,0:T(8,128)S(1)} %shard_map.95.a_ref), channel_id=1, source_target_pairs={{0,32},{16,48},{32,0},{48,16},{1,33},{17,49},{33,1},{49,17},{2,34}... | collective-permute-start | bytes 24584 | tf_op jit(solution)/shard_map/ppermute | solution.py:265
  44.4 5.1 %collective-permute-start.3 = (f32[32,128]{1,0:T(8,128)S(1)}, f32[32,128]{1,0:T(8,128)S(1)}, u32[]{:S(2)}, u32[]{:S(2)}) collective-permute-start(f32[32,128]{1,0:T(8,128)S(1)} %shard_map.96.a_ref), channel_id=1, source_target_pairs={{0,4},{4,0},{8,12},{12,8},{1,5},{5,1},{9,13},{13,9},{2,6},{6,2},{1... | collective-permute-start | bytes 49160 | tf_op jit(solution)/shard_map/ppermute | solution.py:265
  49.4 6.2 %collective-permute-start.4 = (f32[64,128]{1,0:T(8,128)S(1)}, f32[64,128]{1,0:T(8,128)S(1)}, u32[]{:S(2)}, u32[]{:S(2)}) collective-permute-start(f32[64,128]{1,0:T(8,128)S(1)} %shard_map.97.a_ref), channel_id=1, source_target_pairs={{0,8},{4,12},{8,0},{12,4},{1,9},{5,13},{9,1},{13,5},{2,10},{6,14},... | collective-permute-start | bytes 98312 | tf_op jit(solution)/shard_map/ppermute | solution.py:265
  64.2 5.5 %collective-permute-start.5 = (f32[16,72,128]{2,1,0:T(8,128)S(1)}, f32[16,72,128]{2,1,0:T(8,128)S(1)}, u32[]{:S(2)}, u32[]{:S(2)}) collective-permute-start(f32[16,72,128]{2,1,0:T(8,128)S(1)} %all-to-all-done.refs_1_), channel_id=1, source_target_pairs={{0,1},{1,0},{2,3},{3,2},{4,5},{5,4},{6,7},{7,6},{8,9},{9,8},{10,11... | collective-permute-start | bytes 1769480 | tf_op jit(solution)/shard_map/ppermute | solution.py:269
  69.7 18.9 %copy-start.1 = (f32[64,128]{1,0:T(8,128)S(1)}, f32[64,128]{1,0:T(8,128)}, u32[]{:S(2)}) copy-start(f32[64,128]{1,0:T(8,128)} %powers_ref.5) | copy-start | bytes 98308
  69.7 18.8 %copy-start.3 = (s32[2,64]{1,0:T(2,128)S(1)}, s32[2,64]{1,0:T(2,128)}, u32[]{:S(2)}) copy-start(s32[2,64]{1,0:T(2,128)} %sender_ref.3) | copy-start | bytes 1540
  104.1 6.9 %collective-permute-start.7 = (f32[2,512,128]{2,1,0:T(8,128)S(1)}, f32[2,512,128]{2,1,0:T(8,128)S(1)}, u32[]{:S(2)}, u32[]{:S(2)}) collective-permute-start(f32[2,512,128]{2,1,0:T(8,128)S(1)} %shard_map.104), channel_id=1, source_target_pairs={{0,1},{1,0},{2,3},{3,2},{4,5},{5,4},{6,7},{7,6},{8,9},{9,8},{10,11... | collective-permute-start | bytes 1572872 | tf_op jit(solution)/shard_map/ppermute | solution.py:296
  111.0 9.4 %collective-permute-start.8 = (f32[512,128]{1,0:T(8,128)S(1)}, f32[512,128]{1,0:T(8,128)S(1)}, u32[]{:S(2)}, u32[]{:S(2)}) collective-permute-start(f32[512,128]{1,0:T(8,128)S(1)} %shard_map.106), channel_id=1, source_target_pairs={{0,64},{64,0},{1,65},{65,1},{2,66},{66,2},{3,67},{67,3},{4,68},{68... | collective-permute-start | bytes 786440 | tf_op jit(solution)/shard_map/ppermute | solution.py:298
  121.2 25.9 %all-to-all-start.3 = ((f32[8,64,128]{2,1,0:T(8,128)}), f32[8,64,128]{2,1,0:T(8,128)S(1)}, u32[]{:S(2)}, u32[]{:S(2)}) async-start(f32[8,64,128]{2,1,0:T(8,128)} %bitcast.11), calls=%async_computation.3 | async-start | bytes 524288 | tf_op jit(solution)/shard_map/all_to_all | solution.py:301
  147.8 20.1 %all-to-all-start.4 = ((f32[32,1,128]{2,1,0:T(1,128)}), f32[32,1,128]{2,1,0:T(1,128)S(1)}, u32[]{:S(2)}, u32[]{:S(2)}) async-start(f32[32,1,128]{2,1,0:T(1,128)} %get-tuple-element.35), calls=%async_computation.4 | async-start | bytes 32768 | tf_op jit(solution)/shard_map/all_to_all | solution.py:305
  156.1 15.8 %collective-permute-start.6 = (f32[64,128]{1,0:T(8,128)S(1)}, f32[64,128]{1,0:T(8,128)S(1)}, u32[]{:S(2)}, u32[]{:S(2)}) collective-permute-start(f32[64,128]{1,0:T(8,128)S(1)} %get-tuple-element.26), channel_id=1, source_target_pairs={{0,0},{16,1},{32,2},{48,3},{64,4},{80,5},{96,6},{112,7},{128,8},{1... | collective-permute-start | bytes 98312 | tf_op jit(solution)/shard_map/ppermute | solution.py:300
  168.5 9.8 %all-to-all-start.5 = ((f32[16,1,128]{2,1,0:T(1,128)}), f32[16,1,128]{2,1,0:T(1,128)S(1)}, u32[]{:S(2)}, u32[]{:S(2)}) async-start(f32[16,1,128]{2,1,0:T(1,128)} %shard_map.109), calls=%async_computation.5 | async-start | bytes 16384 | tf_op jit(solution)/shard_map/all_to_all | solution.py:307

commit v6 on v5

--- a/solution.py
+++ b/solution.py
@@ -14,7 +14,7 @@
 AXES = ("z2", "z1", "z0", "x", "y", "zhi", "core")
 SIZES = (2, 2, 2, 4, 4, 2, 2)
 EVEN = ("zhi", "z2", "z1")
-Z = ("z0", *EVEN)
+Z = (*EVEN, "z0")
 XY = ("x", "y")
 NZ, NXY = 16, 16
 BLOCK, BANDS = 64, 128
@@ -57,25 +57,19 @@
     return norm - low, low - odd, odd
 
 
-def hear_kernel(info_ref, heard_ref):
-    lx, ly = info_ref[0:1, :], info_ref[1:2, :]
-    one = jnp.ones_like(lx)
-    l1, l2, l3 = split_norm(lx * lx + ly * ly + 1)
-    heard = jnp.concatenate([lx, ly, l1, l2, l3, one, one, one], axis=0).astype(F32)
-    user = jnp.concatenate([info_ref[2:4, :].astype(F32), jnp.zeros((6, BLOCK), F32)], axis=0)
-    heard_ref[...] = jnp.concatenate([heard, user], axis=1)
-
-
-def pack_kernel(sender_ref, powers_ref, sent_ref):
-    sx, sy = sender_ref[0:1, :], sender_ref[1:2, :]
+def pack_kernel(info_ref, powers_ref, sent_ref, heard_ref):
+    sx, sy, lx, ly = (info_ref[i : i + 1, :] for i in range(4))
     one = jnp.ones_like(sx)
     s1, s2, s3 = split_norm(sx * sx + sy * sy)
+    l1, l2, l3 = split_norm(lx * lx + ly * ly + 1)
     sent = jnp.concatenate([-2 * sx, -2 * sy, one, one, one, s1, s2, s3], axis=0).astype(F32)
-    sent = jnp.concatenate([sent, jnp.zeros_like(sent)], axis=1)
-    powers = powers_ref[...]
-    for k in range(NZ):
-        sent_ref[k, 0:BLOCK, :] = powers
-        sent_ref[k, BLOCK:SENT, :] = sent
+    heard = jnp.concatenate([lx, ly, l1, l2, l3, one, one, one], axis=0).astype(F32)
+    pad = jnp.zeros_like(sent)
+    sent_ref[0:BLOCK, :] = powers_ref[...]
+    sent_ref[BLOCK:, :] = jnp.concatenate([sent, pad], axis=1)
+    heard = jnp.concatenate([heard, pad], axis=1)
+    for k in range(NXY):
+        heard_ref[k] = heard
 
 
 def spread(parts, row, index):
@@ -94,30 +88,34 @@
     return high, low
 
 
+def even_first(k):
+    return (k & 7) * 2 + (k >> 3)
+
+
 def interfere_kernel(first, place_ref, sent_ref, heard_ref, *rest):
     if first:
         total_ref, high_ref, low_ref = rest
     else:
-        before_ref, total_ref, high_ref, low_ref = rest
+        near_ref, before_ref, total_ref, high_ref, low_ref = rest
     x, y, z0, z2, z1, zhi, core = (place_ref[i] for i in range(7))
     source_core = core if first else 1 - core
-    senders = spread(sent_ref, BLOCK, lambda k: k)
-    listeners = spread(heard_ref, 0, lambda k: (((k & 3) ^ y) << 2) | ((k >> 2) ^ x))
-    powers = sent_ref[:, 0:BLOCK, :].reshape(HALF, BANDS)
+    senders = spread(sent_ref, BLOCK, even_first)
+    listeners = spread(heard_ref, 0, lambda k: k)
+    powers = jnp.concatenate([sent_ref[even_first(k), 0:BLOCK, :] for k in range(NZ)], axis=0)
     power_high, power_low = split(powers)
     power_both = jnp.concatenate([power_high, power_low], axis=1)
     tile_rows, tile_cols = 256, 128
-    receiver_base = zhi * 4096 + core * 2048 + (z2 * 4 + z1 * 2 + z0) * 256
+    per_tile = tile_rows // BLOCK
+    receiver_base = (z2 * 4 + z1 * 2 + z0) * 4096 + zhi * 128 + core * 64
     sender_base = y * 8192 + source_core * 2048 + x * 64
     for r in range(0, ROWS, tile_rows):
         row = lax.broadcasted_iota(jnp.int32, (tile_rows, tile_cols), 0) + r
         block = row >> 6
-        row_id = receiver_base + (block & 3) * 8192 + (block >> 2) * 64 + (row & 63)
+        row_id = receiver_base + (block >> 2) * 1024 + (block & 3) * 256 + (row & 63)
         for c in range(0, HALF, tile_cols):
             col = lax.broadcasted_iota(jnp.int32, (1, tile_cols), 1) + c
-            zed = col >> 6
-            zlo = ((zed >> 1) & 1) * 4 + (zed & 1) * 2 + (zed >> 3)
-            col_id = sender_base + ((zed >> 2) & 1) * 4096 + zlo * 256 + (col & 63)
+            zed = even_first(col >> 6)
+            col_id = sender_base + (zed >> 3) * 4096 + (zed & 7) * 256 + (col & 63)
             square = lax.dot_general(
                 listeners[:, r : r + tile_rows],
                 senders[:, c : c + tile_cols],
@@ -138,9 +136,17 @@
                 left = gain_ref[side, r : r + tile_rows, :]
                 product = product + jnp.dot(left, right, preferred_element_type=F32)
         part = product[:, :BANDS] + product[:, BANDS:]
-        if not first:
+        if first:
+            total_ref[r : r + tile_rows, :] = part
+        else:
+            k = r // BLOCK
             part = part + before_ref[r : r + tile_rows, :]
-        total_ref[r : r + tile_rows, :] = part
+            total_ref[k : k + per_tile, 0:BLOCK, :] = part.reshape(per_tile, BLOCK, BANDS)
+    if not first:
+        for k in range(NXY):
+            there_x, there_y = k >> 2, k & 3
+            at = z0 * 8 + (there_x & 1) * 4 + there_y
+            total_ref[k, BLOCK:, :] = jnp.where(core == there_x >> 1, near_ref[at], sent_ref[at])
 
 
 def turn_kernel(pressure_ref, both_ref):
@@ -163,17 +169,6 @@
             pushed_ref[k, c : c + step, :] = (product[:BANDS, :] + product[BANDS:, :]).T
 
 
-def join_kernel(a_ref, b_ref, out_ref):
-    rows = a_ref.shape[0]
-    out_ref[0:rows, :] = a_ref[...]
-    out_ref[rows:, :] = b_ref[...]
-
-
-def join(a, b):
-    rows, lanes = a.shape
-    return call(join_kernel, shape(2 * rows, lanes), 2, 0, 16 * a.size)(a, b)
-
-
 def add_kernel(side, near_ref, across_ref, *rest):
     total = near_ref[0] + across_ref[side]
     for ref in rest[:-1]:
@@ -203,15 +198,18 @@
 
 
 def derive_kernel(
-    parts_ref, powers_ref, sender_ref, heard_ref, quality_ref, own_ref, pressure_ref
+    place_ref, parts_ref, listener_ref, weight_ref, fair_ref, quality_ref, own_ref, pressure_ref
 ):
     interference = add_blocks(parts_ref, NXY)
-    powers = powers_ref[...]
-    dx = heard_ref[0:1, 0:BLOCK] - sender_ref[0:1, :].astype(F32)
-    dy = heard_ref[1:2, 0:BLOCK] - sender_ref[1:2, :].astype(F32)
+    z2, z1, zhi, core = (place_ref[i] for i in range(3, 7))
+    source = (zhi * 2 + core) * 4 + z2 * 2 + z1
+    powers = parts_ref[source, BLOCK : 2 * BLOCK, :]
+    sender = -0.5 * parts_ref[source, 2 * BLOCK :, :]
+    dx = listener_ref[0:1, :].astype(F32) - sender[0:1, 0:BLOCK]
+    dy = listener_ref[1:2, :].astype(F32) - sender[1:2, 0:BLOCK]
     own_gain = 1.0 / (1.0 + dx * dx + dy * dy)
-    weight = WEIGHT_UNIT * heard_ref[0:1, BLOCK:]
-    fair = heard_ref[1:2, BLOCK:]
+    weight = WEIGHT_UNIT * weight_ref[...].astype(F32)
+    fair = fair_ref[...].astype(F32)
     rows = jnp.concatenate([own_gain, weight, fair, jnp.zeros((5, BLOCK), F32)], axis=0)
     rows = jnp.concatenate([rows, jnp.zeros_like(rows)], axis=1)
     columns = jnp.concatenate([rows, jnp.zeros((120, 128), F32)], axis=0).T
@@ -249,23 +247,15 @@
 def per_device(sender_xy, listener_xy, powers, weight, fairness, step_code):
     place = jnp.stack([lax.axis_index(name).astype(jnp.int32) for name in PLACE])
     to_sender = [(b, (b % 32) * 16 + b // 32) for b in range(512)]
-    to_receiver = [(s, b) for b, s in to_sender]
     swap = [(0, 1), (1, 0)]
     block, blocks = shape(BLOCK, BANDS), shape(NXY, BLOCK, BANDS)
 
-    rows = [listener_xy, weight[None], fairness[None]]
-    heard = call(hear_kernel, shape(8, 128), 1)(jnp.concatenate(rows, axis=0))
-    heard = lax.ppermute(heard, AXES, to_sender)
-    sent = call(pack_kernel, shape(NZ, SENT, BANDS), 2)(sender_xy, powers)
-    heard, sent = lax.optimization_barrier((heard, sent))
-    mine = heard
-    near = lax.all_to_all(sent, Z, 0, 0)
-    for axis in XY:
-        for bit in (1, 2):
-            other = lax.ppermute(heard, axis, [(i, i ^ bit) for i in range(4)])
-            heard = join(heard, other)
-    near, heard = lax.optimization_barrier((near, heard))
-    listeners = heard.reshape(NXY, 8, 128)
+    sent, heard = call(pack_kernel, (shape(SENT, BANDS), shape(NXY, 8, 128)), 2)(
+        jnp.concatenate([sender_xy, listener_xy], axis=0), powers
+    )
+    near = lax.all_gather(sent, Z, axis=0)
+    listeners = lax.all_to_all(heard, XY, 0, 0)
+    near, listeners = lax.optimization_barrier((near, listeners))
     far = lax.ppermute(near, "core", swap)
 
     gains = shape(2, ROWS, WIDE, dtype=BF16)
@@ -275,12 +265,16 @@
         lambda *refs: interfere_kernel(True, *refs), outs, 3, smem=(0,), **work
     )(place, near, listeners)
     part, far_high, far_low = call(
-        lambda *refs: interfere_kernel(False, *refs), outs, 4, smem=(0,), **work
-    )(place, far, listeners, part)
-
-    parts = lax.all_to_all(part.reshape(NXY, BLOCK, BANDS), XY, 0, 0)
-    quality, own, pressure = call(derive_kernel, (block, block, blocks), 4)(
-        parts, powers, sender_xy, mine
+        lambda *refs: interfere_kernel(False, *refs),
+        (shape(NXY, BLOCK + SENT, BANDS), gains, gains),
+        5,
+        smem=(0,),
+        **work,
+    )(place, far, listeners, near, part)
+
+    parts = lax.all_to_all(part, XY, 0, 0)
+    quality, own, pressure = call(derive_kernel, (block, block, blocks), 5, smem=(0,))(
+        place, parts, listener_xy, weight[None], fairness[None]
     )
     pressures = lax.all_to_all(pressure, XY, 0, 0)
     both = call(turn_kernel, shape(2 * BANDS, ROWS, dtype=BF16), 1)(pressures)
@@ -297,7 +291,7 @@
     passed = add(1, react(near_high, near_low, 1), across)
     passed = lax.ppermute(passed, "z0", swap)
     pushed = add(0, react(near_high, near_low, 0), across, passed)
-    quality = lax.ppermute(quality, AXES, to_receiver)
+    own = lax.ppermute(own, AXES, to_sender)
     parts = lax.all_to_all(pushed.reshape(NZ // 2, BLOCK, BANDS), EVEN, 0, 0)
     gradient, new_power, gap = call(
         finish_kernel, (block, block, shape(2 * NZ, 1, BANDS)), 4, smem=(0,)

time: 183 us -> 178 us (0.973)
  blocking collectives: 28.5 us -> 102 us
  starting transfers between devices: 72.7 us -> 33.8 us
  waiting for transfers between devices: 58.2 us -> 20.1 us
    all_to_all x1 -> x3, blocking collectives: 15.3 us -> 58.2 us  [the longest x1 24.3 us: per_device(): parts = lax.all_to_all(part, XY, 0, 0)]
    all_gather x0 -> x1, blocking collectives: none -> 32.1 us  [per_device(): near = lax.all_gather(sent, Z, axis=0)]
    all_to_all x3 -> x1, starting transfers between devices: 36.9 us -> 7.58 us  [per_device(): listeners = lax.all_to_all(heard, XY, 0, 0)]
    all_to_all x3 -> x1, waiting for transfers between devices: 23.6 us -> 0.01 us  [per_device(): listeners = lax.all_to_all(heard, XY, 0, 0)]
    ppermute x6 -> x1, starting transfers between devices: 17 us -> 2.7 us  [per_device(): own = lax.ppermute(own, AXES, to_sender)]
    ppermute x6 -> x1, waiting for transfers between devices: 12.6 us -> 3.37 us  [per_device(): own = lax.ppermute(own, AXES, to_sender)]
    ppermute x1, starting transfers between devices: 1.91 us -> 9.7 us  [per_device(): far = lax.ppermute(near, 'core', swap)]
    all_to_all x1, waiting for transfers between devices: 16.4 us -> 10.4 us  [per_device(): parts = lax.all_to_all(pushed.reshape(NZ // 2, BLOCK, BANDS), EVEN, 0, 0)]
  transfers between devices with their start and end apart: 13 -> 6, of which waited for: 11 -> 4; matrix products, arithmetic and copies ran while one was open for 0% -> 0% of each run, Pallas kernels for 4% -> 3%
where the time goes in v6:
time: 178 us; the launch traced here: 177 us
  blocking collectives  102 us (57%)
  starting transfers between devices  33.8 us (19%)
  waiting for transfers between devices  20.1 us (11%)
  Pallas kernels  15.3 us (9%)
  between operations  3.21 us (2%)
    all_gather x1, blocking collectives, per_device(): near = lax.all_gather(sent, Z, axis=0)  32.1 us
    all_to_all x1, blocking collectives, per_device(): parts = lax.all_to_all(part, XY, 0, 0)  24.3 us
    all_to_all x1, blocking collectives, per_device(): gap = lax.all_to_all(gap, (*Z, 'core'), 0, 0)  22.8 us
    all_to_all x1, blocking collectives, per_device(): pressures = lax.all_to_all(pressure, XY, 0, 0)  12.1 us
    all_to_all x1, blocking collectives, per_device(): gap = lax.all_to_all(gap, XY, 0, 0)  11.1 us
    all_to_all x1, waiting for transfers between devices, per_device(): parts = lax.all_to_all(pushed.reshape(NZ // 2, BLOCK, BANDS), EVEN, 0, 0)  10.4 us
    ppermute x1, starting transfers between devices, per_device(): far = lax.ppermute(near, 'core', swap)  9.7 us
    all_to_all x1, starting transfers between devices, per_device(): listeners = lax.all_to_all(heard, XY, 0, 0)  7.58 us
  transfers between devices with their start and end apart: 6, of which 4 were waited for; matrix products, arithmetic and copies ran while one was open for 0% of the time, Pallas kernels for 3%

profile of v6, /device:TPU:1, one launch (start us, length us, event | category | flops | bytes accessed | tf_op | source)
XLA Modules:
  0.0 177.0 jit_solution(17013456646344267785)
XLA Ops:
  0.6 0.7 pad_add_fusion.info_ref
  1.3 0.0 copy-start
  1.3 0.8 copy-done
  2.1 0.6 shard_map.93
  2.7 7.6 %all-to-all-start = ((f32[16,8,128]{2,1,0:T(8,128)}), f32[16,8,128]{2,1,0:T(8,128)S(1)}, u32[]{:S(2)}, u32[]{:S(2)}) async-start(f32[16,8,128]{2,1,0:T(8,128)} %get-tuple-element.21), calls=%async_computation | async-start | bytes 131072 | tf_op jit(solution)/shard_map/all_to_all | solution.py:257
  10.3 32.1 %all-gather = f32[1152,128]{1,0:T(8,128)S(1)} all-gather(f32[72,128]{1,0:T(8,128)S(1)} %get-tuple-element.20), channel_id=2, replica_groups=mesh['z2'=2,'z1'=2,'z0'=2,'x'=4,'y'=4,'zhi'=2,'core'=2] {'zhi','z2','z1'..., dimensions={0}, use_global_device_ids=true | all-gather | bytes 626688 | tf_op jit(solution)/shard_map/all_gather | solution.py:256
  42.4 0.0 all-to-all-done.refs_2_
  42.4 9.7 %collective-permute-start = (f32[16,72,128]{2,1,0:T(8,128)S(1)}, f32[16,72,128]{2,1,0:T(8,128)S(1)}, u32[]{:S(2)}, u32[]{:S(2)}) collective-permute-start(f32[16,72,128]{2,1,0:T(8,128)S(1)} %bitcast.12), channel_id=1, source_target_pairs={{0,1},{1,0},{2,3},{3,2},{4,5},{5,4},{6,7},{7,6},{8,9},{9,8},{10,11... | collective-permute-start | bytes 1769480 | tf_op jit(solution)/shard_map/ppermute | solution.py:259
  52.1 0.1 stack.31.refs_0_.place_ref
  52.2 3.5 %shard_map.94 = (f32[1024,128]{1,0:T(8,128)S(1)}, bf16[2,1024,512]{2,1,0:T(8,128)(2,1)S(1)}, bf16[2,1024,512]{2,1,0:T(8,128)(2,1)S(1)}) custom-call(s32[7]{0:T(128)S(1)} %stack.31.refs_0_.place_ref, f32[16,72,128]{2,1,0:T(8,128)S(1)} %bitcast.13, f32[16,8,128]{2,1,0:T(8,128)S(1)} %all-to-all-done.refs_2_), custom_call_target="tpu_custom_call" | custom-call | flops 1073741824 | bytes 8388608 | tf_op jit(solution)/shard_map/pallas_call | solution.py:264
  55.7 0.0 collective-permute-done.refs_1_
  55.7 3.6 %shard_map.95 = (f32[16,136,128]{2,1,0:T(8,128)S(1)}, bf16[2,1024,512]{2,1,0:T(8,128)(2,1)S(1)}, bf16[2,1024,512]{2,1,0:T(8,128)(2,1)S(1)}) custom-call(s32[7]{0:T(128)S(1)} %stack.31.refs_0_.place_ref, f32[16,72,128]{2,1,0:T(8,128)S(1)} %collective-permute-done.refs_1_, f32[16,8,128]{2,1,0:T(8,128)S(1)} %all-to-all-done.refs_2_, ...), custom_call_target="tpu_custom_call" | custom-call | flops 1073741824 | bytes 8388608 | tf_op jit(solution)/shard_map/pallas_call | solution.py:267
  59.3 0.0 copy-start.2
  59.3 0.0 copy-start.3
  59.3 0.0 copy-start.4
  59.3 24.3 %all_to_all.30.parts_ref = f32[16,136,128]{2,1,0:T(8,128)S(1)} all-to-all(f32[16,136,128]{2,1,0:T(8,128)S(1)} %get-tuple-element.25), channel_id=1, replica_groups=mesh['z2'=2,'z1'=2,'z0'=2,'x'=4,'y'=4,'zhi'=2,'core'=2] {'x','y'}, dimensions={0} | all-to-all | bytes 2228224 | tf_op jit(solution)/shard_map/all_to_all | solution.py:275
  83.6 0.0 copy-done.2
  83.6 0.0 copy-done.3
  83.7 0.0 copy-done.4
  83.7 1.3 shard_map.96
  85.0 12.1 %all_to_all.31.pressure_ref = f32[16,64,128]{2,1,0:T(8,128)S(1)} all-to-all(f32[16,64,128]{2,1,0:T(8,128)S(1)} %get-tuple-element.27), channel_id=1, replica_groups=mesh['z2'=2,'z1'=2,'z0'=2,'x'=4,'y'=4,'zhi'=2,'core'=2] {'x','y'}, dimensions={0} | all-to-all | bytes 1048576 | tf_op jit(solution)/shard_map/all_to_all | solution.py:279
  97.1 0.2 shard_map.97.refs_1_
  97.3 1.9 %shard_map.99 = f32[2,512,128]{2,1,0:T(8,128)S(1)} custom-call(s32[7]{0:T(128)S(1)} %stack.31.refs_0_.place_ref, bf16[256,1024]{1,0:T(8,128)(2,1)S(1)} %shard_map.97.refs_1_, bf16[2,1024,512]{2,1,0:T(8,128)(2,1)S(1)} %get-tuple-element.30.refs_2_, bf16[2,1024,512]{2,1,0:T(8,128)(2,1)S(1)} %get-tuple-element.31.refs_3_), custom_call_target="tpu_custom_call" | custom-call | flops 1073741824 | bytes 4194304 | tf_op jit(solution)/shard_map/pallas_call | solution.py:288
  99.2 5.4 %collective-permute-start.1 = (f32[2,512,128]{2,1,0:T(8,128)S(1)}, f32[2,512,128]{2,1,0:T(8,128)S(1)}, u32[]{:S(2)}, u32[]{:S(2)}) collective-permute-start(f32[2,512,128]{2,1,0:T(8,128)S(1)} %shard_map.99), channel_id=1, source_target_pairs={{0,1},{1,0},{2,3},{3,2},{4,5},{5,4},{6,7},{7,6},{8,9},{9,8},{10,11... | collective-permute-start | bytes 1572872 | tf_op jit(solution)/shard_map/ppermute | solution.py:290
  104.6 1.3 shard_map.100.refs_0_
  106.0 0.2 collective-permute-done.1.refs_1_
  106.2 0.0 copy-start.1
  106.2 1.9 %collective-permute-start.2 = (f32[512,128]{1,0:T(8,128)S(1)}, f32[512,128]{1,0:T(8,128)S(1)}, u32[]{:S(2)}, u32[]{:S(2)}) collective-permute-start(f32[512,128]{1,0:T(8,128)S(1)} %shard_map.101), channel_id=1, source_target_pairs={{0,64},{64,0},{1,65},{65,1},{2,66},{66,2},{3,67},{67,3},{4,68},{68... | collective-permute-start | bytes 786440 | tf_op jit(solution)/shard_map/ppermute | solution.py:292
  108.1 1.3 shard_map.98.refs_0_
  109.5 6.1 %collective-permute-done.2.refs_2_ = f32[512,128]{1,0:T(8,128)S(1)} collective-permute-done((f32[512,128]{1,0:T(8,128)S(1)}, f32[512,128]{1,0:T(8,128)S(1)}, u32[]{:S(2)}, u32[]{:S(2)}) %collective-permute-start.2) | collective-permute-done | bytes 262176 | tf_op jit(solution)/shard_map/ppermute | solution.py:292
  115.6 0.7 shard_map.102
  116.3 6.6 %all-to-all-start.3 = ((f32[8,64,128]{2,1,0:T(8,128)}), f32[8,64,128]{2,1,0:T(8,128)S(1)}, u32[]{:S(2)}, u32[]{:S(2)}) async-start(f32[8,64,128]{2,1,0:T(8,128)} %bitcast.10), calls=%async_computation.3 | async-start | bytes 524288 | tf_op jit(solution)/shard_map/all_to_all | solution.py:295
  122.9 2.7 %collective-permute-start.3 = (f32[64,128]{1,0:T(8,128)S(1)}, f32[64,128]{1,0:T(8,128)S(1)}, u32[]{:S(2)}, u32[]{:S(2)}) collective-permute-start(f32[64,128]{1,0:T(8,128)S(1)} %get-tuple-element.32), channel_id=1, source_target_pairs={{0,0},{1,16},{2,32},{3,48},{4,64},{5,80},{6,96},{7,112},{8,128},{9... | collective-permute-start | bytes 98312 | tf_op jit(solution)/shard_map/ppermute | solution.py:294
  126.2 3.4 %collective-permute-done.3.own_ref = f32[64,128]{1,0:T(8,128)S(1)} collective-permute-done((f32[64,128]{1,0:T(8,128)S(1)}, f32[64,128]{1,0:T(8,128)S(1)}, u32[]{:S(2)}, u32[]{:S(2)}) %collective-permute-start.3) | collective-permute-done | bytes 32800 | tf_op jit(solution)/shard_map/ppermute | solution.py:294
  129.6 10.4 %all-to-all-done.3.parts_ref = f32[8,64,128]{2,1,0:T(8,128)S(1)} async-done(((f32[8,64,128]{2,1,0:T(8,128)}), f32[8,64,128]{2,1,0:T(8,128)S(1)}, u32[]{:S(2)}, u32[]{:S(2)}) %all-to-all-start.3) | async-done | bytes 262176 | tf_op jit(solution)/shard_map/all_to_all | solution.py:295
  140.0 0.0 copy-done.1
  140.1 0.7 shard_map.103
  140.7 22.8 %all_to_all.32.parts_ref = f32[32,1,128]{2,1,0:T(1,128)S(1)} all-to-all(f32[32,1,128]{2,1,0:T(1,128)S(1)} %get-tuple-element.35), channel_id=1, replica_groups=mesh['z2'=2,'z1'=2,'z0'=2,'x'=4,'y'=4,'zhi'=2,'core'=2] {'zhi','z2','z1'..., dimensions={0} | all-to-all | bytes 32768 | tf_op jit(solution)/shard_map/all_to_all | solution.py:299
  163.5 11.1 %all_to_all.33 = f32[16,1,128]{2,1,0:T(1,128)S(1)} all-to-all(f32[16,1,128]{2,1,0:T(1,128)S(1)} %shard_map.104), channel_id=1, replica_groups=mesh['z2'=2,'z1'=2,'z0'=2,'x'=4,'y'=4,'zhi'=2,'core'=2] {'x','y'}, dimensions={0} | all-to-all | bytes 16384 | tf_op jit(solution)/shard_map/all_to_all | solution.py:301
  174.6 0.6 reduce_sum.9
  (2 shorter events, 0.1 us)
Async XLA Ops:
  1.3 0.8 copy-start
  2.7 39.7 %all-to-all-start = ((f32[16,8,128]{2,1,0:T(8,128)}), f32[16,8,128]{2,1,0:T(8,128)S(1)}, u32[]{:S(2)}, u32[]{:S(2)}) async-start(f32[16,8,128]{2,1,0:T(8,128)} %get-tuple-element.21), calls=%async_computation | async-start | bytes 131072 | tf_op jit(solution)/shard_map/all_to_all | solution.py:257
  42.4 13.3 %collective-permute-start = (f32[16,72,128]{2,1,0:T(8,128)S(1)}, f32[16,72,128]{2,1,0:T(8,128)S(1)}, u32[]{:S(2)}, u32[]{:S(2)}) collective-permute-start(f32[16,72,128]{2,1,0:T(8,128)S(1)} %bitcast.12), channel_id=1, source_target_pairs={{0,1},{1,0},{2,3},{3,2},{4,5},{5,4},{6,7},{7,6},{8,9},{9,8},{10,11... | collective-permute-start | bytes 1769480 | tf_op jit(solution)/shard_map/ppermute | solution.py:259
  59.3 24.3 %copy-start.2 = (s32[2,64]{1,0:T(2,128)S(1)}, s32[2,64]{1,0:T(2,128)}, u32[]{:S(2)}) copy-start(s32[2,64]{1,0:T(2,128)} %listener_ref.1) | copy-start | bytes 1540
  59.3 24.3 %copy-start.3 = (s32[64]{0:T(128)S(1)}, s32[64]{0:T(128)}, u32[]{:S(2)}) copy-start(s32[64]{0:T(128)} %param.9) | copy-start | bytes 772
  59.3 24.3 %copy-start.4 = (s32[64]{0:T(128)S(1)}, s32[64]{0:T(128)}, u32[]{:S(2)}) copy-start(s32[64]{0:T(128)} %param.10) | copy-start | bytes 772
  99.2 6.9 %collective-permute-start.1 = (f32[2,512,128]{2,1,0:T(8,128)S(1)}, f32[2,512,128]{2,1,0:T(8,128)S(1)}, u32[]{:S(2)}, u32[]{:S(2)}) collective-permute-start(f32[2,512,128]{2,1,0:T(8,128)S(1)} %shard_map.99), channel_id=1, source_target_pairs={{0,1},{1,0},{2,3},{3,2},{4,5},{5,4},{6,7},{7,6},{8,9},{9,8},{10,11... | collective-permute-start | bytes 1572872 | tf_op jit(solution)/shard_map/ppermute | solution.py:290
  106.2 33.9 %copy-start.1 = (f32[64,128]{1,0:T(8,128)S(1)}, f32[64,128]{1,0:T(8,128)}, u32[]{:S(2)}) copy-start(f32[64,128]{1,0:T(8,128)} %powers_ref.3) | copy-start | bytes 98308
  106.2 9.4 %collective-permute-start.2 = (f32[512,128]{1,0:T(8,128)S(1)}, f32[512,128]{1,0:T(8,128)S(1)}, u32[]{:S(2)}, u32[]{:S(2)}) collective-permute-start(f32[512,128]{1,0:T(8,128)S(1)} %shard_map.101), channel_id=1, source_target_pairs={{0,64},{64,0},{1,65},{65,1},{2,66},{66,2},{3,67},{67,3},{4,68},{68... | collective-permute-start | bytes 786440 | tf_op jit(solution)/shard_map/ppermute | solution.py:292
  116.3 23.7 %all-to-all-start.3 = ((f32[8,64,128]{2,1,0:T(8,128)}), f32[8,64,128]{2,1,0:T(8,128)S(1)}, u32[]{:S(2)}, u32[]{:S(2)}) async-start(f32[8,64,128]{2,1,0:T(8,128)} %bitcast.10), calls=%async_computation.3 | async-start | bytes 524288 | tf_op jit(solution)/shard_map/all_to_all | solution.py:295
  122.9 6.7 %collective-permute-start.3 = (f32[64,128]{1,0:T(8,128)S(1)}, f32[64,128]{1,0:T(8,128)S(1)}, u32[]{:S(2)}, u32[]{:S(2)}) collective-permute-start(f32[64,128]{1,0:T(8,128)S(1)} %get-tuple-element.32), channel_id=1, source_target_pairs={{0,0},{1,16},{2,32},{3,48},{4,64},{5,80},{6,96},{7,112},{8,128},{9... | collective-permute-start | bytes 98312 | tf_op jit(solution)/shard_map/ppermute | solution.py:294

commit v7 on v5

v7 whole, which is shorter than its diff:
```python
import jax
import jax.numpy as jnp
from jax import lax
from jax.experimental import pallas as pl
from jax.experimental.pallas import tpu as pltpu
from jax.sharding import Mesh
from jax.sharding import PartitionSpec as P

NOISE_POWER = 0.05
ARRAY_GAIN = 32.0
WEIGHT_UNIT = 1.0 / 16.0
PEAK_POWER = 1.0

AXES = ("z2", "z1", "z0", "x", "y", "zhi", "core")
SIZES = (2, 2, 2, 4, 4, 2, 2)
Z = ("zhi", "z2", "z1", "z0")
XY = ("x", "y")
PLACE = ("x", "y", "z0", "z2", "z1", "zhi", "core")
NZ, NXY = 16, 16
BLOCK, BANDS = 64, 128
SENT = BLOCK + 8
HALF = NZ * BLOCK
ROWS = NXY * BLOCK
USERS = 32768
VMEM_LIMIT = 20 * 1024 * 1024
F32, BF16 = jnp.float32, jnp.bfloat16


def whole():
    return pl.BlockSpec(memory_space=pltpu.VMEM)


def call(kernel, outs, n_in, flops=0, bytes_accessed=1 << 20, smem=()):
    def spec(i):
        return pl.BlockSpec(memory_space=pltpu.SMEM) if i in smem else whole()

    many = isinstance(outs, (list, tuple))
    return pl.pallas_call(
        kernel,
        out_shape=outs,
        in_specs=[spec(i) for i in range(n_in)],
        out_specs=[whole() for _ in outs] if many else whole(),
        compiler_params=pltpu.CompilerParams(vmem_limit_bytes=VMEM_LIMIT),
        cost_estimate=pl.CostEstimate(flops=flops, bytes_accessed=bytes_accessed, transcendentals=0),
    )


def shape(*dims, dtype=F32):
    return jax.ShapeDtypeStruct(dims, dtype)


def split_norm(norm):
    low = norm & 511
    odd = low & 1
    return norm - low, low - odd, odd


def hear_kernel(info_ref, heard_ref):
    lx, ly = info_ref[0:1, :], info_ref[1:2, :]
    one = jnp.ones_like(lx)
    l1, l2, l3 = split_norm(lx * lx + ly * ly + 1)
    heard = jnp.concatenate([lx, ly, l1, l2, l3, one, one, one], axis=0).astype(F32)
    user = jnp.concatenate([info_ref[2:4, :].astype(F32), jnp.zeros((6, BLOCK), F32)], axis=0)
    heard_ref[...] = jnp.concatenate([heard, user], axis=1)


def pack_kernel(sender_ref, powers_ref, sent_ref):
    sx, sy = sender_ref[0:1, :], sender_ref[1:2, :]
    one = jnp.ones_like(sx)
    s1, s2, s3 = split_norm(sx * sx + sy * sy)
    sent = jnp.concatenate([-2 * sx, -2 * sy, one, one, one, s1, s2, s3], axis=0).astype(F32)
    sent_ref[0:BLOCK, :] = powers_ref[...]
    sent_ref[BLOCK:, :] = jnp.concatenate([sent, jnp.zeros_like(sent)], axis=1)


def plane_kernel(heard_ref, sent_ref, plane_ref):
    both = jnp.concatenate([heard_ref[:, 0:BLOCK], sent_ref[BLOCK:, 0:BLOCK]], axis=1)
    for k in range(NXY):
        plane_ref[k] = both


def spread(parts, row, lane):
    pieces = []
    for k in range(0, 16, 2):
        left = parts[k, row : row + 8, lane : lane + BLOCK]
        right = parts[k + 1, row : row + 8, lane : lane + BLOCK]
        pieces.append(jnp.concatenate([left, right], axis=1))
    features = jnp.concatenate(pieces, axis=1)
    return jnp.concatenate([features, jnp.zeros_like(features)], axis=0).astype(BF16)


def split(value):
    high = value.astype(BF16)
    low = (value - high.astype(F32)).astype(BF16)
    return high, low


def gain_kernel(far, lane, place_ref, plane_ref, column_ref, *rest):
    *before, total_ref = rest
    x, y, z0, z2, z1, zhi, core = (place_ref[i] for i in range(7))
    rows = spread(plane_ref, 0, lane)
    columns = spread(column_ref, BLOCK, 0)
    value_high, value_low = split(column_ref[:, 0:BLOCK, :].reshape(HALF, BANDS))
    values = jnp.concatenate([value_high, value_low], axis=1)
    values = jnp.concatenate([values, values], axis=0)
    row_base = zhi * 4096 + core * 2048 + (z2 * 4 + z1 * 2 + z0) * 256
    col_base = y * 8192 + (1 - core if far else core) * 2048 + x * 64
    tile = 128
    for r in range(0, ROWS, tile):
        row = lax.broadcasted_iota(jnp.int32, (tile, tile), 0) + r
        block = row >> 6
        row_id = row_base + (block & 3) * 8192 + (block >> 2) * 64 + (row & 63)
        highs, lows = [], []
        for c in range(0, HALF, tile):
            col = lax.broadcasted_iota(jnp.int32, (1, tile), 1) + c
            zed = col >> 6
            col_id = col_base + (zed >> 3) * 4096 + (zed & 7) * 256 + (col & 63)
            square = lax.dot_general(
                rows[:, r : r + tile],
                columns[:, c : c + tile],
                (((0,), (0,)), ((), ())),
                preferred_element_type=F32,
            )
            guess = pl.reciprocal(square, approx=True)
            gain = guess * (2.0 - square * guess)
            gain = jnp.where(row_id == col_id, 0.0, gain)
            high, low = split(gain)
            highs.append(high)
            lows.append(low)
        gains = jnp.concatenate(highs + lows, axis=1)
        product = jnp.dot(gains, values, preferred_element_type=F32)
        part = product[:, :BANDS] + product[:, BANDS:]
        for ref in before:
            part = part + ref[r : r + tile, :]
        total_ref[r : r + tile, :] = part


def add_blocks(ref):
    total = ref[0]
    for k in range(1, NXY):
        total = total + ref[k]
    return total


def derive_kernel(parts_ref, powers_ref, sent_ref, heard_ref, quality_ref, own_ref, column_ref):
    interference = add_blocks(parts_ref)
    dx = heard_ref[0:1, 0:BLOCK] + 0.5 * sent_ref[BLOCK : BLOCK + 1, 0:BLOCK]
    dy = heard_ref[1:2, 0:BLOCK] + 0.5 * sent_ref[BLOCK + 1 : BLOCK + 2, 0:BLOCK]
    own_gain = 1.0 / (1.0 + dx * dx + dy * dy)
    weight = WEIGHT_UNIT * heard_ref[0:1, BLOCK:]
    fair = heard_ref[1:2, BLOCK:]
    rows = jnp.concatenate([own_gain, weight, fair, jnp.zeros((5, BLOCK), F32)], axis=0)
    rows = jnp.concatenate([rows, jnp.zeros_like(rows)], axis=1)
    columns = jnp.concatenate([rows, jnp.zeros((120, 128), F32)], axis=0).T
    own_gain = columns[0:BLOCK, 0:1]
    weight = columns[0:BLOCK, 1:2]
    fair = columns[0:BLOCK, 2:3]
    signal = ARRAY_GAIN * own_gain * powers_ref[...]
    denominator = NOISE_POWER + interference
    quality = signal / denominator
    marginal = weight * jnp.exp(-fair * jnp.log(quality)) / denominator
    quality_ref[...] = quality
    own_ref[...] = ARRAY_GAIN * own_gain * marginal
    column_ref[0:BLOCK, :] = marginal * quality
    column_ref[BLOCK:, :] = heard_ref[...]


def finish_kernel(step_ref, parts_ref, own_ref, powers_ref, gradient_ref, power_ref, gap_ref):
    gradient = own_ref[...] - add_blocks(parts_ref)
    powers = powers_ref[...]
    target = PEAK_POWER * jax.nn.sigmoid(gradient)
    step_size = step_ref[0].astype(F32) / 4096.0
    gradient_ref[...] = gradient
    power_ref[...] = powers + step_size * (target - powers)
    gap = PEAK_POWER * jnp.maximum(gradient, 0.0) - gradient * powers
    gap = jnp.sum(gap, axis=0, keepdims=True)
    for k in range(2 * NZ):
        gap_ref[k] = gap


def fold_kernel(parts_ref, out_ref):
    total = jnp.sum(parts_ref[...], axis=0)
    for k in range(NXY):
        out_ref[k] = total


def per_device(sender_xy, listener_xy, powers, weight, fairness, step_code):
    place = jnp.stack([lax.axis_index(name).astype(jnp.int32) for name in PLACE])
    to_sender = [(b, (b % 32) * 16 + b // 32) for b in range(512)]
    to_receiver = [(s, b) for b, s in to_sender]
    swap = [(0, 1), (1, 0)]
    block, product = shape(BLOCK, BANDS), shape(ROWS, BANDS)
    work = dict(flops=2 * ROWS * HALF * 512, bytes_accessed=1 << 22)

    def gain_product(far, lane, *args):
        def kernel(*refs):
            gain_kernel(far, lane, *refs)

        return call(kernel, product, 1 + len(args), smem=(0,), **work)(place, *args)

    def spread_sum(near, far, plane, lane):
        part = gain_product(False, lane, plane, near)
        part = gain_product(True, lane, plane, far, part)
        return lax.all_to_all(part.reshape(NXY, BLOCK, BANDS), XY, 0, 0)

    info = jnp.concatenate([listener_xy, weight[None], fairness[None]], axis=0)
    heard = call(hear_kernel, shape(8, 128), 1)(info)
    heard = lax.ppermute(heard, AXES, to_sender)
    sent = call(pack_kernel, shape(SENT, BANDS), 2)(sender_xy, powers)
    near = lax.all_gather(sent, Z, axis=0)
    near, heard = lax.optimization_barrier((near, heard))
    far = lax.ppermute(near, "core", swap)
    plane = call(plane_kernel, shape(NXY, 8, 128), 2)(heard, sent)
    plane = lax.all_to_all(plane, XY, 0, 0)
    parts = spread_sum(near, far, plane, 0)
    quality, own, column = call(derive_kernel, (block, block, shape(SENT, BANDS)), 4)(
        parts, powers, sent, heard
    )

    near = lax.all_gather(column, Z, axis=0)
    far = lax.ppermute(near, "core", swap)
    parts = spread_sum(near, far, plane, BLOCK)
    gradient, new_power, gap = call(
        finish_kernel, (block, block, shape(2 * NZ, 1, BANDS)), 4, smem=(0,)
    )(step_code, parts, own, powers)

    quality = lax.ppermute(quality, AXES, to_receiver)
    gap = lax.all_to_all(gap, (*Z, "core"), 0, 0)
    gap = call(fold_kernel, shape(NXY, 1, BANDS), 1)(gap)
    gap = lax.all_to_all(gap, XY, 0, 0)
    return quality, gradient, new_power, (jnp.sum(gap) / (USERS * BANDS)).reshape(1)


def solution(mesh):
    fine = Mesh(mesh.devices.reshape(SIZES), AXES)
    rx, tx = ("z2", "z1", "z0", "x"), ("y", "zhi", "core")
    by_sender, by_receiver = (*tx, *rx), (*rx, *tx)
    return jax.shard_map(
        per_device,
        mesh=fine,
        in_specs=(
            P(None, by_sender),
            P(None, by_receiver),
            P(by_sender, None),
            P(by_receiver),
            P(by_receiver),
            P(),
        ),
        out_specs=(P(by_receiver, None), P(by_sender, None), P(by_sender, None), P()),
        check_vma=False,
    )
```

time: 183 us -> 176 us (0.962)
  blocking collectives: 28.5 us -> 75.6 us
  waiting for transfers between devices: 58.2 us -> 31.4 us
  starting transfers between devices: 72.7 us -> 46.5 us
    all_gather x0 -> x2, blocking collectives: none -> 63.4 us  [the longest x1 40.2 us: per_device(): near = lax.all_gather(sent, Z, axis=0)]
    all_to_all x2, starting transfers between devices: 34 us -> 7.07 us  [the longest x1 3.57 us: spread_sum(): return lax.all_to_all(part.reshape(NXY, BLOCK, BANDS), XY, 0, 0)]
    ppermute x1 -> x2, starting transfers between devices: 1.91 us -> 20.9 us  [per_device(): far = lax.ppermute(near, 'core', swap)]
    ppermute x6 -> x0, waiting for transfers between devices: 17.8 us -> none  [the longest x4 12.1 us: per_device(): other = lax.ppermute(heard, axis, [(i, i ^ bit) for i in range(4)])]
    ppermute x6 -> x0, starting transfers between devices: 17.5 us -> none  [the longest x4 9.6 us: per_device(): other = lax.ppermute(heard, axis, [(i, i ^ bit) for i in range(4)])]
    all_to_all x2 -> x1, blocking collectives: 28.5 us -> 12.1 us  [spread_sum(): return lax.all_to_all(part.reshape(NXY, BLOCK, BANDS), XY, 0, 0)]
    all_to_all x2, waiting for transfers between devices: 24.9 us -> 16.2 us  [the longest x1 9.86 us: spread_sum(): return lax.all_to_all(part.reshape(NXY, BLOCK, BANDS), XY, 0, 0)]
    pallas_call x15 -> x8, Pallas kernels: 13.8 us -> 14.2 us  [the longest x4 13.1 us: gain_product(): return call(kernel, product, 1 + len(args), smem=(0,), **work)(place, *args)]
  transfers between devices with their start and end apart: 13 -> 8, of which waited for: 11 -> 4; matrix products, arithmetic and copies ran while one was open for 0% -> 0% of each run, Pallas kernels for 4% -> 4%
where the time goes in v7:
time: 176 us; the launch traced here: 175 us
  blocking collectives  75.6 us (43%)
  starting transfers between devices  46.5 us (26%)
  waiting for transfers between devices  31.4 us (18%)
  Pallas kernels  15.5 us (9%)
  between operations  3.26 us (2%)
  local copies, waits for them, and re-layouts  2.14 us (1%)
    all_gather x1, blocking collectives, per_device(): near = lax.all_gather(sent, Z, axis=0)  40.2 us
    all_gather x1, blocking collectives, per_device(): near = lax.all_gather(column, Z, axis=0)  23.3 us
    ppermute x2, starting transfers between devices, per_device(): far = lax.ppermute(near, 'core', swap)  20.9 us
    pallas_call x4, Pallas kernels, gain_product(): return call(kernel, product, 1 + len(args), smem=(0,), **work)(place, *args)  13.1 us
    all_to_all x1, blocking collectives, spread_sum(): return lax.all_to_all(part.reshape(NXY, BLOCK, BANDS), XY, 0, 0)  12.1 us
    all_to_all x1, waiting for transfers between devices, spread_sum(): return lax.all_to_all(part.reshape(NXY, BLOCK, BANDS), XY, 0, 0)  9.86 us
    all_to_all x1, waiting for transfers between devices, per_device(): gap = lax.all_to_all(gap, (*Z, 'core'), 0, 0)  8.91 us
    all_to_all x1, starting transfers between devices, per_device(): gap = lax.all_to_all(gap, (*Z, 'core'), 0, 0)  7.77 us
  transfers between devices with their start and end apart: 8, of which 4 were waited for; matrix products, arithmetic and copies ran while one was open for 0% of the time, Pallas kernels for 4%

profile of v7, /device:TPU:1, one launch (start us, length us, event | category | flops | bytes accessed | tf_op | source)
XLA Modules:
  0.0 175.0 jit_solution(16945289712689441963)
XLA Ops:
  0.6 0.0 copy-start.5
  0.6 0.0 copy-start.3
  0.7 0.0 copy-start.4
  0.7 0.6 copy-done.5
  1.3 0.0 copy-done.3
  1.3 0.0 copy-done.4
  1.3 0.0 copy-start.2
  1.4 0.1 shard_map.94
  1.4 4.5 %collective-permute-start = (f32[8,128]{1,0:T(8,128)S(1)}, f32[8,128]{1,0:T(8,128)S(1)}, u32[]{:S(2)}, u32[]{:S(2)}) collective-permute-start(f32[8,128]{1,0:T(8,128)S(1)} %shard_map.94), channel_id=1, source_target_pairs={{0,0},{1,16},{2,32},{3,48},{4,64},{5,80},{6,96},{7,112},{8,128},{9... | collective-permute-start | bytes 12296 | tf_op jit(solution)/shard_map/ppermute | solution.py:208
  5.9 0.0 copy-done.2
  5.9 0.0 copy-start
  6.0 0.7 copy-done
  6.7 40.2 %all-gather = f32[1152,128]{1,0:T(8,128)S(1)} all-gather(f32[72,128]{1,0:T(8,128)S(1)} %shard_map.93.sent_ref), channel_id=2, replica_groups=mesh['z2'=2,'z1'=2,'z0'=2,'x'=4,'y'=4,'zhi'=2,'core'=2] {'zhi','z2','z1'..., dimensions={0}, use_global_device_ids=true | all-gather | bytes 626688 | tf_op jit(solution)/shard_map/all_gather | solution.py:210
  46.9 0.0 collective-permute-done.heard_ref
  46.9 9.4 %collective-permute-start.1 = (f32[16,72,128]{2,1,0:T(8,128)S(1)}, f32[16,72,128]{2,1,0:T(8,128)S(1)}, u32[]{:S(2)}, u32[]{:S(2)}) collective-permute-start(f32[16,72,128]{2,1,0:T(8,128)S(1)} %bitcast.14), channel_id=1, source_target_pairs={{0,1},{1,0},{2,3},{3,2},{4,5},{5,4},{6,7},{7,6},{8,9},{9,8},{10,11... | collective-permute-start | bytes 1769480 | tf_op jit(solution)/shard_map/ppermute | solution.py:212
  56.3 0.7 shard_map.95
  57.0 3.5 %all-to-all-start = ((f32[16,8,128]{2,1,0:T(8,128)}), f32[16,8,128]{2,1,0:T(8,128)S(1)}, u32[]{:S(2)}, u32[]{:S(2)}) async-start(f32[16,8,128]{2,1,0:T(8,128)} %shard_map.95), calls=%async_computation | async-start | bytes 131072 | tf_op jit(solution)/shard_map/all_to_all | solution.py:214
  60.5 0.1 stack.31.refs_0_
  60.6 6.4 %all-to-all-done.refs_1_ = f32[16,8,128]{2,1,0:T(8,128)S(1)} async-done(((f32[16,8,128]{2,1,0:T(8,128)}), f32[16,8,128]{2,1,0:T(8,128)S(1)}, u32[]{:S(2)}, u32[]{:S(2)}) %all-to-all-start) | async-done | bytes 65568 | tf_op jit(solution)/shard_map/all_to_all | solution.py:214
  67.0 3.1 %shard_map.96.refs_3_ = f32[1024,128]{1,0:T(8,128)S(1)} custom-call(s32[7]{0:T(128)S(1)} %stack.31.refs_0_, f32[16,8,128]{2,1,0:T(8,128)S(1)} %all-to-all-done.refs_1_, f32[16,72,128]{2,1,0:T(8,128)S(1)} %bitcast.15), custom_call_target="tpu_custom_call" | custom-call | flops 1073741824 | bytes 4194304 | tf_op jit(solution)/shard_map/pallas_call | solution.py:199
  70.1 0.0 collective-permute-done.1.refs_2_
  70.1 3.1 %shard_map.97 = f32[1024,128]{1,0:T(8,128)S(1)} custom-call(s32[7]{0:T(128)S(1)} %stack.31.refs_0_, f32[16,8,128]{2,1,0:T(8,128)S(1)} %all-to-all-done.refs_1_, f32[16,72,128]{2,1,0:T(8,128)S(1)} %collective-permute-done.1.refs_2_, f32[1024,128]{1,0:T(8,128)S(1)} %shard_map.96.refs_3_), custom_call_target="tpu_custom_call" | custom-call | flops 1073741824 | bytes 4194304 | tf_op jit(solution)/shard_map/pallas_call | solution.py:199
  73.2 0.0 copy-start.1
  73.2 12.1 %all_to_all.25.parts_ref = f32[16,64,128]{2,1,0:T(8,128)S(1)} all-to-all(f32[16,64,128]{2,1,0:T(8,128)S(1)} %bitcast.18), channel_id=1, replica_groups=mesh['z2'=2,'z1'=2,'z0'=2,'x'=4,'y'=4,'zhi'=2,'core'=2] {'x','y'}, dimensions={0} | all-to-all | bytes 1048576 | tf_op jit(solution)/shard_map/all_to_all | solution.py:204
  85.3 0.0 copy-done.1
  85.3 0.3 shard_map.98
  85.6 23.3 %all-gather.1 = f32[1152,128]{1,0:T(8,128)S(1)} all-gather(f32[72,128]{1,0:T(8,128)S(1)} %get-tuple-element.15), channel_id=3, replica_groups=mesh['z2'=2,'z1'=2,'z0'=2,'x'=4,'y'=4,'zhi'=2,'core'=2] {'zhi','z2','z1'..., dimensions={0}, use_global_device_ids=true | all-gather | bytes 626688 | tf_op jit(solution)/shard_map/all_gather | solution.py:220
  108.9 11.5 %collective-permute-start.3 = (f32[16,72,128]{2,1,0:T(8,128)S(1)}, f32[16,72,128]{2,1,0:T(8,128)S(1)}, u32[]{:S(2)}, u32[]{:S(2)}) collective-permute-start(f32[16,72,128]{2,1,0:T(8,128)S(1)} %bitcast.16), channel_id=1, source_target_pairs={{0,1},{1,0},{2,3},{3,2},{4,5},{5,4},{6,7},{7,6},{8,9},{9,8},{10,11... | collective-permute-start | bytes 1769480 | tf_op jit(solution)/shard_map/ppermute | solution.py:221
  120.3 3.1 %shard_map.99.refs_3_ = f32[1024,128]{1,0:T(8,128)S(1)} custom-call(s32[7]{0:T(128)S(1)} %stack.31.refs_0_, f32[16,8,128]{2,1,0:T(8,128)S(1)} %all-to-all-done.refs_1_, f32[16,72,128]{2,1,0:T(8,128)S(1)} %bitcast.17), custom_call_target="tpu_custom_call" | custom-call | flops 1073741824 | bytes 4194304 | tf_op jit(solution)/shard_map/pallas_call | solution.py:199
  123.4 0.0 collective-permute-done.3.refs_2_
  123.4 3.9 %shard_map.100 = f32[1024,128]{1,0:T(8,128)} custom-call(s32[7]{0:T(128)S(1)} %stack.31.refs_0_, f32[16,8,128]{2,1,0:T(8,128)S(1)} %all-to-all-done.refs_1_, f32[16,72,128]{2,1,0:T(8,128)S(1)} %collective-permute-done.3.refs_2_, f32[1024,128]{1,0:T(8,128)S(1)} %shard_map.99.refs_3_), custom_call_target="tpu_custom_call" | custom-call | flops 1073741824 | bytes 4194304 | tf_op jit(solution)/shard_map/pallas_call | solution.py:199
  127.3 3.6 %all-to-all-start.2 = ((f32[16,64,128]{2,1,0:T(8,128)}), f32[16,64,128]{2,1,0:T(8,128)S(1)}, u32[]{:S(2)}, u32[]{:S(2)}) async-start(f32[16,64,128]{2,1,0:T(8,128)} %bitcast.12), calls=%async_computation.2 | async-start | bytes 1048576 | tf_op jit(solution)/shard_map/all_to_all | solution.py:204
  131.5 9.9 %all-to-all-done.2.parts_ref = f32[16,64,128]{2,1,0:T(8,128)S(1)} async-done(((f32[16,64,128]{2,1,0:T(8,128)}), f32[16,64,128]{2,1,0:T(8,128)S(1)}, u32[]{:S(2)}, u32[]{:S(2)}) %all-to-all-start.2) | async-done | bytes 524320 | tf_op jit(solution)/shard_map/all_to_all | solution.py:204
  141.4 0.7 shard_map.101
  142.1 7.8 %all-to-all-start.3 = ((f32[32,1,128]{2,1,0:T(1,128)}), f32[32,1,128]{2,1,0:T(1,128)S(1)}, u32[]{:S(2)}, u32[]{:S(2)}) async-start(f32[32,1,128]{2,1,0:T(1,128)} %get-tuple-element.19), calls=%async_computation.3 | async-start | bytes 32768 | tf_op jit(solution)/shard_map/all_to_all | solution.py:228
  149.8 2.8 %collective-permute-start.2 = (f32[64,128]{1,0:T(8,128)S(1)}, f32[64,128]{1,0:T(8,128)S(1)}, u32[]{:S(2)}, u32[]{:S(2)}) collective-permute-start(f32[64,128]{1,0:T(8,128)S(1)} %get-tuple-element.14), channel_id=1, source_target_pairs={{0,0},{16,1},{32,2},{48,3},{64,4},{80,5},{96,6},{112,7},{128,8},{1... | collective-permute-start | bytes 98312 | tf_op jit(solution)/shard_map/ppermute | solution.py:227
  152.7 8.9 %all-to-all-done.3.parts_ref = f32[32,1,128]{2,1,0:T(1,128)S(1)} async-done(((f32[32,1,128]{2,1,0:T(1,128)}), f32[32,1,128]{2,1,0:T(1,128)S(1)}, u32[]{:S(2)}, u32[]{:S(2)}) %all-to-all-start.3) | async-done | bytes 16416 | tf_op jit(solution)/shard_map/all_to_all | solution.py:228
  161.6 0.6 shard_map.102
  162.2 3.5 %all-to-all-start.4 = ((f32[16,1,128]{2,1,0:T(1,128)}), f32[16,1,128]{2,1,0:T(1,128)S(1)}, u32[]{:S(2)}, u32[]{:S(2)}) async-start(f32[16,1,128]{2,1,0:T(1,128)} %shard_map.102), calls=%async_computation.4 | async-start | bytes 16384 | tf_op jit(solution)/shard_map/all_to_all | solution.py:230
  165.7 0.0 collective-permute-done.2
  165.7 6.3 %all-to-all-done.4 = f32[16,1,128]{2,1,0:T(1,128)S(1)} async-done(((f32[16,1,128]{2,1,0:T(1,128)}), f32[16,1,128]{2,1,0:T(1,128)S(1)}, u32[]{:S(2)}, u32[]{:S(2)}) %all-to-all-start.4) | async-done | bytes 8224 | tf_op jit(solution)/shard_map/all_to_all | solution.py:230
  172.0 0.6 reduce_sum.9
  173.2 0.6 copy.12
  (2 shorter events, 0.0 us)
Async XLA Ops:
  0.6 0.7 copy-start.5
  0.6 0.7 copy-start.3
  0.7 0.7 copy-start.4
  1.3 4.6 %copy-start.2 = (s32[2,64]{1,0:T(2,128)S(1)}, s32[2,64]{1,0:T(2,128)}, u32[]{:S(2)}) copy-start(s32[2,64]{1,0:T(2,128)} %sender_ref.1) | copy-start | bytes 1540
  1.4 45.5 %collective-permute-start = (f32[8,128]{1,0:T(8,128)S(1)}, f32[8,128]{1,0:T(8,128)S(1)}, u32[]{:S(2)}, u32[]{:S(2)}) collective-permute-start(f32[8,128]{1,0:T(8,128)S(1)} %shard_map.94), channel_id=1, source_target_pairs={{0,0},{1,16},{2,32},{3,48},{4,64},{5,80},{6,96},{7,112},{8,128},{9... | collective-permute-start | bytes 12296 | tf_op jit(solution)/shard_map/ppermute | solution.py:208
  5.9 0.8 copy-start
  46.9 23.2 %collective-permute-start.1 = (f32[16,72,128]{2,1,0:T(8,128)S(1)}, f32[16,72,128]{2,1,0:T(8,128)S(1)}, u32[]{:S(2)}, u32[]{:S(2)}) collective-permute-start(f32[16,72,128]{2,1,0:T(8,128)S(1)} %bitcast.14), channel_id=1, source_target_pairs={{0,1},{1,0},{2,3},{3,2},{4,5},{5,4},{6,7},{7,6},{8,9},{9,8},{10,11... | collective-permute-start | bytes 1769480 | tf_op jit(solution)/shard_map/ppermute | solution.py:212
  57.0 10.0 %all-to-all-start = ((f32[16,8,128]{2,1,0:T(8,128)}), f32[16,8,128]{2,1,0:T(8,128)S(1)}, u32[]{:S(2)}, u32[]{:S(2)}) async-start(f32[16,8,128]{2,1,0:T(8,128)} %shard_map.95), calls=%async_computation | async-start | bytes 131072 | tf_op jit(solution)/shard_map/all_to_all | solution.py:214
  73.2 12.1 %copy-start.1 = (f32[64,128]{1,0:T(8,128)S(1)}, f32[64,128]{1,0:T(8,128)}, u32[]{:S(2)}) copy-start(f32[64,128]{1,0:T(8,128)} %powers_ref.5) | copy-start | bytes 98308
  108.9 14.6 %collective-permute-start.3 = (f32[16,72,128]{2,1,0:T(8,128)S(1)}, f32[16,72,128]{2,1,0:T(8,128)S(1)}, u32[]{:S(2)}, u32[]{:S(2)}) collective-permute-start(f32[16,72,128]{2,1,0:T(8,128)S(1)} %bitcast.16), channel_id=1, source_target_pairs={{0,1},{1,0},{2,3},{3,2},{4,5},{5,4},{6,7},{7,6},{8,9},{9,8},{10,11... | collective-permute-start | bytes 1769480 | tf_op jit(solution)/shard_map/ppermute | solution.py:221
  127.3 14.1 %all-to-all-start.2 = ((f32[16,64,128]{2,1,0:T(8,128)}), f32[16,64,128]{2,1,0:T(8,128)S(1)}, u32[]{:S(2)}, u32[]{:S(2)}) async-start(f32[16,64,128]{2,1,0:T(8,128)} %bitcast.12), calls=%async_computation.2 | async-start | bytes 1048576 | tf_op jit(solution)/shard_map/all_to_all | solution.py:204
  142.1 19.5 %all-to-all-start.3 = ((f32[32,1,128]{2,1,0:T(1,128)}), f32[32,1,128]{2,1,0:T(1,128)S(1)}, u32[]{:S(2)}, u32[]{:S(2)}) async-start(f32[32,1,128]{2,1,0:T(1,128)} %get-tuple-element.19), calls=%async_computation.3 | async-start | bytes 32768 | tf_op jit(solution)/shard_map/all_to_all | solution.py:228
  149.8 15.8 %collective-permute-start.2 = (f32[64,128]{1,0:T(8,128)S(1)}, f32[64,128]{1,0:T(8,128)S(1)}, u32[]{:S(2)}, u32[]{:S(2)}) collective-permute-start(f32[64,128]{1,0:T(8,128)S(1)} %get-tuple-element.14), channel_id=1, source_target_pairs={{0,0},{16,1},{32,2},{48,3},{64,4},{80,5},{96,6},{112,7},{128,8},{1... | collective-permute-start | bytes 98312 | tf_op jit(solution)/shard_map/ppermute | solution.py:227
  162.2 9.8 %all-to-all-start.4 = ((f32[16,1,128]{2,1,0:T(1,128)}), f32[16,1,128]{2,1,0:T(1,128)S(1)}, u32[]{:S(2)}, u32[]{:S(2)}) async-start(f32[16,1,128]{2,1,0:T(1,128)} %shard_map.102), calls=%async_computation.4 | async-start | bytes 16384 | tf_op jit(solution)/shard_map/all_to_all | solution.py:230

commit v8 on v7

--- a/solution.py
+++ b/solution.py
@@ -55,35 +55,70 @@
     return norm - low, low - odd, odd
 
 
-def hear_kernel(info_ref, heard_ref):
-    lx, ly = info_ref[0:1, :], info_ref[1:2, :]
+def listener_features(lx, ly):
     one = jnp.ones_like(lx)
     l1, l2, l3 = split_norm(lx * lx + ly * ly + 1)
-    heard = jnp.concatenate([lx, ly, l1, l2, l3, one, one, one], axis=0).astype(F32)
-    user = jnp.concatenate([info_ref[2:4, :].astype(F32), jnp.zeros((6, BLOCK), F32)], axis=0)
-    heard_ref[...] = jnp.concatenate([heard, user], axis=1)
-
-
-def pack_kernel(sender_ref, powers_ref, sent_ref):
-    sx, sy = sender_ref[0:1, :], sender_ref[1:2, :]
+    return jnp.concatenate([lx, ly, l1, l2, l3, one, one, one], axis=0).astype(F32)
+
+
+def sender_features(sx, sy):
     one = jnp.ones_like(sx)
     s1, s2, s3 = split_norm(sx * sx + sy * sy)
-    sent = jnp.concatenate([-2 * sx, -2 * sy, one, one, one, s1, s2, s3], axis=0).astype(F32)
+    return jnp.concatenate([-2 * sx, -2 * sy, one, one, one, s1, s2, s3], axis=0).astype(F32)
+
+
+def pack_kernel(info_ref, powers_ref, sent_ref):
+    sent = sender_features(info_ref[0:1, :], info_ref[1:2, :])
+    user = jnp.concatenate([info_ref[2:6, :].astype(F32), jnp.zeros((4, BLOCK), F32)], axis=0)
     sent_ref[0:BLOCK, :] = powers_ref[...]
-    sent_ref[BLOCK:, :] = jnp.concatenate([sent, jnp.zeros_like(sent)], axis=1)
-
-
-def plane_kernel(heard_ref, sent_ref, plane_ref):
-    both = jnp.concatenate([heard_ref[:, 0:BLOCK], sent_ref[BLOCK:, 0:BLOCK]], axis=1)
+    sent_ref[BLOCK:, :] = jnp.concatenate([sent, user], axis=1)
+
+
+def chunk_kernel(place_ref, near_ref, far_ref, sent_ref, chunk_ref):
+    zhi, core = place_ref[5], place_ref[6]
+    users = []
     for k in range(NXY):
-        plane_ref[k] = both
-
-
-def spread(parts, row, lane):
+        there_x, there_y = k >> 2, k & 3
+        at = (there_x >> 1) * 8 + there_y * 2 + zhi
+        near, far = near_ref[at, BLOCK:, BLOCK:], far_ref[at, BLOCK:, BLOCK:]
+        users.append(jnp.where(core == there_x & 1, near, far))
+    places = [jnp.concatenate([user[0:1], user[1:2]], axis=1) for user in users]
+    places = jnp.concatenate(places, axis=0)
+    sender = -0.5 * sent_ref[BLOCK : BLOCK + 2, 0:BLOCK]
+    sender = jnp.concatenate([sender[0:1], sender[1:2]], axis=1)
+    for k, user in enumerate(users):
+        weights = jnp.concatenate([user[2:3], user[3:4]], axis=1)
+        tail = jnp.concatenate([sender, weights, jnp.zeros((6, BANDS), F32)], axis=0)
+        chunk_ref[k, 0:NXY, :] = places
+        chunk_ref[k, NXY:, :] = tail
+
+
+def plane_kernel(place_ref, chunk_ref, listeners_ref, senders_ref, user_ref):
+    x, y, z0, z2, z1, zhi, core = (place_ref[i] for i in range(7))
+    source = (core * 2 + z2) * 4 + z1 * 2 + z0
+
+    def line(pieces):
+        pairs = [jnp.concatenate(pieces[k : k + 2], axis=1) for k in range(0, NXY, 2)]
+        return jnp.concatenate(pairs, axis=1).astype(jnp.int32)
+
+    def store(ref, features):
+        ref[...] = jnp.concatenate([features, jnp.zeros_like(features)], axis=0).astype(BF16)
+
+    left, right = slice(0, BLOCK), slice(BLOCK, 2 * BLOCK)
+    places = chunk_ref[source, 0:NXY, :]
+    lx, ly = (line([places[k : k + 1, half] for k in range(NXY)]) for half in (left, right))
+    sx, sy = (line([chunk_ref[k, NXY : NXY + 1, half] for k in range(NXY)]) for half in (left, right))
+    store(listeners_ref, listener_features(lx, ly))
+    store(senders_ref, sender_features(sx, sy))
+    user_ref[0:1, :] = chunk_ref[source, pl.ds(x * 4 + y, 1), :]
+    user_ref[1:8, :] = chunk_ref[source, NXY + 1 :, :]
+
+
+def spread(parts):
     pieces = []
     for k in range(0, 16, 2):
-        left = parts[k, row : row + 8, lane : lane + BLOCK]
-        right = parts[k + 1, row : row + 8, lane : lane + BLOCK]
+        left = parts[k, BLOCK:, 0:BLOCK]
+        right = parts[k + 1, BLOCK:, 0:BLOCK]
         pieces.append(jnp.concatenate([left, right], axis=1))
     features = jnp.concatenate(pieces, axis=1)
     return jnp.concatenate([features, jnp.zeros_like(features)], axis=0).astype(BF16)
@@ -95,11 +130,11 @@
     return high, low
 
 
-def gain_kernel(far, lane, place_ref, plane_ref, column_ref, *rest):
+def gain_kernel(far, place_ref, plane_ref, column_ref, *rest):
     *before, total_ref = rest
     x, y, z0, z2, z1, zhi, core = (place_ref[i] for i in range(7))
-    rows = spread(plane_ref, 0, lane)
-    columns = spread(column_ref, BLOCK, 0)
+    rows = plane_ref[...]
+    columns = spread(column_ref)
     value_high, value_low = split(column_ref[:, 0:BLOCK, :].reshape(HALF, BANDS))
     values = jnp.concatenate([value_high, value_low], axis=1)
     values = jnp.concatenate([values, values], axis=0)
@@ -142,13 +177,14 @@
     return total
 
 
-def derive_kernel(parts_ref, powers_ref, sent_ref, heard_ref, quality_ref, own_ref, column_ref):
+def derive_kernel(parts_ref, powers_ref, sent_ref, user_ref, quality_ref, own_ref, column_ref):
     interference = add_blocks(parts_ref)
-    dx = heard_ref[0:1, 0:BLOCK] + 0.5 * sent_ref[BLOCK : BLOCK + 1, 0:BLOCK]
-    dy = heard_ref[1:2, 0:BLOCK] + 0.5 * sent_ref[BLOCK + 1 : BLOCK + 2, 0:BLOCK]
+    lx, ly = user_ref[0:1, 0:BLOCK], user_ref[0:1, BLOCK:]
+    dx = lx + 0.5 * sent_ref[BLOCK : BLOCK + 1, 0:BLOCK]
+    dy = ly + 0.5 * sent_ref[BLOCK + 1 : BLOCK + 2, 0:BLOCK]
     own_gain = 1.0 / (1.0 + dx * dx + dy * dy)
-    weight = WEIGHT_UNIT * heard_ref[0:1, BLOCK:]
-    fair = heard_ref[1:2, BLOCK:]
+    weight = WEIGHT_UNIT * user_ref[1:2, 0:BLOCK]
+    fair = user_ref[1:2, BLOCK:]
     rows = jnp.concatenate([own_gain, weight, fair, jnp.zeros((5, BLOCK), F32)], axis=0)
     rows = jnp.concatenate([rows, jnp.zeros_like(rows)], axis=1)
     columns = jnp.concatenate([rows, jnp.zeros((120, 128), F32)], axis=0).T
@@ -162,14 +198,15 @@
     quality_ref[...] = quality
     own_ref[...] = ARRAY_GAIN * own_gain * marginal
     column_ref[0:BLOCK, :] = marginal * quality
-    column_ref[BLOCK:, :] = heard_ref[...]
-
-
-def finish_kernel(step_ref, parts_ref, own_ref, powers_ref, gradient_ref, power_ref, gap_ref):
+    features = listener_features(lx.astype(jnp.int32), ly.astype(jnp.int32))
+    column_ref[BLOCK:, :] = jnp.concatenate([features, jnp.zeros_like(features)], axis=1)
+
+
+def finish_kernel(place_ref, parts_ref, own_ref, powers_ref, gradient_ref, power_ref, gap_ref):
     gradient = own_ref[...] - add_blocks(parts_ref)
     powers = powers_ref[...]
     target = PEAK_POWER * jax.nn.sigmoid(gradient)
-    step_size = step_ref[0].astype(F32) / 4096.0
+    step_size = place_ref[7].astype(F32) / 4096.0
     gradient_ref[...] = gradient
     power_ref[...] = powers + step_size * (target - powers)
     gap = PEAK_POWER * jnp.maximum(gradient, 0.0) - gradient * powers
@@ -185,44 +222,45 @@
 
 
 def per_device(sender_xy, listener_xy, powers, weight, fairness, step_code):
-    place = jnp.stack([lax.axis_index(name).astype(jnp.int32) for name in PLACE])
-    to_sender = [(b, (b % 32) * 16 + b // 32) for b in range(512)]
-    to_receiver = [(s, b) for b, s in to_sender]
+    place = [lax.axis_index(name).astype(jnp.int32) for name in PLACE]
+    place = jnp.stack([*place, step_code[0]])
+    to_receiver = [((b % 32) * 16 + b // 32, b) for b in range(512)]
     swap = [(0, 1), (1, 0)]
     block, product = shape(BLOCK, BANDS), shape(ROWS, BANDS)
     work = dict(flops=2 * ROWS * HALF * 512, bytes_accessed=1 << 22)
 
-    def gain_product(far, lane, *args):
+    def gain_product(far, *args):
         def kernel(*refs):
-            gain_kernel(far, lane, *refs)
+            gain_kernel(far, *refs)
 
         return call(kernel, product, 1 + len(args), smem=(0,), **work)(place, *args)
 
-    def spread_sum(near, far, plane, lane):
-        part = gain_product(False, lane, plane, near)
-        part = gain_product(True, lane, plane, far, part)
+    def spread_sum(near, far, plane):
+        part = gain_product(False, plane, near)
+        part = gain_product(True, plane, far, part)
         return lax.all_to_all(part.reshape(NXY, BLOCK, BANDS), XY, 0, 0)
 
-    info = jnp.concatenate([listener_xy, weight[None], fairness[None]], axis=0)
-    heard = call(hear_kernel, shape(8, 128), 1)(info)
-    heard = lax.ppermute(heard, AXES, to_sender)
-    sent = call(pack_kernel, shape(SENT, BANDS), 2)(sender_xy, powers)
+    info = jnp.concatenate([sender_xy, listener_xy, weight[None], fairness[None]], axis=0)
+    sent = call(pack_kernel, shape(SENT, BANDS), 2)(info, powers)
     near = lax.all_gather(sent, Z, axis=0)
-    near, heard = lax.optimization_barrier((near, heard))
     far = lax.ppermute(near, "core", swap)
-    plane = call(plane_kernel, shape(NXY, 8, 128), 2)(heard, sent)
-    plane = lax.all_to_all(plane, XY, 0, 0)
-    parts = spread_sum(near, far, plane, 0)
+    chunks = call(chunk_kernel, shape(NXY, 24, BANDS), 4, smem=(0,))(place, near, far, sent)
+    chunks = lax.all_to_all(chunks, XY, 0, 0)
+    features = shape(16, ROWS, dtype=BF16)
+    listeners, senders, user = call(
+        plane_kernel, (features, features, shape(8, BANDS)), 2, smem=(0,)
+    )(place, chunks)
+    parts = spread_sum(near, far, listeners)
     quality, own, column = call(derive_kernel, (block, block, shape(SENT, BANDS)), 4)(
-        parts, powers, sent, heard
+        parts, powers, sent, user
     )
 
     near = lax.all_gather(column, Z, axis=0)
     far = lax.ppermute(near, "core", swap)
-    parts = spread_sum(near, far, plane, BLOCK)
+    parts = spread_sum(near, far, senders)
     gradient, new_power, gap = call(
         finish_kernel, (block, block, shape(2 * NZ, 1, BANDS)), 4, smem=(0,)
-    )(step_code, parts, own, powers)
+    )(place, parts, own, powers)
 
     quality = lax.ppermute(quality, AXES, to_receiver)
     gap = lax.all_to_all(gap, (*Z, "core"), 0, 0)

time: 176 us -> 171 us (0.972)
  blocking collectives: 75.6 us -> 94.5 us
  waiting for transfers between devices: 31.4 us -> 15.9 us
  starting transfers between devices: 46.5 us -> 38 us
    all_to_all x2 -> x0, waiting for transfers between devices: 16.2 us -> none  [the longest x1 9.86 us: spread_sum(): return lax.all_to_all(part.reshape(NXY, BLOCK, BANDS), XY, 0, 0)]
    all_to_all x0 -> x1, blocking collectives: none -> 13.6 us  [per_device(): chunks = lax.all_to_all(chunks, XY, 0, 0)]
    all_to_all x1 -> x2, blocking collectives: 12.1 us -> 25.6 us  [spread_sum(): return lax.all_to_all(part.reshape(NXY, BLOCK, BANDS), XY, 0, 0)]
    all_gather x1, blocking collectives: 40.2 us -> 32.1 us  [per_device(): near = lax.all_gather(sent, Z, axis=0)]
    all_to_all x2 -> x0, starting transfers between devices: 7.07 us -> none  [the longest x1 3.57 us: spread_sum(): return lax.all_to_all(part.reshape(NXY, BLOCK, BANDS), XY, 0, 0)]
    ppermute x1 -> x0, starting transfers between devices: 4.5 us -> none  [per_device(): heard = lax.ppermute(heard, AXES, to_sender)]
    all_to_all x1, starting transfers between devices: 7.77 us -> 10.1 us  [per_device(): gap = lax.all_to_all(gap, (*Z, 'core'), 0, 0)]
  transfers between devices with their start and end apart: 8 -> 5, of which waited for: 4 -> 3; matrix products, arithmetic and copies ran while one was open for 0% -> 0% of each run, Pallas kernels for 4% -> 2%
where the time goes in v8:
time: 171 us; the launch traced here: 170 us
  blocking collectives  94.5 us (55%)
  starting transfers between devices  38 us (22%)
  waiting for transfers between devices  15.9 us (9%)
  Pallas kernels  15.8 us (9%)
  between operations  3.24 us (2%)
  local copies, waits for them, and re-layouts  2.14 us (1%)
    all_gather x1, blocking collectives, per_device(): near = lax.all_gather(sent, Z, axis=0)  32.1 us
    all_to_all x2, blocking collectives, spread_sum(): return lax.all_to_all(part.reshape(NXY, BLOCK, BANDS), XY, 0, 0)  25.6 us
    all_gather x1, blocking collectives, per_device(): near = lax.all_gather(column, Z, axis=0)  23.2 us
    ppermute x2, starting transfers between devices, per_device(): far = lax.ppermute(near, 'core', swap)  21.6 us
    all_to_all x1, blocking collectives, per_device(): chunks = lax.all_to_all(chunks, XY, 0, 0)  13.6 us
    pallas_call x4, Pallas kernels, gain_product(): return call(kernel, product, 1 + len(args), smem=(0,), **work)(place, *args)  12.3 us
    all_to_all x1, starting transfers between devices, per_device(): gap = lax.all_to_all(gap, (*Z, 'core'), 0, 0)  10.1 us
    all_to_all x1, waiting for transfers between devices, per_device(): gap = lax.all_to_all(gap, (*Z, 'core'), 0, 0)  8.79 us
  transfers between devices with their start and end apart: 5, of which 3 were waited for; matrix products, arithmetic and copies ran while one was open for 0% of the time, Pallas kernels for 2%

profile of v8, /device:TPU:1, one launch (start us, length us, event | category | flops | bytes accessed | tf_op | source)
XLA Modules:
  0.0 170.3 jit_solution(17775895412438884882)
XLA Ops:
  0.6 0.0 copy-start.3
  0.6 0.0 copy-start.5
  0.7 0.0 copy-start.2
  0.7 0.0 copy-start.4
  0.7 0.6 copy-done.3
  1.3 0.0 copy-done.5
  1.3 0.0 copy-done.2
  1.3 0.0 copy-done.4
  1.4 0.0 copy-start
  1.4 0.7 copy-done
  2.1 0.1 shard_map.93.sent_ref
  2.2 32.1 %all-gather = f32[1152,128]{1,0:T(8,128)S(1)} all-gather(f32[72,128]{1,0:T(8,128)S(1)} %shard_map.93.sent_ref), channel_id=2, replica_groups=mesh['z2'=2,'z1'=2,'z0'=2,'x'=4,'y'=4,'zhi'=2,'core'=2] {'zhi','z2','z1'..., dimensions={0}, use_global_device_ids=true | all-gather | bytes 626688 | tf_op jit(solution)/shard_map/all_gather | solution.py:245
  34.3 10.1 %collective-permute-start = (f32[16,72,128]{2,1,0:T(8,128)S(1)}, f32[16,72,128]{2,1,0:T(8,128)S(1)}, u32[]{:S(2)}, u32[]{:S(2)}) collective-permute-start(f32[16,72,128]{2,1,0:T(8,128)S(1)} %bitcast.14), channel_id=1, source_target_pairs={{0,1},{1,0},{2,3},{3,2},{4,5},{5,4},{6,7},{7,6},{8,9},{9,8},{10,11... | collective-permute-start | bytes 1769480 | tf_op jit(solution)/shard_map/ppermute | solution.py:246
  45.1 0.1 stack.31.place_ref.refs_0_
  45.2 0.9 collective-permute-done.far_ref.refs_2_
  46.1 0.6 shard_map.94
  46.7 13.6 %all_to_all.25.chunk_ref = f32[16,24,128]{2,1,0:T(8,128)S(1)} all-to-all(f32[16,24,128]{2,1,0:T(8,128)S(1)} %shard_map.94), channel_id=1, replica_groups=mesh['z2'=2,'z1'=2,'z0'=2,'x'=4,'y'=4,'zhi'=2,'core'=2] {'x','y'}, dimensions={0} | all-to-all | bytes 393216 | tf_op jit(solution)/shard_map/all_to_all | solution.py:248
  60.3 0.7 shard_map.95
  61.0 3.1 %shard_map.96.refs_3_ = f32[1024,128]{1,0:T(8,128)S(1)} custom-call(s32[8]{0:T(128)S(1)} %stack.31.place_ref.refs_0_, bf16[16,1024]{1,0:T(8,128)(2,1)S(1)} %get-tuple-element.13.refs_1_, f32[16,72,128]{2,1,0:T(8,128)S(1)} %bitcast.16), custom_call_target="tpu_custom_call" | custom-call | flops 1073741824 | bytes 4194304 | tf_op jit(solution)/shard_map/pallas_call | solution.py:236
  64.1 3.1 %shard_map.97 = f32[1024,128]{1,0:T(8,128)S(1)} custom-call(s32[8]{0:T(128)S(1)} %stack.31.place_ref.refs_0_, bf16[16,1024]{1,0:T(8,128)(2,1)S(1)} %get-tuple-element.13.refs_1_, f32[16,72,128]{2,1,0:T(8,128)S(1)} %collective-permute-done.far_ref.refs_2_, f32[1024,128]{1,0:T(8,128)S(1)} %shard_map.96.refs_3_), custom_call_target="tpu_custom_call" | custom-call | flops 1073741824 | bytes 4194304 | tf_op jit(solution)/shard_map/pallas_call | solution.py:236
  67.2 0.0 copy-start.1
  67.2 12.6 %all_to_all.26.parts_ref = f32[16,64,128]{2,1,0:T(8,128)S(1)} all-to-all(f32[16,64,128]{2,1,0:T(8,128)S(1)} %bitcast.19), channel_id=1, replica_groups=mesh['z2'=2,'z1'=2,'z0'=2,'x'=4,'y'=4,'zhi'=2,'core'=2] {'x','y'}, dimensions={0} | all-to-all | bytes 1048576 | tf_op jit(solution)/shard_map/all_to_all | solution.py:241
  79.7 0.0 copy-done.1
  79.7 0.3 shard_map.98
  80.1 23.2 %all-gather.1 = f32[1152,128]{1,0:T(8,128)S(1)} all-gather(f32[72,128]{1,0:T(8,128)S(1)} %get-tuple-element.17), channel_id=3, replica_groups=mesh['z2'=2,'z1'=2,'z0'=2,'x'=4,'y'=4,'zhi'=2,'core'=2] {'zhi','z2','z1'..., dimensions={0}, use_global_device_ids=true | all-gather | bytes 626688 | tf_op jit(solution)/shard_map/all_gather | solution.py:258
  103.3 11.4 %collective-permute-start.2 = (f32[16,72,128]{2,1,0:T(8,128)S(1)}, f32[16,72,128]{2,1,0:T(8,128)S(1)}, u32[]{:S(2)}, u32[]{:S(2)}) collective-permute-start(f32[16,72,128]{2,1,0:T(8,128)S(1)} %bitcast.17), channel_id=1, source_target_pairs={{0,1},{1,0},{2,3},{3,2},{4,5},{5,4},{6,7},{7,6},{8,9},{9,8},{10,11... | collective-permute-start | bytes 1769480 | tf_op jit(solution)/shard_map/ppermute | solution.py:259
  114.7 3.1 %shard_map.99.refs_3_ = f32[1024,128]{1,0:T(8,128)S(1)} custom-call(s32[8]{0:T(128)S(1)} %stack.31.place_ref.refs_0_, bf16[16,1024]{1,0:T(8,128)(2,1)S(1)} %get-tuple-element.16.refs_1_, f32[16,72,128]{2,1,0:T(8,128)S(1)} %bitcast.18), custom_call_target="tpu_custom_call" | custom-call | flops 1073741824 | bytes 4194304 | tf_op jit(solution)/shard_map/pallas_call | solution.py:236
  117.8 0.0 collective-permute-done.2.refs_2_
  117.8 3.1 %shard_map.100 = f32[1024,128]{1,0:T(8,128)S(1)} custom-call(s32[8]{0:T(128)S(1)} %stack.31.place_ref.refs_0_, bf16[16,1024]{1,0:T(8,128)(2,1)S(1)} %get-tuple-element.16.refs_1_, f32[16,72,128]{2,1,0:T(8,128)S(1)} %collective-permute-done.2.refs_2_, f32[1024,128]{1,0:T(8,128)S(1)} %shard_map.99.refs_3_), custom_call_target="tpu_custom_call" | custom-call | flops 1073741824 | bytes 4194304 | tf_op jit(solution)/shard_map/pallas_call | solution.py:236
  120.9 13.0 %all_to_all.27.parts_ref = f32[16,64,128]{2,1,0:T(8,128)S(1)} all-to-all(f32[16,64,128]{2,1,0:T(8,128)S(1)} %bitcast.20), channel_id=1, replica_groups=mesh['z2'=2,'z1'=2,'z0'=2,'x'=4,'y'=4,'zhi'=2,'core'=2] {'x','y'}, dimensions={0} | all-to-all | bytes 1048576 | tf_op jit(solution)/shard_map/all_to_all | solution.py:241
  133.9 1.2 shard_map.101
  135.1 10.1 %all-to-all-start.3 = ((f32[32,1,128]{2,1,0:T(1,128)}), f32[32,1,128]{2,1,0:T(1,128)S(1)}, u32[]{:S(2)}, u32[]{:S(2)}) async-start(f32[32,1,128]{2,1,0:T(1,128)} %get-tuple-element.21), calls=%async_computation.3 | async-start | bytes 32768 | tf_op jit(solution)/shard_map/all_to_all | solution.py:266
  145.2 2.9 %collective-permute-start.1 = (f32[64,128]{1,0:T(8,128)S(1)}, f32[64,128]{1,0:T(8,128)S(1)}, u32[]{:S(2)}, u32[]{:S(2)}) collective-permute-start(f32[64,128]{1,0:T(8,128)S(1)} %get-tuple-element.15), channel_id=1, source_target_pairs={{0,0},{16,1},{32,2},{48,3},{64,4},{80,5},{96,6},{112,7},{128,8},{1... | collective-permute-start | bytes 98312 | tf_op jit(solution)/shard_map/ppermute | solution.py:265
  148.1 8.8 %all-to-all-done.3.parts_ref = f32[32,1,128]{2,1,0:T(1,128)S(1)} async-done(((f32[32,1,128]{2,1,0:T(1,128)}), f32[32,1,128]{2,1,0:T(1,128)S(1)}, u32[]{:S(2)}, u32[]{:S(2)}) %all-to-all-start.3) | async-done | bytes 16416 | tf_op jit(solution)/shard_map/all_to_all | solution.py:266
  156.9 0.6 shard_map.102
  157.5 3.5 %all-to-all-start.4 = ((f32[16,1,128]{2,1,0:T(1,128)}), f32[16,1,128]{2,1,0:T(1,128)S(1)}, u32[]{:S(2)}, u32[]{:S(2)}) async-start(f32[16,1,128]{2,1,0:T(1,128)} %shard_map.102), calls=%async_computation.4 | async-start | bytes 16384 | tf_op jit(solution)/shard_map/all_to_all | solution.py:268
  161.0 0.0 collective-permute-done.1
  161.0 6.3 %all-to-all-done.4 = f32[16,1,128]{2,1,0:T(1,128)S(1)} async-done(((f32[16,1,128]{2,1,0:T(1,128)}), f32[16,1,128]{2,1,0:T(1,128)S(1)}, u32[]{:S(2)}, u32[]{:S(2)}) %all-to-all-start.4) | async-done | bytes 8224 | tf_op jit(solution)/shard_map/all_to_all | solution.py:268
  167.3 0.6 reduce_sum.9
  168.5 0.6 copy.12
  (1 shorter events, 0.0 us)
Async XLA Ops:
  0.6 0.7 copy-start.3
  0.6 0.7 copy-start.5
  0.7 0.7 copy-start.2
  0.7 0.7 copy-start.4
  1.4 0.8 copy-start
  34.3 11.7 %collective-permute-start = (f32[16,72,128]{2,1,0:T(8,128)S(1)}, f32[16,72,128]{2,1,0:T(8,128)S(1)}, u32[]{:S(2)}, u32[]{:S(2)}) collective-permute-start(f32[16,72,128]{2,1,0:T(8,128)S(1)} %bitcast.14), channel_id=1, source_target_pairs={{0,1},{1,0},{2,3},{3,2},{4,5},{5,4},{6,7},{7,6},{8,9},{9,8},{10,11... | collective-permute-start | bytes 1769480 | tf_op jit(solution)/shard_map/ppermute | solution.py:246
  67.2 12.6 %copy-start.1 = (f32[64,128]{1,0:T(8,128)S(1)}, f32[64,128]{1,0:T(8,128)}, u32[]{:S(2)}) copy-start(f32[64,128]{1,0:T(8,128)} %powers_ref.5) | copy-start | bytes 98308
  103.3 14.5 %collective-permute-start.2 = (f32[16,72,128]{2,1,0:T(8,128)S(1)}, f32[16,72,128]{2,1,0:T(8,128)S(1)}, u32[]{:S(2)}, u32[]{:S(2)}) collective-permute-start(f32[16,72,128]{2,1,0:T(8,128)S(1)} %bitcast.17), channel_id=1, source_target_pairs={{0,1},{1,0},{2,3},{3,2},{4,5},{5,4},{6,7},{7,6},{8,9},{9,8},{10,11... | collective-permute-start | bytes 1769480 | tf_op jit(solution)/shard_map/ppermute | solution.py:259
  135.1 21.8 %all-to-all-start.3 = ((f32[32,1,128]{2,1,0:T(1,128)}), f32[32,1,128]{2,1,0:T(1,128)S(1)}, u32[]{:S(2)}, u32[]{:S(2)}) async-start(f32[32,1,128]{2,1,0:T(1,128)} %get-tuple-element.21), calls=%async_computation.3 | async-start | bytes 32768 | tf_op jit(solution)/shard_map/all_to_all | solution.py:266
  145.2 15.8 %collective-permute-start.1 = (f32[64,128]{1,0:T(8,128)S(1)}, f32[64,128]{1,0:T(8,128)S(1)}, u32[]{:S(2)}, u32[]{:S(2)}) collective-permute-start(f32[64,128]{1,0:T(8,128)S(1)} %get-tuple-element.15), channel_id=1, source_target_pairs={{0,0},{16,1},{32,2},{48,3},{64,4},{80,5},{96,6},{112,7},{128,8},{1... | collective-permute-start | bytes 98312 | tf_op jit(solution)/shard_map/ppermute | solution.py:265
  157.5 9.8 %all-to-all-start.4 = ((f32[16,1,128]{2,1,0:T(1,128)}), f32[16,1,128]{2,1,0:T(1,128)S(1)}, u32[]{:S(2)}, u32[]{:S(2)}) async-start(f32[16,1,128]{2,1,0:T(1,128)} %shard_map.102), calls=%async_computation.4 | async-start | bytes 16384 | tf_op jit(solution)/shard_map/all_to_all | solution.py:268

commit v9 on v8

--- a/solution.py
+++ b/solution.py
@@ -139,7 +139,7 @@
     values = jnp.concatenate([value_high, value_low], axis=1)
     values = jnp.concatenate([values, values], axis=0)
     row_base = zhi * 4096 + core * 2048 + (z2 * 4 + z1 * 2 + z0) * 256
-    col_base = y * 8192 + (1 - core if far else core) * 2048 + x * 64
+    col_base = y * 8192 + core * 2048 + x * 64
     tile = 128
     for r in range(0, ROWS, tile):
         row = lax.broadcasted_iota(jnp.int32, (tile, tile), 0) + r
@@ -158,7 +158,8 @@
             )
             guess = pl.reciprocal(square, approx=True)
             gain = guess * (2.0 - square * guess)
-            gain = jnp.where(row_id == col_id, 0.0, gain)
+            if not far:
+                gain = jnp.where(row_id == col_id, 0.0, gain)
             high, low = split(gain)
             highs.append(high)
             lows.append(low)
@@ -221,6 +222,12 @@
         out_ref[k] = total
 
 
+def last_kernel(parts_ref, late_ref, gap_ref, quality_ref):
+    total = jnp.sum(jnp.sum(parts_ref[...], axis=0), axis=1, keepdims=True)
+    gap_ref[...] = total / (USERS * BANDS)
+    quality_ref[...] = late_ref[...]
+
+
 def per_device(sender_xy, listener_xy, powers, weight, fairness, step_code):
     place = [lax.axis_index(name).astype(jnp.int32) for name in PLACE]
     place = jnp.stack([*place, step_code[0]])
@@ -266,7 +273,8 @@
     gap = lax.all_to_all(gap, (*Z, "core"), 0, 0)
     gap = call(fold_kernel, shape(NXY, 1, BANDS), 1)(gap)
     gap = lax.all_to_all(gap, XY, 0, 0)
-    return quality, gradient, new_power, (jnp.sum(gap) / (USERS * BANDS)).reshape(1)
+    gap, quality = call(last_kernel, (shape(1, 1), block), 2)(gap, quality)
+    return quality, gradient, new_power, gap.reshape(1)
 
 
 def solution(mesh):

time: 171 us -> 168 us (0.982)
  between operations: 3.24 us -> 1.45 us
where the time goes in v9:
time: 168 us; the launch traced here: 167 us
  blocking collectives  94.5 us (56%)
  starting transfers between devices  38 us (23%)
  waiting for transfers between devices  15.9 us (9%)
  Pallas kernels  15.7 us (9%)
    all_gather x1, blocking collectives, per_device(): near = lax.all_gather(sent, Z, axis=0)  32.1 us
    all_to_all x2, blocking collectives, spread_sum(): return lax.all_to_all(part.reshape(NXY, BLOCK, BANDS), XY, 0, 0)  25.6 us
    all_gather x1, blocking collectives, per_device(): near = lax.all_gather(column, Z, axis=0)  23.2 us
    ppermute x2, starting transfers between devices, per_device(): far = lax.ppermute(near, 'core', swap)  21.6 us
    all_to_all x1, blocking collectives, per_device(): chunks = lax.all_to_all(chunks, XY, 0, 0)  13.6 us
    pallas_call x4, Pallas kernels, gain_product(): return call(kernel, product, 1 + len(args), smem=(0,), **work)(place, *args)  11.5 us
    all_to_all x1, starting transfers between devices, per_device(): gap = lax.all_to_all(gap, (*Z, 'core'), 0, 0)  10.1 us
    all_to_all x1, waiting for transfers between devices, per_device(): gap = lax.all_to_all(gap, (*Z, 'core'), 0, 0)  8.79 us
  transfers between devices with their start and end apart: 5, of which 3 were waited for; matrix products, arithmetic and copies ran while one was open for 0% of the time, Pallas kernels for 2%

profile of v9, /device:TPU:1, one launch (start us, length us, event | category | flops | bytes accessed | tf_op | source)
XLA Modules:
  0.0 167.1 jit_solution(17799152748200711534)
XLA Ops:
  0.6 0.0 copy-start.3
  0.6 0.0 copy-start.5
  0.7 0.0 copy-start.2
  0.7 0.0 copy-start.4
  0.7 0.6 copy-done.3
  1.3 0.0 copy-done.5
  1.3 0.0 copy-done.2
  1.3 0.0 copy-done.4
  1.4 0.0 copy-start
  1.4 0.7 copy-done
  2.1 0.1 shard_map.93.sent_ref
  2.2 32.1 %all-gather = f32[1152,128]{1,0:T(8,128)S(1)} all-gather(f32[72,128]{1,0:T(8,128)S(1)} %shard_map.93.sent_ref), channel_id=2, replica_groups=mesh['z2'=2,'z1'=2,'z0'=2,'x'=4,'y'=4,'zhi'=2,'core'=2] {'zhi','z2','z1'..., dimensions={0}, use_global_device_ids=true | all-gather | bytes 626688 | tf_op jit(solution)/shard_map/all_gather | solution.py:252
  34.3 10.1 %collective-permute-start = (f32[16,72,128]{2,1,0:T(8,128)S(1)}, f32[16,72,128]{2,1,0:T(8,128)S(1)}, u32[]{:S(2)}, u32[]{:S(2)}) collective-permute-start(f32[16,72,128]{2,1,0:T(8,128)S(1)} %bitcast.14), channel_id=1, source_target_pairs={{0,1},{1,0},{2,3},{3,2},{4,5},{5,4},{6,7},{7,6},{8,9},{9,8},{10,11... | collective-permute-start | bytes 1769480 | tf_op jit(solution)/shard_map/ppermute | solution.py:253
  45.1 0.1 stack.31.place_ref.refs_0_
  45.2 0.9 collective-permute-done.far_ref.refs_2_
  46.1 0.6 shard_map.94
  46.7 13.6 %all_to_all.25.chunk_ref = f32[16,24,128]{2,1,0:T(8,128)S(1)} all-to-all(f32[16,24,128]{2,1,0:T(8,128)S(1)} %shard_map.94), channel_id=1, replica_groups=mesh['z2'=2,'z1'=2,'z0'=2,'x'=4,'y'=4,'zhi'=2,'core'=2] {'x','y'}, dimensions={0} | all-to-all | bytes 393216 | tf_op jit(solution)/shard_map/all_to_all | solution.py:255
  60.3 0.7 shard_map.95
  61.0 3.1 %shard_map.96.refs_3_ = f32[1024,128]{1,0:T(8,128)S(1)} custom-call(s32[8]{0:T(128)S(1)} %stack.31.place_ref.refs_0_, bf16[16,1024]{1,0:T(8,128)(2,1)S(1)} %get-tuple-element.16.refs_1_, f32[16,72,128]{2,1,0:T(8,128)S(1)} %bitcast.16), custom_call_target="tpu_custom_call" | custom-call | flops 1073741824 | bytes 4194304 | tf_op jit(solution)/shard_map/pallas_call | solution.py:243
  64.1 2.7 %shard_map.97 = f32[1024,128]{1,0:T(8,128)S(1)} custom-call(s32[8]{0:T(128)S(1)} %stack.31.place_ref.refs_0_, bf16[16,1024]{1,0:T(8,128)(2,1)S(1)} %get-tuple-element.16.refs_1_, f32[16,72,128]{2,1,0:T(8,128)S(1)} %collective-permute-done.far_ref.refs_2_, f32[1024,128]{1,0:T(8,128)S(1)} %shard_map.96.refs_3_), custom_call_target="tpu_custom_call" | custom-call | flops 1073741824 | bytes 4194304 | tf_op jit(solution)/shard_map/pallas_call | solution.py:243
  66.8 0.0 copy-start.1
  66.8 12.6 %all_to_all.26.parts_ref = f32[16,64,128]{2,1,0:T(8,128)S(1)} all-to-all(f32[16,64,128]{2,1,0:T(8,128)S(1)} %bitcast.19), channel_id=1, replica_groups=mesh['z2'=2,'z1'=2,'z0'=2,'x'=4,'y'=4,'zhi'=2,'core'=2] {'x','y'}, dimensions={0} | all-to-all | bytes 1048576 | tf_op jit(solution)/shard_map/all_to_all | solution.py:248
  79.3 0.0 copy-done.1
  79.3 0.3 shard_map.98
  79.7 23.2 %all-gather.1 = f32[1152,128]{1,0:T(8,128)S(1)} all-gather(f32[72,128]{1,0:T(8,128)S(1)} %get-tuple-element.18), channel_id=3, replica_groups=mesh['z2'=2,'z1'=2,'z0'=2,'x'=4,'y'=4,'zhi'=2,'core'=2] {'zhi','z2','z1'..., dimensions={0}, use_global_device_ids=true | all-gather | bytes 626688 | tf_op jit(solution)/shard_map/all_gather | solution.py:265
  102.9 11.4 %collective-permute-start.1 = (f32[16,72,128]{2,1,0:T(8,128)S(1)}, f32[16,72,128]{2,1,0:T(8,128)S(1)}, u32[]{:S(2)}, u32[]{:S(2)}) collective-permute-start(f32[16,72,128]{2,1,0:T(8,128)S(1)} %bitcast.17), channel_id=1, source_target_pairs={{0,1},{1,0},{2,3},{3,2},{4,5},{5,4},{6,7},{7,6},{8,9},{9,8},{10,11... | collective-permute-start | bytes 1769480 | tf_op jit(solution)/shard_map/ppermute | solution.py:266
  114.3 3.1 %shard_map.99.refs_3_ = f32[1024,128]{1,0:T(8,128)S(1)} custom-call(s32[8]{0:T(128)S(1)} %stack.31.place_ref.refs_0_, bf16[16,1024]{1,0:T(8,128)(2,1)S(1)} %get-tuple-element.15.refs_1_, f32[16,72,128]{2,1,0:T(8,128)S(1)} %bitcast.18), custom_call_target="tpu_custom_call" | custom-call | flops 1073741824 | bytes 4194304 | tf_op jit(solution)/shard_map/pallas_call | solution.py:243
  117.4 0.0 collective-permute-done.1.refs_2_
  117.4 2.7 %shard_map.100 = f32[1024,128]{1,0:T(8,128)S(1)} custom-call(s32[8]{0:T(128)S(1)} %stack.31.place_ref.refs_0_, bf16[16,1024]{1,0:T(8,128)(2,1)S(1)} %get-tuple-element.15.refs_1_, f32[16,72,128]{2,1,0:T(8,128)S(1)} %collective-permute-done.1.refs_2_, f32[1024,128]{1,0:T(8,128)S(1)} %shard_map.99.refs_3_), custom_call_target="tpu_custom_call" | custom-call | flops 1073741824 | bytes 4194304 | tf_op jit(solution)/shard_map/pallas_call | solution.py:243
  120.1 13.0 %all_to_all.27.parts_ref = f32[16,64,128]{2,1,0:T(8,128)S(1)} all-to-all(f32[16,64,128]{2,1,0:T(8,128)S(1)} %bitcast.20), channel_id=1, replica_groups=mesh['z2'=2,'z1'=2,'z0'=2,'x'=4,'y'=4,'zhi'=2,'core'=2] {'x','y'}, dimensions={0} | all-to-all | bytes 1048576 | tf_op jit(solution)/shard_map/all_to_all | solution.py:248
  133.1 1.2 shard_map.101
  134.3 10.1 %all-to-all-start.3 = ((f32[32,1,128]{2,1,0:T(1,128)}), f32[32,1,128]{2,1,0:T(1,128)S(1)}, u32[]{:S(2)}, u32[]{:S(2)}) async-start(f32[32,1,128]{2,1,0:T(1,128)} %get-tuple-element.20), calls=%async_computation.3 | async-start | bytes 32768 | tf_op jit(solution)/shard_map/all_to_all | solution.py:273
  144.4 2.9 %collective-permute-start.2 = (f32[64,128]{1,0:T(8,128)S(1)}, f32[64,128]{1,0:T(8,128)S(1)}, u32[]{:S(2)}, u32[]{:S(2)}) collective-permute-start(f32[64,128]{1,0:T(8,128)S(1)} %get-tuple-element.21), channel_id=1, source_target_pairs={{0,0},{16,1},{32,2},{48,3},{64,4},{80,5},{96,6},{112,7},{128,8},{1... | collective-permute-start | bytes 98312 | tf_op jit(solution)/shard_map/ppermute | solution.py:272
  147.3 8.8 %all-to-all-done.3.parts_ref = f32[32,1,128]{2,1,0:T(1,128)S(1)} async-done(((f32[32,1,128]{2,1,0:T(1,128)}), f32[32,1,128]{2,1,0:T(1,128)S(1)}, u32[]{:S(2)}, u32[]{:S(2)}) %all-to-all-start.3) | async-done | bytes 16416 | tf_op jit(solution)/shard_map/all_to_all | solution.py:273
  156.1 0.6 shard_map.102
  156.7 3.5 %all-to-all-start.4 = ((f32[16,1,128]{2,1,0:T(1,128)}), f32[16,1,128]{2,1,0:T(1,128)S(1)}, u32[]{:S(2)}, u32[]{:S(2)}) async-start(f32[16,1,128]{2,1,0:T(1,128)} %shard_map.102), calls=%async_computation.4 | async-start | bytes 16384 | tf_op jit(solution)/shard_map/all_to_all | solution.py:275
  160.2 0.0 collective-permute-done.2.late_ref
  160.2 6.3 %all-to-all-done.4.parts_ref = f32[16,1,128]{2,1,0:T(1,128)S(1)} async-done(((f32[16,1,128]{2,1,0:T(1,128)}), f32[16,1,128]{2,1,0:T(1,128)S(1)}, u32[]{:S(2)}, u32[]{:S(2)}) %all-to-all-start.4) | async-done | bytes 8224 | tf_op jit(solution)/shard_map/all_to_all | solution.py:275
  166.5 0.6 shard_map.103
  (1 shorter events, 0.0 us)
Async XLA Ops:
  0.6 0.7 copy-start.3
  0.6 0.7 copy-start.5
  0.7 0.7 copy-start.2
  0.7 0.7 copy-start.4
  1.4 0.8 copy-start
  34.3 11.7 %collective-permute-start = (f32[16,72,128]{2,1,0:T(8,128)S(1)}, f32[16,72,128]{2,1,0:T(8,128)S(1)}, u32[]{:S(2)}, u32[]{:S(2)}) collective-permute-start(f32[16,72,128]{2,1,0:T(8,128)S(1)} %bitcast.14), channel_id=1, source_target_pairs={{0,1},{1,0},{2,3},{3,2},{4,5},{5,4},{6,7},{7,6},{8,9},{9,8},{10,11... | collective-permute-start | bytes 1769480 | tf_op jit(solution)/shard_map/ppermute | solution.py:253
  66.8 12.6 %copy-start.1 = (f32[64,128]{1,0:T(8,128)S(1)}, f32[64,128]{1,0:T(8,128)}, u32[]{:S(2)}) copy-start(f32[64,128]{1,0:T(8,128)} %powers_ref.5) | copy-start | bytes 98308
  102.9 14.5 %collective-permute-start.1 = (f32[16,72,128]{2,1,0:T(8,128)S(1)}, f32[16,72,128]{2,1,0:T(8,128)S(1)}, u32[]{:S(2)}, u32[]{:S(2)}) collective-permute-start(f32[16,72,128]{2,1,0:T(8,128)S(1)} %bitcast.17), channel_id=1, source_target_pairs={{0,1},{1,0},{2,3},{3,2},{4,5},{5,4},{6,7},{7,6},{8,9},{9,8},{10,11... | collective-permute-start | bytes 1769480 | tf_op jit(solution)/shard_map/ppermute | solution.py:266
  134.3 21.8 %all-to-all-start.3 = ((f32[32,1,128]{2,1,0:T(1,128)}), f32[32,1,128]{2,1,0:T(1,128)S(1)}, u32[]{:S(2)}, u32[]{:S(2)}) async-start(f32[32,1,128]{2,1,0:T(1,128)} %get-tuple-element.20), calls=%async_computation.3 | async-start | bytes 32768 | tf_op jit(solution)/shard_map/all_to_all | solution.py:273
  144.4 15.8 %collective-permute-start.2 = (f32[64,128]{1,0:T(8,128)S(1)}, f32[64,128]{1,0:T(8,128)S(1)}, u32[]{:S(2)}, u32[]{:S(2)}) collective-permute-start(f32[64,128]{1,0:T(8,128)S(1)} %get-tuple-element.21), channel_id=1, source_target_pairs={{0,0},{16,1},{32,2},{48,3},{64,4},{80,5},{96,6},{112,7},{128,8},{1... | collective-permute-start | bytes 98312 | tf_op jit(solution)/shard_map/ppermute | solution.py:272
  156.7 9.8 %all-to-all-start.4 = ((f32[16,1,128]{2,1,0:T(1,128)}), f32[16,1,128]{2,1,0:T(1,128)S(1)}, u32[]{:S(2)}, u32[]{:S(2)}) async-start(f32[16,1,128]{2,1,0:T(1,128)} %shard_map.102), calls=%async_computation.4 | async-start | bytes 16384 | tf_op jit(solution)/shard_map/all_to_all | solution.py:275

commit v10 on v9

--- a/solution.py
+++ b/solution.py
@@ -270,6 +270,7 @@
     )(place, parts, own, powers)
 
     quality = lax.ppermute(quality, AXES, to_receiver)
+    gap, quality = lax.optimization_barrier((gap, quality))
     gap = lax.all_to_all(gap, (*Z, "core"), 0, 0)
     gap = call(fold_kernel, shape(NXY, 1, BANDS), 1)(gap)
     gap = lax.all_to_all(gap, XY, 0, 0)

time: 168 us -> 174 us (1.036)
  blocking collectives: 94.5 us -> 118 us
  waiting for transfers between devices: 15.9 us -> 6.97 us
  starting transfers between devices: 38 us -> 30 us
    all_to_all x0 -> x2, blocking collectives: none -> 36.1 us  [the longest x1 24.5 us: per_device(): gap = lax.all_to_all(gap, (*Z, 'core'), 0, 0)]
    all_to_all x2 -> x1, blocking collectives: 25.6 us -> 12.6 us  [spread_sum(): return lax.all_to_all(part.reshape(NXY, BLOCK, BANDS), XY, 0, 0)]
    all_to_all x2 -> x1, starting transfers between devices: 13.5 us -> 3.57 us  [spread_sum(): return lax.all_to_all(part.reshape(NXY, BLOCK, BANDS), XY, 0, 0)]
    all_to_all x2 -> x1, waiting for transfers between devices: 15.1 us -> 6.1 us  [spread_sum(): return lax.all_to_all(part.reshape(NXY, BLOCK, BANDS), XY, 0, 0)]
    ppermute x1, starting transfers between devices: 2.92 us -> 4.87 us  [per_device(): quality = lax.ppermute(quality, AXES, to_receiver)]
  transfers between devices with their start and end apart: 5 -> 4, of which waited for: 3 -> 2; matrix products, arithmetic and copies ran while one was open for 0% -> 0% of each run, Pallas kernels for 2% -> 2%
where the time goes in v10:
time: 174 us; the launch traced here: 173 us
  blocking collectives  118 us (68%)
  starting transfers between devices  30 us (17%)
  Pallas kernels  15.9 us (9%)
  waiting for transfers between devices  6.97 us (4%)
    all_gather x1, blocking collectives, per_device(): near = lax.all_gather(sent, Z, axis=0)  32.1 us
    all_to_all x1, blocking collectives, per_device(): gap = lax.all_to_all(gap, (*Z, 'core'), 0, 0)  24.5 us
    all_gather x1, blocking collectives, per_device(): near = lax.all_gather(column, Z, axis=0)  23.2 us
    ppermute x2, starting transfers between devices, per_device(): far = lax.ppermute(near, 'core', swap)  21.6 us
    all_to_all x1, blocking collectives, per_device(): chunks = lax.all_to_all(chunks, XY, 0, 0)  13.6 us
    all_to_all x1, blocking collectives, spread_sum(): return lax.all_to_all(part.reshape(NXY, BLOCK, BANDS), XY, 0, 0)  12.6 us
    pallas_call x4, Pallas kernels, gain_product(): return call(kernel, product, 1 + len(args), smem=(0,), **work)(place, *args)  12.3 us
    all_to_all x1, blocking collectives, per_device(): gap = lax.all_to_all(gap, XY, 0, 0)  11.6 us
  transfers between devices with their start and end apart: 4, of which 2 were waited for; matrix products, arithmetic and copies ran while one was open for 0% of the time, Pallas kernels for 2%

profile of v10, /device:TPU:1, one launch (start us, length us, event | category | flops | bytes accessed | tf_op | source)
XLA Modules:
  0.0 173.4 jit_solution(8824019663864697003)
XLA Ops:
  0.6 0.0 copy-start.3
  0.6 0.0 copy-start.5
  0.7 0.0 copy-start.2
  0.7 0.0 copy-start.4
  0.7 0.6 copy-done.3
  1.3 0.0 copy-done.5
  1.3 0.0 copy-done.2
  1.3 0.0 copy-done.4
  1.4 0.0 copy-start
  1.4 0.7 copy-done
  2.1 0.1 shard_map.93.sent_ref
  2.2 32.1 %all-gather = f32[1152,128]{1,0:T(8,128)S(1)} all-gather(f32[72,128]{1,0:T(8,128)S(1)} %shard_map.93.sent_ref), channel_id=2, replica_groups=mesh['z2'=2,'z1'=2,'z0'=2,'x'=4,'y'=4,'zhi'=2,'core'=2] {'zhi','z2','z1'..., dimensions={0}, use_global_device_ids=true | all-gather | bytes 626688 | tf_op jit(solution)/shard_map/all_gather | solution.py:252
  34.3 10.1 %collective-permute-start = (f32[16,72,128]{2,1,0:T(8,128)S(1)}, f32[16,72,128]{2,1,0:T(8,128)S(1)}, u32[]{:S(2)}, u32[]{:S(2)}) collective-permute-start(f32[16,72,128]{2,1,0:T(8,128)S(1)} %bitcast.14), channel_id=1, source_target_pairs={{0,1},{1,0},{2,3},{3,2},{4,5},{5,4},{6,7},{7,6},{8,9},{9,8},{10,11... | collective-permute-start | bytes 1769480 | tf_op jit(solution)/shard_map/ppermute | solution.py:253
  45.1 0.1 stack.31.place_ref.refs_0_
  45.2 0.9 collective-permute-done.far_ref.refs_2_
  46.1 0.6 shard_map.94
  46.7 13.6 %all_to_all.25.chunk_ref = f32[16,24,128]{2,1,0:T(8,128)S(1)} all-to-all(f32[16,24,128]{2,1,0:T(8,128)S(1)} %shard_map.94), channel_id=1, replica_groups=mesh['z2'=2,'z1'=2,'z0'=2,'x'=4,'y'=4,'zhi'=2,'core'=2] {'x','y'}, dimensions={0} | all-to-all | bytes 393216 | tf_op jit(solution)/shard_map/all_to_all | solution.py:255
  60.3 0.7 shard_map.95
  61.0 3.1 %shard_map.96.refs_3_ = f32[1024,128]{1,0:T(8,128)S(1)} custom-call(s32[8]{0:T(128)S(1)} %stack.31.place_ref.refs_0_, bf16[16,1024]{1,0:T(8,128)(2,1)S(1)} %get-tuple-element.18.refs_1_, f32[16,72,128]{2,1,0:T(8,128)S(1)} %bitcast.16), custom_call_target="tpu_custom_call" | custom-call | flops 1073741824 | bytes 4194304 | tf_op jit(solution)/shard_map/pallas_call | solution.py:243
  64.1 2.7 %shard_map.97 = f32[1024,128]{1,0:T(8,128)S(1)} custom-call(s32[8]{0:T(128)S(1)} %stack.31.place_ref.refs_0_, bf16[16,1024]{1,0:T(8,128)(2,1)S(1)} %get-tuple-element.18.refs_1_, f32[16,72,128]{2,1,0:T(8,128)S(1)} %collective-permute-done.far_ref.refs_2_, f32[1024,128]{1,0:T(8,128)S(1)} %shard_map.96.refs_3_), custom_call_target="tpu_custom_call" | custom-call | flops 1073741824 | bytes 4194304 | tf_op jit(solution)/shard_map/pallas_call | solution.py:243
  66.8 0.0 copy-start.1
  66.8 12.6 %all_to_all.26.parts_ref = f32[16,64,128]{2,1,0:T(8,128)S(1)} all-to-all(f32[16,64,128]{2,1,0:T(8,128)S(1)} %bitcast.19), channel_id=1, replica_groups=mesh['z2'=2,'z1'=2,'z0'=2,'x'=4,'y'=4,'zhi'=2,'core'=2] {'x','y'}, dimensions={0} | all-to-all | bytes 1048576 | tf_op jit(solution)/shard_map/all_to_all | solution.py:248
  79.3 0.0 copy-done.1
  79.3 0.3 shard_map.98
  79.7 23.2 %all-gather.1 = f32[1152,128]{1,0:T(8,128)S(1)} all-gather(f32[72,128]{1,0:T(8,128)S(1)} %get-tuple-element.20), channel_id=3, replica_groups=mesh['z2'=2,'z1'=2,'z0'=2,'x'=4,'y'=4,'zhi'=2,'core'=2] {'zhi','z2','z1'..., dimensions={0}, use_global_device_ids=true | all-gather | bytes 626688 | tf_op jit(solution)/shard_map/all_gather | solution.py:265
  102.9 11.4 %collective-permute-start.1 = (f32[16,72,128]{2,1,0:T(8,128)S(1)}, f32[16,72,128]{2,1,0:T(8,128)S(1)}, u32[]{:S(2)}, u32[]{:S(2)}) collective-permute-start(f32[16,72,128]{2,1,0:T(8,128)S(1)} %bitcast.17), channel_id=1, source_target_pairs={{0,1},{1,0},{2,3},{3,2},{4,5},{5,4},{6,7},{7,6},{8,9},{9,8},{10,11... | collective-permute-start | bytes 1769480 | tf_op jit(solution)/shard_map/ppermute | solution.py:266
  114.3 3.1 %shard_map.99.refs_3_ = f32[1024,128]{1,0:T(8,128)S(1)} custom-call(s32[8]{0:T(128)S(1)} %stack.31.place_ref.refs_0_, bf16[16,1024]{1,0:T(8,128)(2,1)S(1)} %get-tuple-element.17.refs_1_, f32[16,72,128]{2,1,0:T(8,128)S(1)} %bitcast.18), custom_call_target="tpu_custom_call" | custom-call | flops 1073741824 | bytes 4194304 | tf_op jit(solution)/shard_map/pallas_call | solution.py:243
  117.4 0.0 collective-permute-done.1.refs_2_
  117.4 3.5 %shard_map.100 = f32[1024,128]{1,0:T(8,128)} custom-call(s32[8]{0:T(128)S(1)} %stack.31.place_ref.refs_0_, bf16[16,1024]{1,0:T(8,128)(2,1)S(1)} %get-tuple-element.17.refs_1_, f32[16,72,128]{2,1,0:T(8,128)S(1)} %collective-permute-done.1.refs_2_, f32[1024,128]{1,0:T(8,128)S(1)} %shard_map.99.refs_3_), custom_call_target="tpu_custom_call" | custom-call | flops 1073741824 | bytes 4194304 | tf_op jit(solution)/shard_map/pallas_call | solution.py:243
  120.9 3.6 %all-to-all-start.2 = ((f32[16,64,128]{2,1,0:T(8,128)}), f32[16,64,128]{2,1,0:T(8,128)S(1)}, u32[]{:S(2)}, u32[]{:S(2)}) async-start(f32[16,64,128]{2,1,0:T(8,128)} %bitcast.12), calls=%async_computation.2 | async-start | bytes 1048576 | tf_op jit(solution)/shard_map/all_to_all | solution.py:248
  124.4 4.9 %collective-permute-start.2 = (f32[64,128]{1,0:T(8,128)S(1)}, f32[64,128]{1,0:T(8,128)S(1)}, u32[]{:S(2)}, u32[]{:S(2)}) collective-permute-start(f32[64,128]{1,0:T(8,128)S(1)} %get-tuple-element.23), channel_id=1, source_target_pairs={{0,0},{16,1},{32,2},{48,3},{64,4},{80,5},{96,6},{112,7},{128,8},{1... | collective-permute-start | bytes 98312 | tf_op jit(solution)/shard_map/ppermute | solution.py:272
  129.3 6.1 %all-to-all-done.2.parts_ref = f32[16,64,128]{2,1,0:T(8,128)S(1)} async-done(((f32[16,64,128]{2,1,0:T(8,128)}), f32[16,64,128]{2,1,0:T(8,128)S(1)}, u32[]{:S(2)}, u32[]{:S(2)}) %all-to-all-start.2) | async-done | bytes 524320 | tf_op jit(solution)/shard_map/all_to_all | solution.py:248
  135.4 1.2 shard_map.101
  136.6 0.0 collective-permute-done.2.late_ref
  136.6 24.5 %all_to_all.27.parts_ref = f32[32,1,128]{2,1,0:T(1,128)S(1)} all-to-all(f32[32,1,128]{2,1,0:T(1,128)S(1)} %get-tuple-element.24), channel_id=1, replica_groups=mesh['z2'=2,'z1'=2,'z0'=2,'x'=4,'y'=4,'zhi'=2,'core'=2] {'zhi','z2','z1'..., dimensions={0} | all-to-all | bytes 32768 | tf_op jit(solution)/shard_map/all_to_all | solution.py:274
  161.2 11.6 %all_to_all.28.parts_ref = f32[16,1,128]{2,1,0:T(1,128)S(1)} all-to-all(f32[16,1,128]{2,1,0:T(1,128)S(1)} %shard_map.102), channel_id=1, replica_groups=mesh['z2'=2,'z1'=2,'z0'=2,'x'=4,'y'=4,'zhi'=2,'core'=2] {'x','y'}, dimensions={0} | all-to-all | bytes 16384 | tf_op jit(solution)/shard_map/all_to_all | solution.py:276
  172.8 0.6 shard_map.103
  (2 shorter events, 0.0 us)
Async XLA Ops:
  0.6 0.7 copy-start.3
  0.6 0.7 copy-start.5
  0.7 0.7 copy-start.2
  0.7 0.7 copy-start.4
  1.4 0.8 copy-start
  34.3 11.7 %collective-permute-start = (f32[16,72,128]{2,1,0:T(8,128)S(1)}, f32[16,72,128]{2,1,0:T(8,128)S(1)}, u32[]{:S(2)}, u32[]{:S(2)}) collective-permute-start(f32[16,72,128]{2,1,0:T(8,128)S(1)} %bitcast.14), channel_id=1, source_target_pairs={{0,1},{1,0},{2,3},{3,2},{4,5},{5,4},{6,7},{7,6},{8,9},{9,8},{10,11... | collective-permute-start | bytes 1769480 | tf_op jit(solution)/shard_map/ppermute | solution.py:253
  66.8 12.6 %copy-start.1 = (f32[64,128]{1,0:T(8,128)S(1)}, f32[64,128]{1,0:T(8,128)}, u32[]{:S(2)}) copy-start(f32[64,128]{1,0:T(8,128)} %powers_ref.5) | copy-start | bytes 98308
  102.9 14.5 %collective-permute-start.1 = (f32[16,72,128]{2,1,0:T(8,128)S(1)}, f32[16,72,128]{2,1,0:T(8,128)S(1)}, u32[]{:S(2)}, u32[]{:S(2)}) collective-permute-start(f32[16,72,128]{2,1,0:T(8,128)S(1)} %bitcast.17), channel_id=1, source_target_pairs={{0,1},{1,0},{2,3},{3,2},{4,5},{5,4},{6,7},{7,6},{8,9},{9,8},{10,11... | collective-permute-start | bytes 1769480 | tf_op jit(solution)/shard_map/ppermute | solution.py:266
  120.9 14.6 %all-to-all-start.2 = ((f32[16,64,128]{2,1,0:T(8,128)}), f32[16,64,128]{2,1,0:T(8,128)S(1)}, u32[]{:S(2)}, u32[]{:S(2)}) async-start(f32[16,64,128]{2,1,0:T(8,128)} %bitcast.12), calls=%async_computation.2 | async-start | bytes 1048576 | tf_op jit(solution)/shard_map/all_to_all | solution.py:248
  124.4 12.2 %collective-permute-start.2 = (f32[64,128]{1,0:T(8,128)S(1)}, f32[64,128]{1,0:T(8,128)S(1)}, u32[]{:S(2)}, u32[]{:S(2)}) collective-permute-start(f32[64,128]{1,0:T(8,128)S(1)} %get-tuple-element.23), channel_id=1, source_target_pairs={{0,0},{16,1},{32,2},{48,3},{64,4},{80,5},{96,6},{112,7},{128,8},{1... | collective-permute-start | bytes 98312 | tf_op jit(solution)/shard_map/ppermute | solution.py:272

commit v11 on v9

--- a/solution.py
+++ b/solution.py
@@ -212,13 +212,13 @@
     power_ref[...] = powers + step_size * (target - powers)
     gap = PEAK_POWER * jnp.maximum(gradient, 0.0) - gradient * powers
     gap = jnp.sum(gap, axis=0, keepdims=True)
-    for k in range(2 * NZ):
+    for k in range(2 * NXY):
         gap_ref[k] = gap
 
 
 def fold_kernel(parts_ref, out_ref):
     total = jnp.sum(parts_ref[...], axis=0)
-    for k in range(NXY):
+    for k in range(NZ):
         out_ref[k] = total
 
 
@@ -266,13 +266,13 @@
     far = lax.ppermute(near, "core", swap)
     parts = spread_sum(near, far, senders)
     gradient, new_power, gap = call(
-        finish_kernel, (block, block, shape(2 * NZ, 1, BANDS)), 4, smem=(0,)
+        finish_kernel, (block, block, shape(2 * NXY, 1, BANDS)), 4, smem=(0,)
     )(place, parts, own, powers)
 
     quality = lax.ppermute(quality, AXES, to_receiver)
-    gap = lax.all_to_all(gap, (*Z, "core"), 0, 0)
-    gap = call(fold_kernel, shape(NXY, 1, BANDS), 1)(gap)
-    gap = lax.all_to_all(gap, XY, 0, 0)
+    gap = lax.all_to_all(gap, (*XY, "core"), 0, 0)
+    gap = call(fold_kernel, shape(NZ, 1, BANDS), 1)(gap)
+    gap = lax.all_to_all(gap, Z, 0, 0)
     gap, quality = call(last_kernel, (shape(1, 1), block), 2)(gap, quality)
     return quality, gradient, new_power, gap.reshape(1)
 

time: 168 us -> 172 us (1.024)
  starting transfers between devices: 38 us -> 44.1 us
  waiting for transfers between devices: 15.9 us -> 13.9 us
    all_to_all x2, starting transfers between devices: 13.5 us -> 17.4 us  [the longest x1 11.6 us: per_device(): gap = lax.all_to_all(gap, Z, 0, 0)]
    ppermute x1, starting transfers between devices: 2.92 us -> 5.09 us  [per_device(): quality = lax.ppermute(quality, AXES, to_receiver)]
    all_to_all x2, waiting for transfers between devices: 15.1 us -> 13 us  [the longest x1 11.2 us: per_device(): gap = lax.all_to_all(gap, Z, 0, 0)]
where the time goes in v11:
time: 172 us; the launch traced here: 171 us
  blocking collectives  94.5 us (55%)
  starting transfers between devices  44.1 us (26%)
  Pallas kernels  15.7 us (9%)
  waiting for transfers between devices  13.9 us (8%)
    all_gather x1, blocking collectives, per_device(): near = lax.all_gather(sent, Z, axis=0)  32.1 us
    all_to_all x2, blocking collectives, spread_sum(): return lax.all_to_all(part.reshape(NXY, BLOCK, BANDS), XY, 0, 0)  25.6 us
    all_gather x1, blocking collectives, per_device(): near = lax.all_gather(column, Z, axis=0)  23.2 us
    ppermute x2, starting transfers between devices, per_device(): far = lax.ppermute(near, 'core', swap)  21.6 us
    all_to_all x1, blocking collectives, per_device(): chunks = lax.all_to_all(chunks, XY, 0, 0)  13.6 us
    all_to_all x1, starting transfers between devices, per_device(): gap = lax.all_to_all(gap, Z, 0, 0)  11.6 us
    pallas_call x4, Pallas kernels, gain_product(): return call(kernel, product, 1 + len(args), smem=(0,), **work)(place, *args)  11.5 us
    all_to_all x1, waiting for transfers between devices, per_device(): gap = lax.all_to_all(gap, Z, 0, 0)  11.2 us
  transfers between devices with their start and end apart: 5, of which 3 were waited for; matrix products, arithmetic and copies ran while one was open for 0% of the time, Pallas kernels for 2%

profile of v11, /device:TPU:1, one launch (start us, length us, event | category | flops | bytes accessed | tf_op | source)
XLA Modules:
  0.0 171.1 jit_solution(932834250257693711)
XLA Ops:
  0.6 0.0 copy-start.3
  0.6 0.0 copy-start.5
  0.7 0.0 copy-start.2
  0.7 0.0 copy-start.4
  0.7 0.6 copy-done.3
  1.3 0.0 copy-done.5
  1.3 0.0 copy-done.2
  1.3 0.0 copy-done.4
  1.4 0.0 copy-start
  1.4 0.7 copy-done
  2.1 0.1 shard_map.93.sent_ref
  2.2 32.1 %all-gather = f32[1152,128]{1,0:T(8,128)S(1)} all-gather(f32[72,128]{1,0:T(8,128)S(1)} %shard_map.93.sent_ref), channel_id=2, replica_groups=mesh['z2'=2,'z1'=2,'z0'=2,'x'=4,'y'=4,'zhi'=2,'core'=2] {'zhi','z2','z1'..., dimensions={0}, use_global_device_ids=true | all-gather | bytes 626688 | tf_op jit(solution)/shard_map/all_gather | solution.py:252
  34.3 10.1 %collective-permute-start = (f32[16,72,128]{2,1,0:T(8,128)S(1)}, f32[16,72,128]{2,1,0:T(8,128)S(1)}, u32[]{:S(2)}, u32[]{:S(2)}) collective-permute-start(f32[16,72,128]{2,1,0:T(8,128)S(1)} %bitcast.14), channel_id=1, source_target_pairs={{0,1},{1,0},{2,3},{3,2},{4,5},{5,4},{6,7},{7,6},{8,9},{9,8},{10,11... | collective-permute-start | bytes 1769480 | tf_op jit(solution)/shard_map/ppermute | solution.py:253
  45.1 0.1 stack.31.place_ref.refs_0_
  45.2 0.9 collective-permute-done.far_ref.refs_2_
  46.1 0.6 shard_map.94
  46.7 13.6 %all_to_all.25.chunk_ref = f32[16,24,128]{2,1,0:T(8,128)S(1)} all-to-all(f32[16,24,128]{2,1,0:T(8,128)S(1)} %shard_map.94), channel_id=1, replica_groups=mesh['z2'=2,'z1'=2,'z0'=2,'x'=4,'y'=4,'zhi'=2,'core'=2] {'x','y'}, dimensions={0} | all-to-all | bytes 393216 | tf_op jit(solution)/shard_map/all_to_all | solution.py:255
  60.3 0.7 shard_map.95
  61.0 3.1 %shard_map.96.refs_3_ = f32[1024,128]{1,0:T(8,128)S(1)} custom-call(s32[8]{0:T(128)S(1)} %stack.31.place_ref.refs_0_, bf16[16,1024]{1,0:T(8,128)(2,1)S(1)} %get-tuple-element.16.refs_1_, f32[16,72,128]{2,1,0:T(8,128)S(1)} %bitcast.16), custom_call_target="tpu_custom_call" | custom-call | flops 1073741824 | bytes 4194304 | tf_op jit(solution)/shard_map/pallas_call | solution.py:243
  64.1 2.7 %shard_map.97 = f32[1024,128]{1,0:T(8,128)S(1)} custom-call(s32[8]{0:T(128)S(1)} %stack.31.place_ref.refs_0_, bf16[16,1024]{1,0:T(8,128)(2,1)S(1)} %get-tuple-element.16.refs_1_, f32[16,72,128]{2,1,0:T(8,128)S(1)} %collective-permute-done.far_ref.refs_2_, f32[1024,128]{1,0:T(8,128)S(1)} %shard_map.96.refs_3_), custom_call_target="tpu_custom_call" | custom-call | flops 1073741824 | bytes 4194304 | tf_op jit(solution)/shard_map/pallas_call | solution.py:243
  66.8 0.0 copy-start.1
  66.8 12.6 %all_to_all.26.parts_ref = f32[16,64,128]{2,1,0:T(8,128)S(1)} all-to-all(f32[16,64,128]{2,1,0:T(8,128)S(1)} %bitcast.19), channel_id=1, replica_groups=mesh['z2'=2,'z1'=2,'z0'=2,'x'=4,'y'=4,'zhi'=2,'core'=2] {'x','y'}, dimensions={0} | all-to-all | bytes 1048576 | tf_op jit(solution)/shard_map/all_to_all | solution.py:248
  79.3 0.0 copy-done.1
  79.3 0.3 shard_map.98
  79.7 23.2 %all-gather.1 = f32[1152,128]{1,0:T(8,128)S(1)} all-gather(f32[72,128]{1,0:T(8,128)S(1)} %get-tuple-element.18), channel_id=3, replica_groups=mesh['z2'=2,'z1'=2,'z0'=2,'x'=4,'y'=4,'zhi'=2,'core'=2] {'zhi','z2','z1'..., dimensions={0}, use_global_device_ids=true | all-gather | bytes 626688 | tf_op jit(solution)/shard_map/all_gather | solution.py:265
  102.9 11.4 %collective-permute-start.1 = (f32[16,72,128]{2,1,0:T(8,128)S(1)}, f32[16,72,128]{2,1,0:T(8,128)S(1)}, u32[]{:S(2)}, u32[]{:S(2)}) collective-permute-start(f32[16,72,128]{2,1,0:T(8,128)S(1)} %bitcast.17), channel_id=1, source_target_pairs={{0,1},{1,0},{2,3},{3,2},{4,5},{5,4},{6,7},{7,6},{8,9},{9,8},{10,11... | collective-permute-start | bytes 1769480 | tf_op jit(solution)/shard_map/ppermute | solution.py:266
  114.3 3.1 %shard_map.99.refs_3_ = f32[1024,128]{1,0:T(8,128)S(1)} custom-call(s32[8]{0:T(128)S(1)} %stack.31.place_ref.refs_0_, bf16[16,1024]{1,0:T(8,128)(2,1)S(1)} %get-tuple-element.15.refs_1_, f32[16,72,128]{2,1,0:T(8,128)S(1)} %bitcast.18), custom_call_target="tpu_custom_call" | custom-call | flops 1073741824 | bytes 4194304 | tf_op jit(solution)/shard_map/pallas_call | solution.py:243
  117.4 0.0 collective-permute-done.1.refs_2_
  117.4 2.7 %shard_map.100 = f32[1024,128]{1,0:T(8,128)S(1)} custom-call(s32[8]{0:T(128)S(1)} %stack.31.place_ref.refs_0_, bf16[16,1024]{1,0:T(8,128)(2,1)S(1)} %get-tuple-element.15.refs_1_, f32[16,72,128]{2,1,0:T(8,128)S(1)} %collective-permute-done.1.refs_2_, f32[1024,128]{1,0:T(8,128)S(1)} %shard_map.99.refs_3_), custom_call_target="tpu_custom_call" | custom-call | flops 1073741824 | bytes 4194304 | tf_op jit(solution)/shard_map/pallas_call | solution.py:243
  120.1 13.0 %all_to_all.27.parts_ref = f32[16,64,128]{2,1,0:T(8,128)S(1)} all-to-all(f32[16,64,128]{2,1,0:T(8,128)S(1)} %bitcast.20), channel_id=1, replica_groups=mesh['z2'=2,'z1'=2,'z0'=2,'x'=4,'y'=4,'zhi'=2,'core'=2] {'x','y'}, dimensions={0} | all-to-all | bytes 1048576 | tf_op jit(solution)/shard_map/all_to_all | solution.py:248
  133.1 1.2 shard_map.101
  134.3 5.9 %all-to-all-start.3 = ((f32[32,1,128]{2,1,0:T(1,128)}), f32[32,1,128]{2,1,0:T(1,128)S(1)}, u32[]{:S(2)}, u32[]{:S(2)}) async-start(f32[32,1,128]{2,1,0:T(1,128)} %get-tuple-element.20), calls=%async_computation.3 | async-start | bytes 32768 | tf_op jit(solution)/shard_map/all_to_all | solution.py:273
  140.1 5.1 %collective-permute-start.2 = (f32[64,128]{1,0:T(8,128)S(1)}, f32[64,128]{1,0:T(8,128)S(1)}, u32[]{:S(2)}, u32[]{:S(2)}) collective-permute-start(f32[64,128]{1,0:T(8,128)S(1)} %get-tuple-element.21), channel_id=1, source_target_pairs={{0,0},{16,1},{32,2},{48,3},{64,4},{80,5},{96,6},{112,7},{128,8},{1... | collective-permute-start | bytes 98312 | tf_op jit(solution)/shard_map/ppermute | solution.py:272
  145.2 1.8 %all-to-all-done.3.parts_ref = f32[32,1,128]{2,1,0:T(1,128)S(1)} async-done(((f32[32,1,128]{2,1,0:T(1,128)}), f32[32,1,128]{2,1,0:T(1,128)S(1)}, u32[]{:S(2)}, u32[]{:S(2)}) %all-to-all-start.3) | async-done | bytes 16416 | tf_op jit(solution)/shard_map/all_to_all | solution.py:273
  147.1 0.6 shard_map.102
  147.7 11.6 %all-to-all-start.4 = ((f32[16,1,128]{2,1,0:T(1,128)}), f32[16,1,128]{2,1,0:T(1,128)S(1)}, u32[]{:S(2)}, u32[]{:S(2)}) async-start(f32[16,1,128]{2,1,0:T(1,128)} %shard_map.102), calls=%async_computation.4 | async-start | bytes 16384 | tf_op jit(solution)/shard_map/all_to_all | solution.py:275
  159.3 0.0 collective-permute-done.2.late_ref
  159.3 11.2 %all-to-all-done.4.parts_ref = f32[16,1,128]{2,1,0:T(1,128)S(1)} async-done(((f32[16,1,128]{2,1,0:T(1,128)}), f32[16,1,128]{2,1,0:T(1,128)S(1)}, u32[]{:S(2)}, u32[]{:S(2)}) %all-to-all-start.4) | async-done | bytes 8224 | tf_op jit(solution)/shard_map/all_to_all | solution.py:275
  170.5 0.6 shard_map.103
  (1 shorter events, 0.0 us)
Async XLA Ops:
  0.6 0.7 copy-start.3
  0.6 0.7 copy-start.5
  0.7 0.7 copy-start.2
  0.7 0.7 copy-start.4
  1.4 0.8 copy-start
  34.3 11.7 %collective-permute-start = (f32[16,72,128]{2,1,0:T(8,128)S(1)}, f32[16,72,128]{2,1,0:T(8,128)S(1)}, u32[]{:S(2)}, u32[]{:S(2)}) collective-permute-start(f32[16,72,128]{2,1,0:T(8,128)S(1)} %bitcast.14), channel_id=1, source_target_pairs={{0,1},{1,0},{2,3},{3,2},{4,5},{5,4},{6,7},{7,6},{8,9},{9,8},{10,11... | collective-permute-start | bytes 1769480 | tf_op jit(solution)/shard_map/ppermute | solution.py:253
  66.8 12.6 %copy-start.1 = (f32[64,128]{1,0:T(8,128)S(1)}, f32[64,128]{1,0:T(8,128)}, u32[]{:S(2)}) copy-start(f32[64,128]{1,0:T(8,128)} %powers_ref.5) | copy-start | bytes 98308
  102.9 14.5 %collective-permute-start.1 = (f32[16,72,128]{2,1,0:T(8,128)S(1)}, f32[16,72,128]{2,1,0:T(8,128)S(1)}, u32[]{:S(2)}, u32[]{:S(2)}) collective-permute-start(f32[16,72,128]{2,1,0:T(8,128)S(1)} %bitcast.17), channel_id=1, source_target_pairs={{0,1},{1,0},{2,3},{3,2},{4,5},{5,4},{6,7},{7,6},{8,9},{9,8},{10,11... | collective-permute-start | bytes 1769480 | tf_op jit(solution)/shard_map/ppermute | solution.py:266
  134.3 12.8 %all-to-all-start.3 = ((f32[32,1,128]{2,1,0:T(1,128)}), f32[32,1,128]{2,1,0:T(1,128)S(1)}, u32[]{:S(2)}, u32[]{:S(2)}) async-start(f32[32,1,128]{2,1,0:T(1,128)} %get-tuple-element.20), calls=%async_computation.3 | async-start | bytes 32768 | tf_op jit(solution)/shard_map/all_to_all | solution.py:273
  140.1 19.1 %collective-permute-start.2 = (f32[64,128]{1,0:T(8,128)S(1)}, f32[64,128]{1,0:T(8,128)S(1)}, u32[]{:S(2)}, u32[]{:S(2)}) collective-permute-start(f32[64,128]{1,0:T(8,128)S(1)} %get-tuple-element.21), channel_id=1, source_target_pairs={{0,0},{16,1},{32,2},{48,3},{64,4},{80,5},{96,6},{112,7},{128,8},{1... | collective-permute-start | bytes 98312 | tf_op jit(solution)/shard_map/ppermute | solution.py:272
  147.7 22.8 %all-to-all-start.4 = ((f32[16,1,128]{2,1,0:T(1,128)}), f32[16,1,128]{2,1,0:T(1,128)S(1)}, u32[]{:S(2)}, u32[]{:S(2)}) async-start(f32[16,1,128]{2,1,0:T(1,128)} %shard_map.102), calls=%async_computation.4 | async-start | bytes 16384 | tf_op jit(solution)/shard_map/all_to_all | solution.py:275

commit v12 on v11

--- a/solution.py
+++ b/solution.py
@@ -212,13 +212,13 @@
     power_ref[...] = powers + step_size * (target - powers)
     gap = PEAK_POWER * jnp.maximum(gradient, 0.0) - gradient * powers
     gap = jnp.sum(gap, axis=0, keepdims=True)
-    for k in range(2 * NXY):
+    for k in range(NZ):
         gap_ref[k] = gap
 
 
 def fold_kernel(parts_ref, out_ref):
     total = jnp.sum(parts_ref[...], axis=0)
-    for k in range(NZ):
+    for k in range(2 * NXY):
         out_ref[k] = total
 
 
@@ -266,13 +266,13 @@
     far = lax.ppermute(near, "core", swap)
     parts = spread_sum(near, far, senders)
     gradient, new_power, gap = call(
-        finish_kernel, (block, block, shape(2 * NXY, 1, BANDS)), 4, smem=(0,)
+        finish_kernel, (block, block, shape(NZ, 1, BANDS)), 4, smem=(0,)
     )(place, parts, own, powers)
 
     quality = lax.ppermute(quality, AXES, to_receiver)
+    gap = lax.all_to_all(gap, Z, 0, 0)
+    gap = call(fold_kernel, shape(2 * NXY, 1, BANDS), 1)(gap)
     gap = lax.all_to_all(gap, (*XY, "core"), 0, 0)
-    gap = call(fold_kernel, shape(NZ, 1, BANDS), 1)(gap)
-    gap = lax.all_to_all(gap, Z, 0, 0)
     gap, quality = call(last_kernel, (shape(1, 1), block), 2)(gap, quality)
     return quality, gradient, new_power, gap.reshape(1)
 

time: 172 us -> 170 us (0.988)
    all_to_all x1, waiting for transfers between devices: 11.2 us -> 5.95 us  [per_device(): gap = lax.all_to_all(gap, Z, 0, 0)]
    all_to_all x1, waiting for transfers between devices: 1.83 us -> 6.86 us  [per_device(): gap = lax.all_to_all(gap, (*XY, 'core'), 0, 0)]
    all_to_all x1, starting transfers between devices: 11.6 us -> 7.42 us  [per_device(): gap = lax.all_to_all(gap, Z, 0, 0)]
    all_to_all x1, starting transfers between devices: 5.85 us -> 8.31 us  [per_device(): gap = lax.all_to_all(gap, (*XY, 'core'), 0, 0)]
where the time goes in v12:
time: 170 us; the launch traced here: 169 us
  blocking collectives  94.5 us (56%)
  starting transfers between devices  42.6 us (25%)
  Pallas kernels  15.7 us (9%)
  waiting for transfers between devices  13.7 us (8%)
    all_gather x1, blocking collectives, per_device(): near = lax.all_gather(sent, Z, axis=0)  32.1 us
    all_to_all x2, blocking collectives, spread_sum(): return lax.all_to_all(part.reshape(NXY, BLOCK, BANDS), XY, 0, 0)  25.6 us
    all_gather x1, blocking collectives, per_device(): near = lax.all_gather(column, Z, axis=0)  23.2 us
    ppermute x2, starting transfers between devices, per_device(): far = lax.ppermute(near, 'core', swap)  21.6 us
    all_to_all x1, blocking collectives, per_device(): chunks = lax.all_to_all(chunks, XY, 0, 0)  13.6 us
    pallas_call x4, Pallas kernels, gain_product(): return call(kernel, product, 1 + len(args), smem=(0,), **work)(place, *args)  11.5 us
    all_to_all x1, starting transfers between devices, per_device(): gap = lax.all_to_all(gap, (*XY, 'core'), 0, 0)  8.31 us
    all_to_all x1, starting transfers between devices, per_device(): gap = lax.all_to_all(gap, Z, 0, 0)  7.42 us
  transfers between devices with their start and end apart: 5, of which 3 were waited for; matrix products, arithmetic and copies ran while one was open for 0% of the time, Pallas kernels for 2%

profile of v12, /device:TPU:1, one launch (start us, length us, event | category | flops | bytes accessed | tf_op | source)
XLA Modules:
  0.0 169.4 jit_solution(5676488824100229443)
XLA Ops:
  0.6 0.0 copy-start.3
  0.6 0.0 copy-start.5
  0.7 0.0 copy-start.2
  0.7 0.0 copy-start.4
  0.7 0.6 copy-done.3
  1.3 0.0 copy-done.5
  1.3 0.0 copy-done.2
  1.3 0.0 copy-done.4
  1.4 0.0 copy-start
  1.4 0.7 copy-done
  2.1 0.1 shard_map.93.sent_ref
  2.2 32.1 %all-gather = f32[1152,128]{1,0:T(8,128)S(1)} all-gather(f32[72,128]{1,0:T(8,128)S(1)} %shard_map.93.sent_ref), channel_id=2, replica_groups=mesh['z2'=2,'z1'=2,'z0'=2,'x'=4,'y'=4,'zhi'=2,'core'=2] {'zhi','z2','z1'..., dimensions={0}, use_global_device_ids=true | all-gather | bytes 626688 | tf_op jit(solution)/shard_map/all_gather | solution.py:252
  34.3 10.1 %collective-permute-start = (f32[16,72,128]{2,1,0:T(8,128)S(1)}, f32[16,72,128]{2,1,0:T(8,128)S(1)}, u32[]{:S(2)}, u32[]{:S(2)}) collective-permute-start(f32[16,72,128]{2,1,0:T(8,128)S(1)} %bitcast.14), channel_id=1, source_target_pairs={{0,1},{1,0},{2,3},{3,2},{4,5},{5,4},{6,7},{7,6},{8,9},{9,8},{10,11... | collective-permute-start | bytes 1769480 | tf_op jit(solution)/shard_map/ppermute | solution.py:253
  45.1 0.1 stack.31.place_ref.refs_0_
  45.2 0.9 collective-permute-done.far_ref.refs_2_
  46.1 0.6 shard_map.94
  46.7 13.6 %all_to_all.25.chunk_ref = f32[16,24,128]{2,1,0:T(8,128)S(1)} all-to-all(f32[16,24,128]{2,1,0:T(8,128)S(1)} %shard_map.94), channel_id=1, replica_groups=mesh['z2'=2,'z1'=2,'z0'=2,'x'=4,'y'=4,'zhi'=2,'core'=2] {'x','y'}, dimensions={0} | all-to-all | bytes 393216 | tf_op jit(solution)/shard_map/all_to_all | solution.py:255
  60.3 0.7 shard_map.95
  61.0 3.1 %shard_map.96.refs_3_ = f32[1024,128]{1,0:T(8,128)S(1)} custom-call(s32[8]{0:T(128)S(1)} %stack.31.place_ref.refs_0_, bf16[16,1024]{1,0:T(8,128)(2,1)S(1)} %get-tuple-element.16.refs_1_, f32[16,72,128]{2,1,0:T(8,128)S(1)} %bitcast.16), custom_call_target="tpu_custom_call" | custom-call | flops 1073741824 | bytes 4194304 | tf_op jit(solution)/shard_map/pallas_call | solution.py:243
  64.1 2.7 %shard_map.97 = f32[1024,128]{1,0:T(8,128)S(1)} custom-call(s32[8]{0:T(128)S(1)} %stack.31.place_ref.refs_0_, bf16[16,1024]{1,0:T(8,128)(2,1)S(1)} %get-tuple-element.16.refs_1_, f32[16,72,128]{2,1,0:T(8,128)S(1)} %collective-permute-done.far_ref.refs_2_, f32[1024,128]{1,0:T(8,128)S(1)} %shard_map.96.refs_3_), custom_call_target="tpu_custom_call" | custom-call | flops 1073741824 | bytes 4194304 | tf_op jit(solution)/shard_map/pallas_call | solution.py:243
  66.8 0.0 copy-start.1
  66.8 12.6 %all_to_all.26.parts_ref = f32[16,64,128]{2,1,0:T(8,128)S(1)} all-to-all(f32[16,64,128]{2,1,0:T(8,128)S(1)} %bitcast.19), channel_id=1, replica_groups=mesh['z2'=2,'z1'=2,'z0'=2,'x'=4,'y'=4,'zhi'=2,'core'=2] {'x','y'}, dimensions={0} | all-to-all | bytes 1048576 | tf_op jit(solution)/shard_map/all_to_all | solution.py:248
  79.3 0.0 copy-done.1
  79.3 0.3 shard_map.98
  79.7 23.2 %all-gather.1 = f32[1152,128]{1,0:T(8,128)S(1)} all-gather(f32[72,128]{1,0:T(8,128)S(1)} %get-tuple-element.18), channel_id=3, replica_groups=mesh['z2'=2,'z1'=2,'z0'=2,'x'=4,'y'=4,'zhi'=2,'core'=2] {'zhi','z2','z1'..., dimensions={0}, use_global_device_ids=true | all-gather | bytes 626688 | tf_op jit(solution)/shard_map/all_gather | solution.py:265
  102.9 11.4 %collective-permute-start.1 = (f32[16,72,128]{2,1,0:T(8,128)S(1)}, f32[16,72,128]{2,1,0:T(8,128)S(1)}, u32[]{:S(2)}, u32[]{:S(2)}) collective-permute-start(f32[16,72,128]{2,1,0:T(8,128)S(1)} %bitcast.17), channel_id=1, source_target_pairs={{0,1},{1,0},{2,3},{3,2},{4,5},{5,4},{6,7},{7,6},{8,9},{9,8},{10,11... | collective-permute-start | bytes 1769480 | tf_op jit(solution)/shard_map/ppermute | solution.py:266
  114.3 3.1 %shard_map.99.refs_3_ = f32[1024,128]{1,0:T(8,128)S(1)} custom-call(s32[8]{0:T(128)S(1)} %stack.31.place_ref.refs_0_, bf16[16,1024]{1,0:T(8,128)(2,1)S(1)} %get-tuple-element.15.refs_1_, f32[16,72,128]{2,1,0:T(8,128)S(1)} %bitcast.18), custom_call_target="tpu_custom_call" | custom-call | flops 1073741824 | bytes 4194304 | tf_op jit(solution)/shard_map/pallas_call | solution.py:243
  117.4 0.0 collective-permute-done.1.refs_2_
  117.4 2.7 %shard_map.100 = f32[1024,128]{1,0:T(8,128)S(1)} custom-call(s32[8]{0:T(128)S(1)} %stack.31.place_ref.refs_0_, bf16[16,1024]{1,0:T(8,128)(2,1)S(1)} %get-tuple-element.15.refs_1_, f32[16,72,128]{2,1,0:T(8,128)S(1)} %collective-permute-done.1.refs_2_, f32[1024,128]{1,0:T(8,128)S(1)} %shard_map.99.refs_3_), custom_call_target="tpu_custom_call" | custom-call | flops 1073741824 | bytes 4194304 | tf_op jit(solution)/shard_map/pallas_call | solution.py:243
  120.1 13.0 %all_to_all.27.parts_ref = f32[16,64,128]{2,1,0:T(8,128)S(1)} all-to-all(f32[16,64,128]{2,1,0:T(8,128)S(1)} %bitcast.20), channel_id=1, replica_groups=mesh['z2'=2,'z1'=2,'z0'=2,'x'=4,'y'=4,'zhi'=2,'core'=2] {'x','y'}, dimensions={0} | all-to-all | bytes 1048576 | tf_op jit(solution)/shard_map/all_to_all | solution.py:248
  133.1 1.2 shard_map.101
  134.3 7.4 %all-to-all-start.3 = ((f32[16,1,128]{2,1,0:T(1,128)}), f32[16,1,128]{2,1,0:T(1,128)S(1)}, u32[]{:S(2)}, u32[]{:S(2)}) async-start(f32[16,1,128]{2,1,0:T(1,128)} %get-tuple-element.20), calls=%async_computation.3 | async-start | bytes 16384 | tf_op jit(solution)/shard_map/all_to_all | solution.py:273
  141.7 5.3 %collective-permute-start.2 = (f32[64,128]{1,0:T(8,128)S(1)}, f32[64,128]{1,0:T(8,128)S(1)}, u32[]{:S(2)}, u32[]{:S(2)}) collective-permute-start(f32[64,128]{1,0:T(8,128)S(1)} %get-tuple-element.21), channel_id=1, source_target_pairs={{0,0},{16,1},{32,2},{48,3},{64,4},{80,5},{96,6},{112,7},{128,8},{1... | collective-permute-start | bytes 98312 | tf_op jit(solution)/shard_map/ppermute | solution.py:272
  147.0 5.9 %all-to-all-done.3.parts_ref = f32[16,1,128]{2,1,0:T(1,128)S(1)} async-done(((f32[16,1,128]{2,1,0:T(1,128)}), f32[16,1,128]{2,1,0:T(1,128)S(1)}, u32[]{:S(2)}, u32[]{:S(2)}) %all-to-all-start.3) | async-done | bytes 8224 | tf_op jit(solution)/shard_map/all_to_all | solution.py:273
  152.9 0.6 shard_map.102
  153.6 8.3 %all-to-all-start.4 = ((f32[32,1,128]{2,1,0:T(1,128)}), f32[32,1,128]{2,1,0:T(1,128)S(1)}, u32[]{:S(2)}, u32[]{:S(2)}) async-start(f32[32,1,128]{2,1,0:T(1,128)} %shard_map.102), calls=%async_computation.4 | async-start | bytes 32768 | tf_op jit(solution)/shard_map/all_to_all | solution.py:275
  161.9 0.0 collective-permute-done.2.late_ref
  161.9 6.9 %all-to-all-done.4.parts_ref = f32[32,1,128]{2,1,0:T(1,128)S(1)} async-done(((f32[32,1,128]{2,1,0:T(1,128)}), f32[32,1,128]{2,1,0:T(1,128)S(1)}, u32[]{:S(2)}, u32[]{:S(2)}) %all-to-all-start.4) | async-done | bytes 16416 | tf_op jit(solution)/shard_map/all_to_all | solution.py:275
  168.8 0.6 shard_map.103
  (1 shorter events, 0.0 us)
Async XLA Ops:
  0.6 0.7 copy-start.3
  0.6 0.7 copy-start.5
  0.7 0.7 copy-start.2
  0.7 0.7 copy-start.4
  1.4 0.8 copy-start
  34.3 11.7 %collective-permute-start = (f32[16,72,128]{2,1,0:T(8,128)S(1)}, f32[16,72,128]{2,1,0:T(8,128)S(1)}, u32[]{:S(2)}, u32[]{:S(2)}) collective-permute-start(f32[16,72,128]{2,1,0:T(8,128)S(1)} %bitcast.14), channel_id=1, source_target_pairs={{0,1},{1,0},{2,3},{3,2},{4,5},{5,4},{6,7},{7,6},{8,9},{9,8},{10,11... | collective-permute-start | bytes 1769480 | tf_op jit(solution)/shard_map/ppermute | solution.py:253
  66.8 12.6 %copy-start.1 = (f32[64,128]{1,0:T(8,128)S(1)}, f32[64,128]{1,0:T(8,128)}, u32[]{:S(2)}) copy-start(f32[64,128]{1,0:T(8,128)} %powers_ref.5) | copy-start | bytes 98308
  102.9 14.5 %collective-permute-start.1 = (f32[16,72,128]{2,1,0:T(8,128)S(1)}, f32[16,72,128]{2,1,0:T(8,128)S(1)}, u32[]{:S(2)}, u32[]{:S(2)}) collective-permute-start(f32[16,72,128]{2,1,0:T(8,128)S(1)} %bitcast.17), channel_id=1, source_target_pairs={{0,1},{1,0},{2,3},{3,2},{4,5},{5,4},{6,7},{7,6},{8,9},{9,8},{10,11... | collective-permute-start | bytes 1769480 | tf_op jit(solution)/shard_map/ppermute | solution.py:266
  134.3 18.7 %all-to-all-start.3 = ((f32[16,1,128]{2,1,0:T(1,128)}), f32[16,1,128]{2,1,0:T(1,128)S(1)}, u32[]{:S(2)}, u32[]{:S(2)}) async-start(f32[16,1,128]{2,1,0:T(1,128)} %get-tuple-element.20), calls=%async_computation.3 | async-start | bytes 16384 | tf_op jit(solution)/shard_map/all_to_all | solution.py:273
  141.7 20.2 %collective-permute-start.2 = (f32[64,128]{1,0:T(8,128)S(1)}, f32[64,128]{1,0:T(8,128)S(1)}, u32[]{:S(2)}, u32[]{:S(2)}) collective-permute-start(f32[64,128]{1,0:T(8,128)S(1)} %get-tuple-element.21), channel_id=1, source_target_pairs={{0,0},{16,1},{32,2},{48,3},{64,4},{80,5},{96,6},{112,7},{128,8},{1... | collective-permute-start | bytes 98312 | tf_op jit(solution)/shard_map/ppermute | solution.py:272
  153.6 15.2 %all-to-all-start.4 = ((f32[32,1,128]{2,1,0:T(1,128)}), f32[32,1,128]{2,1,0:T(1,128)S(1)}, u32[]{:S(2)}, u32[]{:S(2)}) async-start(f32[32,1,128]{2,1,0:T(1,128)} %shard_map.102), calls=%async_computation.4 | async-start | bytes 32768 | tf_op jit(solution)/shard_map/all_to_all | solution.py:275

commit v13 on v9

--- a/solution.py
+++ b/solution.py
@@ -133,7 +133,6 @@
 def gain_kernel(far, place_ref, plane_ref, column_ref, *rest):
     *before, total_ref = rest
     x, y, z0, z2, z1, zhi, core = (place_ref[i] for i in range(7))
-    rows = plane_ref[...]
     columns = spread(column_ref)
     value_high, value_low = split(column_ref[:, 0:BLOCK, :].reshape(HALF, BANDS))
     values = jnp.concatenate([value_high, value_low], axis=1)
@@ -141,8 +140,11 @@
     row_base = zhi * 4096 + core * 2048 + (z2 * 4 + z1 * 2 + z0) * 256
     col_base = y * 8192 + core * 2048 + x * 64
     tile = 128
-    for r in range(0, ROWS, tile):
+    mine = (x * 4 + y) >> 1
+    for turn in range(ROWS // tile):
+        r = turn * tile if far else pl.multiple_of(((mine + turn) & 7) * tile, tile)
         row = lax.broadcasted_iota(jnp.int32, (tile, tile), 0) + r
+        row_features = plane_ref[:, pl.ds(r, tile)]
         block = row >> 6
         row_id = row_base + (block & 3) * 8192 + (block >> 2) * 64 + (row & 63)
         highs, lows = [], []
@@ -151,14 +153,14 @@
             zed = col >> 6
             col_id = col_base + (zed >> 3) * 4096 + (zed & 7) * 256 + (col & 63)
             square = lax.dot_general(
-                rows[:, r : r + tile],
+                row_features,
                 columns[:, c : c + tile],
                 (((0,), (0,)), ((), ())),
                 preferred_element_type=F32,
             )
             guess = pl.reciprocal(square, approx=True)
             gain = guess * (2.0 - square * guess)
-            if not far:
+            if not far and turn == 0:
                 gain = jnp.where(row_id == col_id, 0.0, gain)
             high, low = split(gain)
             highs.append(high)
@@ -167,8 +169,8 @@
         product = jnp.dot(gains, values, preferred_element_type=F32)
         part = product[:, :BANDS] + product[:, BANDS:]
         for ref in before:
-            part = part + ref[r : r + tile, :]
-        total_ref[r : r + tile, :] = part
+            part = part + ref[pl.ds(r, tile), :]
+        total_ref[pl.ds(r, tile), :] = part
 
 
 def add_blocks(ref):

time: 168 us -> 168 us (level)
  no operation moved by 1% of the time
where the time goes in v13:
time: 168 us; the launch traced here: 166 us
  blocking collectives  94.5 us (56%)
  starting transfers between devices  38.1 us (23%)
  waiting for transfers between devices  15.9 us (9%)
  Pallas kernels  14.9 us (9%)
    all_gather x1, blocking collectives, per_device(): near = lax.all_gather(sent, Z, axis=0)  32.1 us
    all_to_all x2, blocking collectives, spread_sum(): return lax.all_to_all(part.reshape(NXY, BLOCK, BANDS), XY, 0, 0)  25.6 us
    all_gather x1, blocking collectives, per_device(): near = lax.all_gather(column, Z, axis=0)  23.2 us
    ppermute x2, starting transfers between devices, per_device(): far = lax.ppermute(near, 'core', swap)  21.5 us
    all_to_all x1, blocking collectives, per_device(): chunks = lax.all_to_all(chunks, XY, 0, 0)  13.6 us
    pallas_call x4, Pallas kernels, gain_product(): return call(kernel, product, 1 + len(args), smem=(0,), **work)(place, *args)  10.8 us
    all_to_all x1, starting transfers between devices, per_device(): gap = lax.all_to_all(gap, (*Z, 'core'), 0, 0)  10.1 us
    all_to_all x1, waiting for transfers between devices, per_device(): gap = lax.all_to_all(gap, (*Z, 'core'), 0, 0)  8.79 us
  transfers between devices with their start and end apart: 5, of which 3 were waited for; matrix products, arithmetic and copies ran while one was open for 0% of the time, Pallas kernels for 2%

profile of v13, /device:TPU:1, one launch (start us, length us, event | category | flops | bytes accessed | tf_op | source)
XLA Modules:
  0.0 166.4 jit_solution(11528048494583710749)
XLA Ops:
  0.6 0.0 copy-start.3
  0.6 0.0 copy-start.5
  0.7 0.0 copy-start.2
  0.7 0.0 copy-start.4
  0.7 0.6 copy-done.3
  1.3 0.0 copy-done.5
  1.3 0.0 copy-done.2
  1.3 0.0 copy-done.4
  1.4 0.0 copy-start
  1.4 0.7 copy-done
  2.1 0.1 shard_map.93.sent_ref
  2.2 32.1 %all-gather = f32[1152,128]{1,0:T(8,128)S(1)} all-gather(f32[72,128]{1,0:T(8,128)S(1)} %shard_map.93.sent_ref), channel_id=2, replica_groups=mesh['z2'=2,'z1'=2,'z0'=2,'x'=4,'y'=4,'zhi'=2,'core'=2] {'zhi','z2','z1'..., dimensions={0}, use_global_device_ids=true | all-gather | bytes 626688 | tf_op jit(solution)/shard_map/all_gather | solution.py:254
  34.3 10.1 %collective-permute-start = (f32[16,72,128]{2,1,0:T(8,128)S(1)}, f32[16,72,128]{2,1,0:T(8,128)S(1)}, u32[]{:S(2)}, u32[]{:S(2)}) collective-permute-start(f32[16,72,128]{2,1,0:T(8,128)S(1)} %bitcast.14), channel_id=1, source_target_pairs={{0,1},{1,0},{2,3},{3,2},{4,5},{5,4},{6,7},{7,6},{8,9},{9,8},{10,11... | collective-permute-start | bytes 1769480 | tf_op jit(solution)/shard_map/ppermute | solution.py:255
  45.1 0.1 stack.31.place_ref.refs_0_
  45.2 0.9 collective-permute-done.far_ref.refs_2_
  46.1 0.6 shard_map.94
  46.7 13.6 %all_to_all.25.chunk_ref = f32[16,24,128]{2,1,0:T(8,128)S(1)} all-to-all(f32[16,24,128]{2,1,0:T(8,128)S(1)} %shard_map.94), channel_id=1, replica_groups=mesh['z2'=2,'z1'=2,'z0'=2,'x'=4,'y'=4,'zhi'=2,'core'=2] {'x','y'}, dimensions={0} | all-to-all | bytes 393216 | tf_op jit(solution)/shard_map/all_to_all | solution.py:257
  60.3 0.7 shard_map.95
  61.0 2.7 %shard_map.96.refs_3_ = f32[1024,128]{1,0:T(8,128)S(1)} custom-call(s32[8]{0:T(128)S(1)} %stack.31.place_ref.refs_0_, bf16[16,1024]{1,0:T(8,128)(2,1)S(1)} %get-tuple-element.16.refs_1_, f32[16,72,128]{2,1,0:T(8,128)S(1)} %bitcast.16), custom_call_target="tpu_custom_call" | custom-call | flops 1073741824 | bytes 4194304 | tf_op jit(solution)/shard_map/pallas_call | solution.py:245
  63.7 2.7 %shard_map.97 = f32[1024,128]{1,0:T(8,128)S(1)} custom-call(s32[8]{0:T(128)S(1)} %stack.31.place_ref.refs_0_, bf16[16,1024]{1,0:T(8,128)(2,1)S(1)} %get-tuple-element.16.refs_1_, f32[16,72,128]{2,1,0:T(8,128)S(1)} %collective-permute-done.far_ref.refs_2_, f32[1024,128]{1,0:T(8,128)S(1)} %shard_map.96.refs_3_), custom_call_target="tpu_custom_call" | custom-call | flops 1073741824 | bytes 4194304 | tf_op jit(solution)/shard_map/pallas_call | solution.py:245
  66.4 0.0 copy-start.1
  66.4 12.6 %all_to_all.26.parts_ref = f32[16,64,128]{2,1,0:T(8,128)S(1)} all-to-all(f32[16,64,128]{2,1,0:T(8,128)S(1)} %bitcast.19), channel_id=1, replica_groups=mesh['z2'=2,'z1'=2,'z0'=2,'x'=4,'y'=4,'zhi'=2,'core'=2] {'x','y'}, dimensions={0} | all-to-all | bytes 1048576 | tf_op jit(solution)/shard_map/all_to_all | solution.py:250
  79.0 0.0 copy-done.1
  79.0 0.3 shard_map.98
  79.3 23.2 %all-gather.1 = f32[1152,128]{1,0:T(8,128)S(1)} all-gather(f32[72,128]{1,0:T(8,128)S(1)} %get-tuple-element.18), channel_id=3, replica_groups=mesh['z2'=2,'z1'=2,'z0'=2,'x'=4,'y'=4,'zhi'=2,'core'=2] {'zhi','z2','z1'..., dimensions={0}, use_global_device_ids=true | all-gather | bytes 626688 | tf_op jit(solution)/shard_map/all_gather | solution.py:267
  102.6 11.4 %collective-permute-start.1 = (f32[16,72,128]{2,1,0:T(8,128)S(1)}, f32[16,72,128]{2,1,0:T(8,128)S(1)}, u32[]{:S(2)}, u32[]{:S(2)}) collective-permute-start(f32[16,72,128]{2,1,0:T(8,128)S(1)} %bitcast.17), channel_id=1, source_target_pairs={{0,1},{1,0},{2,3},{3,2},{4,5},{5,4},{6,7},{7,6},{8,9},{9,8},{10,11... | collective-permute-start | bytes 1769480 | tf_op jit(solution)/shard_map/ppermute | solution.py:268
  114.0 2.7 %shard_map.99.refs_3_ = f32[1024,128]{1,0:T(8,128)S(1)} custom-call(s32[8]{0:T(128)S(1)} %stack.31.place_ref.refs_0_, bf16[16,1024]{1,0:T(8,128)(2,1)S(1)} %get-tuple-element.15.refs_1_, f32[16,72,128]{2,1,0:T(8,128)S(1)} %bitcast.18), custom_call_target="tpu_custom_call" | custom-call | flops 1073741824 | bytes 4194304 | tf_op jit(solution)/shard_map/pallas_call | solution.py:245
  116.7 0.0 collective-permute-done.1.refs_2_
  116.7 2.7 %shard_map.100 = f32[1024,128]{1,0:T(8,128)S(1)} custom-call(s32[8]{0:T(128)S(1)} %stack.31.place_ref.refs_0_, bf16[16,1024]{1,0:T(8,128)(2,1)S(1)} %get-tuple-element.15.refs_1_, f32[16,72,128]{2,1,0:T(8,128)S(1)} %collective-permute-done.1.refs_2_, f32[1024,128]{1,0:T(8,128)S(1)} %shard_map.99.refs_3_), custom_call_target="tpu_custom_call" | custom-call | flops 1073741824 | bytes 4194304 | tf_op jit(solution)/shard_map/pallas_call | solution.py:245
  119.4 13.0 %all_to_all.27.parts_ref = f32[16,64,128]{2,1,0:T(8,128)S(1)} all-to-all(f32[16,64,128]{2,1,0:T(8,128)S(1)} %bitcast.20), channel_id=1, replica_groups=mesh['z2'=2,'z1'=2,'z0'=2,'x'=4,'y'=4,'zhi'=2,'core'=2] {'x','y'}, dimensions={0} | all-to-all | bytes 1048576 | tf_op jit(solution)/shard_map/all_to_all | solution.py:250
  132.4 1.2 shard_map.101
  133.6 10.1 %all-to-all-start.3 = ((f32[32,1,128]{2,1,0:T(1,128)}), f32[32,1,128]{2,1,0:T(1,128)S(1)}, u32[]{:S(2)}, u32[]{:S(2)}) async-start(f32[32,1,128]{2,1,0:T(1,128)} %get-tuple-element.20), calls=%async_computation.3 | async-start | bytes 32768 | tf_op jit(solution)/shard_map/all_to_all | solution.py:275
  143.7 2.9 %collective-permute-start.2 = (f32[64,128]{1,0:T(8,128)S(1)}, f32[64,128]{1,0:T(8,128)S(1)}, u32[]{:S(2)}, u32[]{:S(2)}) collective-permute-start(f32[64,128]{1,0:T(8,128)S(1)} %get-tuple-element.21), channel_id=1, source_target_pairs={{0,0},{16,1},{32,2},{48,3},{64,4},{80,5},{96,6},{112,7},{128,8},{1... | collective-permute-start | bytes 98312 | tf_op jit(solution)/shard_map/ppermute | solution.py:274
  146.6 8.8 %all-to-all-done.3.parts_ref = f32[32,1,128]{2,1,0:T(1,128)S(1)} async-done(((f32[32,1,128]{2,1,0:T(1,128)}), f32[32,1,128]{2,1,0:T(1,128)S(1)}, u32[]{:S(2)}, u32[]{:S(2)}) %all-to-all-start.3) | async-done | bytes 16416 | tf_op jit(solution)/shard_map/all_to_all | solution.py:275
  155.4 0.6 shard_map.102
  156.1 3.5 %all-to-all-start.4 = ((f32[16,1,128]{2,1,0:T(1,128)}), f32[16,1,128]{2,1,0:T(1,128)S(1)}, u32[]{:S(2)}, u32[]{:S(2)}) async-start(f32[16,1,128]{2,1,0:T(1,128)} %shard_map.102), calls=%async_computation.4 | async-start | bytes 16384 | tf_op jit(solution)/shard_map/all_to_all | solution.py:277
  159.5 0.0 collective-permute-done.2.late_ref
  159.5 6.3 %all-to-all-done.4.parts_ref = f32[16,1,128]{2,1,0:T(1,128)S(1)} async-done(((f32[16,1,128]{2,1,0:T(1,128)}), f32[16,1,128]{2,1,0:T(1,128)S(1)}, u32[]{:S(2)}, u32[]{:S(2)}) %all-to-all-start.4) | async-done | bytes 8224 | tf_op jit(solution)/shard_map/all_to_all | solution.py:277
  165.8 0.6 shard_map.103
  (1 shorter events, 0.0 us)
Async XLA Ops:
  0.6 0.7 copy-start.3
  0.6 0.7 copy-start.5
  0.7 0.7 copy-start.2
  0.7 0.7 copy-start.4
  1.4 0.8 copy-start
  34.3 11.7 %collective-permute-start = (f32[16,72,128]{2,1,0:T(8,128)S(1)}, f32[16,72,128]{2,1,0:T(8,128)S(1)}, u32[]{:S(2)}, u32[]{:S(2)}) collective-permute-start(f32[16,72,128]{2,1,0:T(8,128)S(1)} %bitcast.14), channel_id=1, source_target_pairs={{0,1},{1,0},{2,3},{3,2},{4,5},{5,4},{6,7},{7,6},{8,9},{9,8},{10,11... | collective-permute-start | bytes 1769480 | tf_op jit(solution)/shard_map/ppermute | solution.py:255
  66.4 12.6 %copy-start.1 = (f32[64,128]{1,0:T(8,128)S(1)}, f32[64,128]{1,0:T(8,128)}, u32[]{:S(2)}) copy-start(f32[64,128]{1,0:T(8,128)} %powers_ref.5) | copy-start | bytes 98308
  102.6 14.1 %collective-permute-start.1 = (f32[16,72,128]{2,1,0:T(8,128)S(1)}, f32[16,72,128]{2,1,0:T(8,128)S(1)}, u32[]{:S(2)}, u32[]{:S(2)}) collective-permute-start(f32[16,72,128]{2,1,0:T(8,128)S(1)} %bitcast.17), channel_id=1, source_target_pairs={{0,1},{1,0},{2,3},{3,2},{4,5},{5,4},{6,7},{7,6},{8,9},{9,8},{10,11... | collective-permute-start | bytes 1769480 | tf_op jit(solution)/shard_map/ppermute | solution.py:268
  133.6 21.8 %all-to-all-start.3 = ((f32[32,1,128]{2,1,0:T(1,128)}), f32[32,1,128]{2,1,0:T(1,128)S(1)}, u32[]{:S(2)}, u32[]{:S(2)}) async-start(f32[32,1,128]{2,1,0:T(1,128)} %get-tuple-element.20), calls=%async_computation.3 | async-start | bytes 32768 | tf_op jit(solution)/shard_map/all_to_all | solution.py:275
  143.7 15.8 %collective-permute-start.2 = (f32[64,128]{1,0:T(8,128)S(1)}, f32[64,128]{1,0:T(8,128)S(1)}, u32[]{:S(2)}, u32[]{:S(2)}) collective-permute-start(f32[64,128]{1,0:T(8,128)S(1)} %get-tuple-element.21), channel_id=1, source_target_pairs={{0,0},{16,1},{32,2},{48,3},{64,4},{80,5},{96,6},{112,7},{128,8},{1... | collective-permute-start | bytes 98312 | tf_op jit(solution)/shard_map/ppermute | solution.py:274
  156.1 9.8 %all-to-all-start.4 = ((f32[16,1,128]{2,1,0:T(1,128)}), f32[16,1,128]{2,1,0:T(1,128)S(1)}, u32[]{:S(2)}, u32[]{:S(2)}) async-start(f32[16,1,128]{2,1,0:T(1,128)} %shard_map.102), calls=%async_computation.4 | async-start | bytes 16384 | tf_op jit(solution)/shard_map/all_to_all | solution.py:277

commit v14 on v13

--- a/solution.py
+++ b/solution.py
@@ -136,15 +136,14 @@
     columns = spread(column_ref)
     value_high, value_low = split(column_ref[:, 0:BLOCK, :].reshape(HALF, BANDS))
     values = jnp.concatenate([value_high, value_low], axis=1)
-    values = jnp.concatenate([values, values], axis=0)
     row_base = zhi * 4096 + core * 2048 + (z2 * 4 + z1 * 2 + z0) * 256
     col_base = y * 8192 + core * 2048 + x * 64
-    tile = 128
-    mine = (x * 4 + y) >> 1
-    for turn in range(ROWS // tile):
-        r = turn * tile if far else pl.multiple_of(((mine + turn) & 7) * tile, tile)
-        row = lax.broadcasted_iota(jnp.int32, (tile, tile), 0) + r
-        row_features = plane_ref[:, pl.ds(r, tile)]
+    tile, wide = 128, 256
+    mine = (x * 4 + y) >> 2
+    for turn in range(ROWS // wide):
+        r = turn * wide if far else pl.multiple_of(((mine + turn) & 3) * wide, wide)
+        row = lax.broadcasted_iota(jnp.int32, (wide, tile), 0) + r
+        row_features = plane_ref[:, pl.ds(r, wide)]
         block = row >> 6
         row_id = row_base + (block & 3) * 8192 + (block >> 2) * 64 + (row & 63)
         highs, lows = [], []
@@ -159,18 +158,18 @@
                 preferred_element_type=F32,
             )
             guess = pl.reciprocal(square, approx=True)
-            gain = guess * (2.0 - square * guess)
             if not far and turn == 0:
-                gain = jnp.where(row_id == col_id, 0.0, gain)
-            high, low = split(gain)
+                guess = jnp.where(row_id == col_id, 0.0, guess)
+            high = guess.astype(BF16)
             highs.append(high)
-            lows.append(low)
-        gains = jnp.concatenate(highs + lows, axis=1)
-        product = jnp.dot(gains, values, preferred_element_type=F32)
+            lows.append((guess * (1.0 - square * high.astype(F32))).astype(BF16))
+        product = jnp.dot(jnp.concatenate(highs, axis=1), values, preferred_element_type=F32)
         part = product[:, :BANDS] + product[:, BANDS:]
+        low_gain = jnp.concatenate(lows, axis=1)
+        part = part + jnp.dot(low_gain, value_high, preferred_element_type=F32)
         for ref in before:
-            part = part + ref[pl.ds(r, tile), :]
-        total_ref[pl.ds(r, tile), :] = part
+            part = part + ref[pl.ds(r, wide), :]
+        total_ref[pl.ds(r, wide), :] = part
 
 
 def add_blocks(ref):

time: 168 us -> 167 us (level)
  no operation moved by 1% of the time
where the time goes in v14:
time: 167 us; the launch traced here: 166 us
  blocking collectives  94.5 us (57%)
  starting transfers between devices  38.1 us (23%)
  waiting for transfers between devices  15.9 us (10%)
  Pallas kernels  14.1 us (8%)
    all_gather x1, blocking collectives, per_device(): near = lax.all_gather(sent, Z, axis=0)  32.1 us
    all_to_all x2, blocking collectives, spread_sum(): return lax.all_to_all(part.reshape(NXY, BLOCK, BANDS), XY, 0, 0)  25.5 us
    all_gather x1, blocking collectives, per_device(): near = lax.all_gather(column, Z, axis=0)  23.2 us
    ppermute x2, starting transfers between devices, per_device(): far = lax.ppermute(near, 'core', swap)  21.5 us
    all_to_all x1, blocking collectives, per_device(): chunks = lax.all_to_all(chunks, XY, 0, 0)  13.6 us
    all_to_all x1, starting transfers between devices, per_device(): gap = lax.all_to_all(gap, (*Z, 'core'), 0, 0)  10.1 us
    pallas_call x4, Pallas kernels, gain_product(): return call(kernel, product, 1 + len(args), smem=(0,), **work)(place, *args)  9.92 us
    all_to_all x1, waiting for transfers between devices, per_device(): gap = lax.all_to_all(gap, (*Z, 'core'), 0, 0)  8.79 us
  transfers between devices with their start and end apart: 5, of which 3 were waited for; matrix products, arithmetic and copies ran while one was open for 0% of the time, Pallas kernels for 2%

profile of v14, /device:TPU:1, one launch (start us, length us, event | category | flops | bytes accessed | tf_op | source)
XLA Modules:
  0.0 165.6 jit_solution(3606760406244701846)
XLA Ops:
  0.6 0.0 copy-start.3
  0.6 0.0 copy-start.5
  0.7 0.0 copy-start.2
  0.7 0.0 copy-start.4
  0.7 0.6 copy-done.3
  1.3 0.0 copy-done.5
  1.3 0.0 copy-done.2
  1.3 0.0 copy-done.4
  1.4 0.0 copy-start
  1.4 0.7 copy-done
  2.1 0.1 shard_map.93.sent_ref
  2.2 32.1 %all-gather = f32[1152,128]{1,0:T(8,128)S(1)} all-gather(f32[72,128]{1,0:T(8,128)S(1)} %shard_map.93.sent_ref), channel_id=2, replica_groups=mesh['z2'=2,'z1'=2,'z0'=2,'x'=4,'y'=4,'zhi'=2,'core'=2] {'zhi','z2','z1'..., dimensions={0}, use_global_device_ids=true | all-gather | bytes 626688 | tf_op jit(solution)/shard_map/all_gather | solution.py:253
  34.3 10.1 %collective-permute-start = (f32[16,72,128]{2,1,0:T(8,128)S(1)}, f32[16,72,128]{2,1,0:T(8,128)S(1)}, u32[]{:S(2)}, u32[]{:S(2)}) collective-permute-start(f32[16,72,128]{2,1,0:T(8,128)S(1)} %bitcast.14), channel_id=1, source_target_pairs={{0,1},{1,0},{2,3},{3,2},{4,5},{5,4},{6,7},{7,6},{8,9},{9,8},{10,11... | collective-permute-start | bytes 1769480 | tf_op jit(solution)/shard_map/ppermute | solution.py:254
  45.1 0.1 stack.31.place_ref.refs_0_
  45.2 0.9 collective-permute-done.far_ref.refs_2_
  46.1 0.6 shard_map.94
  46.7 13.6 %all_to_all.25.chunk_ref = f32[16,24,128]{2,1,0:T(8,128)S(1)} all-to-all(f32[16,24,128]{2,1,0:T(8,128)S(1)} %shard_map.94), channel_id=1, replica_groups=mesh['z2'=2,'z1'=2,'z0'=2,'x'=4,'y'=4,'zhi'=2,'core'=2] {'x','y'}, dimensions={0} | all-to-all | bytes 393216 | tf_op jit(solution)/shard_map/all_to_all | solution.py:256
  60.3 0.7 shard_map.95
  61.0 2.5 %shard_map.96.refs_3_ = f32[1024,128]{1,0:T(8,128)S(1)} custom-call(s32[8]{0:T(128)S(1)} %stack.31.place_ref.refs_0_, bf16[16,1024]{1,0:T(8,128)(2,1)S(1)} %get-tuple-element.16.refs_1_, f32[16,72,128]{2,1,0:T(8,128)S(1)} %bitcast.16), custom_call_target="tpu_custom_call" | custom-call | flops 1073741824 | bytes 4194304 | tf_op jit(solution)/shard_map/pallas_call | solution.py:244
  63.5 2.4 %shard_map.97 = f32[1024,128]{1,0:T(8,128)S(1)} custom-call(s32[8]{0:T(128)S(1)} %stack.31.place_ref.refs_0_, bf16[16,1024]{1,0:T(8,128)(2,1)S(1)} %get-tuple-element.16.refs_1_, f32[16,72,128]{2,1,0:T(8,128)S(1)} %collective-permute-done.far_ref.refs_2_, f32[1024,128]{1,0:T(8,128)S(1)} %shard_map.96.refs_3_), custom_call_target="tpu_custom_call" | custom-call | flops 1073741824 | bytes 4194304 | tf_op jit(solution)/shard_map/pallas_call | solution.py:244
  66.0 0.0 copy-start.1
  66.0 12.6 %all_to_all.26.parts_ref = f32[16,64,128]{2,1,0:T(8,128)S(1)} all-to-all(f32[16,64,128]{2,1,0:T(8,128)S(1)} %bitcast.19), channel_id=1, replica_groups=mesh['z2'=2,'z1'=2,'z0'=2,'x'=4,'y'=4,'zhi'=2,'core'=2] {'x','y'}, dimensions={0} | all-to-all | bytes 1048576 | tf_op jit(solution)/shard_map/all_to_all | solution.py:249
  78.6 0.0 copy-done.1
  78.6 0.3 shard_map.98
  78.9 23.2 %all-gather.1 = f32[1152,128]{1,0:T(8,128)S(1)} all-gather(f32[72,128]{1,0:T(8,128)S(1)} %get-tuple-element.18), channel_id=3, replica_groups=mesh['z2'=2,'z1'=2,'z0'=2,'x'=4,'y'=4,'zhi'=2,'core'=2] {'zhi','z2','z1'..., dimensions={0}, use_global_device_ids=true | all-gather | bytes 626688 | tf_op jit(solution)/shard_map/all_gather | solution.py:266
  102.1 11.4 %collective-permute-start.1 = (f32[16,72,128]{2,1,0:T(8,128)S(1)}, f32[16,72,128]{2,1,0:T(8,128)S(1)}, u32[]{:S(2)}, u32[]{:S(2)}) collective-permute-start(f32[16,72,128]{2,1,0:T(8,128)S(1)} %bitcast.17), channel_id=1, source_target_pairs={{0,1},{1,0},{2,3},{3,2},{4,5},{5,4},{6,7},{7,6},{8,9},{9,8},{10,11... | collective-permute-start | bytes 1769480 | tf_op jit(solution)/shard_map/ppermute | solution.py:267
  113.5 2.5 %shard_map.99.refs_3_ = f32[1024,128]{1,0:T(8,128)S(1)} custom-call(s32[8]{0:T(128)S(1)} %stack.31.place_ref.refs_0_, bf16[16,1024]{1,0:T(8,128)(2,1)S(1)} %get-tuple-element.15.refs_1_, f32[16,72,128]{2,1,0:T(8,128)S(1)} %bitcast.18), custom_call_target="tpu_custom_call" | custom-call | flops 1073741824 | bytes 4194304 | tf_op jit(solution)/shard_map/pallas_call | solution.py:244
  116.1 0.0 collective-permute-done.1.refs_2_
  116.1 2.4 %shard_map.100 = f32[1024,128]{1,0:T(8,128)S(1)} custom-call(s32[8]{0:T(128)S(1)} %stack.31.place_ref.refs_0_, bf16[16,1024]{1,0:T(8,128)(2,1)S(1)} %get-tuple-element.15.refs_1_, f32[16,72,128]{2,1,0:T(8,128)S(1)} %collective-permute-done.1.refs_2_, f32[1024,128]{1,0:T(8,128)S(1)} %shard_map.99.refs_3_), custom_call_target="tpu_custom_call" | custom-call | flops 1073741824 | bytes 4194304 | tf_op jit(solution)/shard_map/pallas_call | solution.py:244
  118.5 13.0 %all_to_all.27.parts_ref = f32[16,64,128]{2,1,0:T(8,128)S(1)} all-to-all(f32[16,64,128]{2,1,0:T(8,128)S(1)} %bitcast.20), channel_id=1, replica_groups=mesh['z2'=2,'z1'=2,'z0'=2,'x'=4,'y'=4,'zhi'=2,'core'=2] {'x','y'}, dimensions={0} | all-to-all | bytes 1048576 | tf_op jit(solution)/shard_map/all_to_all | solution.py:249
  131.5 1.2 shard_map.101
  132.7 10.1 %all-to-all-start.3 = ((f32[32,1,128]{2,1,0:T(1,128)}), f32[32,1,128]{2,1,0:T(1,128)S(1)}, u32[]{:S(2)}, u32[]{:S(2)}) async-start(f32[32,1,128]{2,1,0:T(1,128)} %get-tuple-element.20), calls=%async_computation.3 | async-start | bytes 32768 | tf_op jit(solution)/shard_map/all_to_all | solution.py:274
  142.9 2.9 %collective-permute-start.2 = (f32[64,128]{1,0:T(8,128)S(1)}, f32[64,128]{1,0:T(8,128)S(1)}, u32[]{:S(2)}, u32[]{:S(2)}) collective-permute-start(f32[64,128]{1,0:T(8,128)S(1)} %get-tuple-element.21), channel_id=1, source_target_pairs={{0,0},{16,1},{32,2},{48,3},{64,4},{80,5},{96,6},{112,7},{128,8},{1... | collective-permute-start | bytes 98312 | tf_op jit(solution)/shard_map/ppermute | solution.py:273
  145.8 8.8 %all-to-all-done.3.parts_ref = f32[32,1,128]{2,1,0:T(1,128)S(1)} async-done(((f32[32,1,128]{2,1,0:T(1,128)}), f32[32,1,128]{2,1,0:T(1,128)S(1)}, u32[]{:S(2)}, u32[]{:S(2)}) %all-to-all-start.3) | async-done | bytes 16416 | tf_op jit(solution)/shard_map/all_to_all | solution.py:274
  154.6 0.6 shard_map.102
  155.2 3.5 %all-to-all-start.4 = ((f32[16,1,128]{2,1,0:T(1,128)}), f32[16,1,128]{2,1,0:T(1,128)S(1)}, u32[]{:S(2)}, u32[]{:S(2)}) async-start(f32[16,1,128]{2,1,0:T(1,128)} %shard_map.102), calls=%async_computation.4 | async-start | bytes 16384 | tf_op jit(solution)/shard_map/all_to_all | solution.py:276
  158.7 0.0 collective-permute-done.2.late_ref
  158.7 6.3 %all-to-all-done.4.parts_ref = f32[16,1,128]{2,1,0:T(1,128)S(1)} async-done(((f32[16,1,128]{2,1,0:T(1,128)}), f32[16,1,128]{2,1,0:T(1,128)S(1)}, u32[]{:S(2)}, u32[]{:S(2)}) %all-to-all-start.4) | async-done | bytes 8224 | tf_op jit(solution)/shard_map/all_to_all | solution.py:276
  165.0 0.6 shard_map.103
  (1 shorter events, 0.0 us)
Async XLA Ops:
  0.6 0.7 copy-start.3
  0.6 0.7 copy-start.5
  0.7 0.7 copy-start.2
  0.7 0.7 copy-start.4
  1.4 0.8 copy-start
  34.3 11.7 %collective-permute-start = (f32[16,72,128]{2,1,0:T(8,128)S(1)}, f32[16,72,128]{2,1,0:T(8,128)S(1)}, u32[]{:S(2)}, u32[]{:S(2)}) collective-permute-start(f32[16,72,128]{2,1,0:T(8,128)S(1)} %bitcast.14), channel_id=1, source_target_pairs={{0,1},{1,0},{2,3},{3,2},{4,5},{5,4},{6,7},{7,6},{8,9},{9,8},{10,11... | collective-permute-start | bytes 1769480 | tf_op jit(solution)/shard_map/ppermute | solution.py:254
  66.0 12.6 %copy-start.1 = (f32[64,128]{1,0:T(8,128)S(1)}, f32[64,128]{1,0:T(8,128)}, u32[]{:S(2)}) copy-start(f32[64,128]{1,0:T(8,128)} %powers_ref.5) | copy-start | bytes 98308
  102.1 13.9 %collective-permute-start.1 = (f32[16,72,128]{2,1,0:T(8,128)S(1)}, f32[16,72,128]{2,1,0:T(8,128)S(1)}, u32[]{:S(2)}, u32[]{:S(2)}) collective-permute-start(f32[16,72,128]{2,1,0:T(8,128)S(1)} %bitcast.17), channel_id=1, source_target_pairs={{0,1},{1,0},{2,3},{3,2},{4,5},{5,4},{6,7},{7,6},{8,9},{9,8},{10,11... | collective-permute-start | bytes 1769480 | tf_op jit(solution)/shard_map/ppermute | solution.py:267
  132.7 21.9 %all-to-all-start.3 = ((f32[32,1,128]{2,1,0:T(1,128)}), f32[32,1,128]{2,1,0:T(1,128)S(1)}, u32[]{:S(2)}, u32[]{:S(2)}) async-start(f32[32,1,128]{2,1,0:T(1,128)} %get-tuple-element.20), calls=%async_computation.3 | async-start | bytes 32768 | tf_op jit(solution)/shard_map/all_to_all | solution.py:274
  142.9 15.8 %collective-permute-start.2 = (f32[64,128]{1,0:T(8,128)S(1)}, f32[64,128]{1,0:T(8,128)S(1)}, u32[]{:S(2)}, u32[]{:S(2)}) collective-permute-start(f32[64,128]{1,0:T(8,128)S(1)} %get-tuple-element.21), channel_id=1, source_target_pairs={{0,0},{16,1},{32,2},{48,3},{64,4},{80,5},{96,6},{112,7},{128,8},{1... | collective-permute-start | bytes 98312 | tf_op jit(solution)/shard_map/ppermute | solution.py:273
  155.2 9.8 %all-to-all-start.4 = ((f32[16,1,128]{2,1,0:T(1,128)}), f32[16,1,128]{2,1,0:T(1,128)S(1)}, u32[]{:S(2)}, u32[]{:S(2)}) async-start(f32[16,1,128]{2,1,0:T(1,128)} %shard_map.102), calls=%async_computation.4 | async-start | bytes 16384 | tf_op jit(solution)/shard_map/all_to_all | solution.py:276
